TPU v7x, 512 devices: a whole 4x4x16 slice. The times are simulated.
512 devices in a mesh: sib: 32 (over y, x, core), ctx: 8 (over z_lo), tp: 2 (over z_hi).
Axes of the slice: x: 4, y: 4, z: 16 (z_hi: 2, z_lo: 8; z = z_hi * 8 + z_lo), core: 2. Of those that a mesh axis runs over, the one named last changes fastest.
Arguments:
- queries: bfloat16 [32, 4, 1024, 512], P('sib', 'tp', 'ctx'), may hold values from -27 to 27
- output_gradient: bfloat16 [32, 4, 1024, 512], P('sib', 'tp', 'ctx'), may hold values from -6 to 6
- forward_output: bfloat16 [32, 4, 1024, 512], P('sib', 'tp', 'ctx'), may hold values from -6 to 6
- sibling_key_matrix: bfloat16 [32, 1024, 512], P('sib', 'ctx'), may hold values from -6 to 6
- sibling_value_matrix: bfloat16 [32, 1024, 512], P('sib', 'ctx'), may hold values from -6 to 6
- prefix_keys: bfloat16 [1024, 512], P(('sib', 'ctx')), may hold values from -9 to 9
- prefix_value_matrix: bfloat16 [1024, 512], P(('sib', 'ctx')), may hold values from -6 to 6
- lengths: int32 [32], replicated, may hold values from 1 to 1024, 20480 in all
Outputs:
- query_grads: bfloat16 [32, 4, 1024, 512], P('sib', 'tp', 'ctx')
- sibling_key_grads: bfloat16 [32, 1024, 512], P('sib', ('ctx', 'tp'))
- sibling_value_grads: bfloat16 [32, 1024, 512], P('sib', ('ctx', 'tp'))
- prefix_key_grads: bfloat16 [1024, 512], P(('sib', 'ctx', 'tp'))
- prefix_value_grads: bfloat16 [1024, 512], P(('sib', 'ctx', 'tp'))
Inputs may be any that keep to these rules, and one draw needn't show every extreme that they name: `lengths`: at least one sibling is full, with 1024 live tokens.
All inputs are finite; a program needn't handle non-finite values.
Results may differ from a plain program's by a relative error of at most 0.015.
Values may be sent and summed in bfloat16 or wider, within the bound.
No kernel may reach another device: no remote copies, remote signals or barrier semaphores. Data moves between devices by JAX's collectives and lax.ppermute only.
A program may use at most 64 MiB of HBM per device.

v0:
```python
import math

import jax
import jax.numpy as jnp
from jax import lax
from jax.sharding import PartitionSpec as P

KV_HEAD_COUNT = 4


def merged(part, axis, combine):
    gathered = jax.tree.map(lambda a: lax.all_gather(a, axis), part)

    def take(source):
        return jax.tree.map(lambda a: lax.dynamic_index_in_dim(a, source, 0, False), gathered)

    return lax.fori_loop(
        1, lax.axis_size(axis), lambda source, state: combine(state, take(source)), take(0)
    )


def column_slice(array, head_number, head_dim):
    return array[..., head_number * head_dim : (head_number + 1) * head_dim]


def merge_stats(first, second):
    max_first, sum_first = first
    max_second, sum_second = second
    largest = jnp.maximum(max_first, max_second)
    return (
        largest,
        sum_first * jnp.exp(max_first - largest) + sum_second * jnp.exp(max_second - largest),
    )


def score_pair(query_head, prefix_head, sibling_head, causal, score_scale):
    prefix_scores = (
        jnp.einsum("gid,jd->gij", query_head, prefix_head, preferred_element_type=jnp.float32)
        * score_scale
    )
    sibling_scores = (
        jnp.einsum("gid,jd->gij", query_head, sibling_head, preferred_element_type=jnp.float32)
        * score_scale
    )
    sibling_scores = jnp.where(causal[None], sibling_scores, -jnp.inf)
    return (prefix_scores, sibling_scores)


def on_device(
    queries,
    output_gradient,
    forward_output,
    sibling_key_matrix,
    sibling_value_matrix,
    prefix_keys,
    prefix_value_matrix,
    lengths,
):
    key_value_heads = KV_HEAD_COUNT
    row_width = queries.shape[3]
    head_dim = row_width // key_value_heads
    score_scale = 1.0 / math.sqrt(head_dim)
    groups_here = queries.shape[1]
    own_rows = queries.shape[2]
    ctx_count = lax.axis_size("ctx")
    ctx_index = lax.axis_index("ctx")
    sib_index = lax.axis_index("sib")
    length = lax.dynamic_index_in_dim(lengths, sib_index, 0, keepdims=False)
    own_positions = ctx_index * own_rows + jnp.arange(own_rows, dtype=jnp.int32)
    live_mask = (own_positions < length)[None, None, :, None]
    live_gradient = jnp.where(live_mask, output_gradient, jnp.zeros_like(output_gradient))
    row_delta_term = jnp.sum(
        (live_gradient.astype(jnp.float32) * forward_output.astype(jnp.float32)).reshape(
            1, groups_here, own_rows, key_value_heads, head_dim
        ),
        -1,
    ).astype(jnp.bfloat16)
    queries_all, grads_all, delta_all = (
        lax.all_gather(queries, "ctx", axis=2, tiled=True),
        lax.all_gather(live_gradient, "ctx", axis=2, tiled=True),
        lax.all_gather(row_delta_term, "ctx", axis=2, tiled=True),
    )
    prefix_key_rows, prefix_value_rows = (
        lax.all_gather(prefix_keys, "sib", axis=0, tiled=True),
        lax.all_gather(prefix_value_matrix, "sib", axis=0, tiled=True),
    )
    queries_all = queries_all[0]
    grads_all = grads_all[0]
    delta_all = delta_all[0].astype(jnp.float32)
    sibling_key_rows = sibling_key_matrix[0]
    sibling_value_rows = sibling_value_matrix[0]
    all_rows = own_rows * ctx_count
    causal = own_positions[None, :] <= jnp.arange(all_rows, dtype=jnp.int32)[:, None]
    stored = []
    row_maxima = []
    row_sums = []
    for head_number in range(key_value_heads):
        prefix_scores, sibling_scores = score_pair(
            column_slice(queries_all, head_number, head_dim),
            column_slice(prefix_key_rows, head_number, head_dim),
            column_slice(sibling_key_rows, head_number, head_dim),
            causal,
            score_scale,
        )
        stored.append((prefix_scores, sibling_scores))
        row_max = jnp.maximum(jnp.max(prefix_scores, 2), jnp.max(sibling_scores, 2))
        row_sum = jnp.sum(jnp.exp(prefix_scores - row_max[..., None]), 2) + jnp.sum(
            jnp.exp(sibling_scores - row_max[..., None]), 2
        )
        row_maxima.append(row_max)
        row_sums.append(row_sum)
    row_maxima, row_sums = merged((jnp.stack(row_maxima), jnp.stack(row_sums)), "ctx", merge_stats)
    log_norm = row_maxima + jnp.log(row_sums)
    query_terms = []
    prefix_dk_heads, prefix_dv_heads, sibling_dk_heads, sibling_dv_heads = ([], [], [], [])
    for head_number in range(key_value_heads):
        query_head = column_slice(queries_all, head_number, head_dim)
        grad_head = column_slice(grads_all, head_number, head_dim)
        prefix_head = column_slice(prefix_key_rows, head_number, head_dim)
        sibling_head = column_slice(sibling_key_rows, head_number, head_dim)
        prefix_scores, sibling_scores = score_pair(
            query_head, prefix_head, sibling_head, causal, score_scale
        )
        head_norm = log_norm[head_number][..., None]
        delta_head = delta_all[:, :, head_number][..., None]
        prefix_probs = jnp.exp(prefix_scores - head_norm)
        sibling_probs = jnp.exp(sibling_scores - head_norm)
        prefix_dprobs = jnp.einsum(
            "gid,jd->gij",
            grad_head,
            column_slice(prefix_value_rows, head_number, head_dim),
            preferred_element_type=jnp.float32,
        )
        sibling_dprobs = jnp.einsum(
            "gid,jd->gij",
            grad_head,
            column_slice(sibling_value_rows, head_number, head_dim),
            preferred_element_type=jnp.float32,
        )
        prefix_dscores = (prefix_probs * (prefix_dprobs - delta_head)).astype(jnp.bfloat16)
        sibling_dscores = (sibling_probs * (sibling_dprobs - delta_head)).astype(jnp.bfloat16)
        prefix_dv_heads.append(
            jnp.einsum(
                "gij,gid->jd",
                prefix_probs.astype(jnp.bfloat16),
                grad_head,
                preferred_element_type=jnp.float32,
            )
        )
        prefix_dk_heads.append(
            jnp.einsum(
                "gij,gid->jd", prefix_dscores, query_head, preferred_element_type=jnp.float32
            )
            * score_scale
        )
        sibling_dv_heads.append(
            jnp.einsum(
                "gij,gid->jd",
                sibling_probs.astype(jnp.bfloat16),
                grad_head,
                preferred_element_type=jnp.float32,
            )
        )
        sibling_dk_heads.append(
            jnp.einsum(
                "gij,gid->jd", sibling_dscores, query_head, preferred_element_type=jnp.float32
            )
            * score_scale
        )
        query_term = jnp.einsum(
            "gij,jd->gid", prefix_dscores, prefix_head, preferred_element_type=jnp.float32
        )
        query_term = query_term + jnp.einsum(
            "gij,jd->gid", sibling_dscores, sibling_head, preferred_element_type=jnp.float32
        )
        query_terms.append(query_term * score_scale)
    query_total = jnp.concatenate(query_terms, 2)[None]
    query_grads = lax.psum_scatter(
        query_total.astype(jnp.bfloat16), "ctx", scatter_dimension=2, tiled=True
    )
    prefix_key_grad = jnp.concatenate(prefix_dk_heads, 1)
    prefix_value_grad = jnp.concatenate(prefix_dv_heads, 1)
    sibling_key_grad = jnp.concatenate(sibling_dk_heads, 1)[None]
    sibling_value_grad = jnp.concatenate(sibling_dv_heads, 1)[None]
    prefix_dk, prefix_dv = (
        lax.psum_scatter(prefix_key_grad, ("sib", "tp"), scatter_dimension=0, tiled=True),
        lax.psum_scatter(prefix_value_grad, ("sib", "tp"), scatter_dimension=0, tiled=True),
    )
    sibling_dk, sibling_dv = (
        lax.psum_scatter(sibling_key_grad, "tp", scatter_dimension=1, tiled=True),
        lax.psum_scatter(sibling_value_grad, "tp", scatter_dimension=1, tiled=True),
    )
    return (
        query_grads,
        sibling_dk.astype(jnp.bfloat16),
        sibling_dv.astype(jnp.bfloat16),
        prefix_dk.astype(jnp.bfloat16),
        prefix_dv.astype(jnp.bfloat16),
    )


def solution(mesh):
    placed = (
        P("sib", "tp", "ctx", None),
        P("sib", "tp", "ctx", None),
        P("sib", "tp", "ctx", None),
        P("sib", "ctx", None),
        P("sib", "ctx", None),
        P(("sib", "ctx"), None),
        P(("sib", "ctx"), None),
        P(),
    )
    return jax.shard_map(
        on_device,
        mesh=mesh,
        in_specs=placed,
        out_specs=(
            P("sib", "tp", "ctx", None),
            P("sib", ("ctx", "tp"), None),
            P("sib", ("ctx", "tp"), None),
            P(("sib", "ctx", "tp"), None),
            P(("sib", "ctx", "tp"), None),
        ),
        check_vma=False,
    )
```

profile of v0, /device:TPU:1, one launch (start us, length us, event | category | flops | bytes accessed | tf_op | source)
XLA Modules:
  0.0 1222.0 jit_solution(16360116683885236460)
XLA Ops:
  7.2 0.7 all-gather.8.cloned.1.call-update
  8.0 1.2 dynamic_slice.33
  9.2 0.7 broadcast_compare_fusion
  9.9 1.9 convert_multiply_fusion
  11.8 1.3 dynamic-slice.4
  13.1 1.3 dynamic-slice
  14.5 27.5 %all-gather.3 = bf16[32,4,512]{2,1,0:T(4,128)(2,1)S(1)} all-gather(bf16[1,4,512]{2,1,0:T(4,128)(2,1)} %bitcast.272), channel_id=1, replica_groups=mesh['sib'=32,'ctx'=8,'tp'=2] {'sib'}, dimensions={0}, use_global_device_ids=true | all-gather | bytes 135168 | tf_op jit(solution)/shard_map/all_gather | solution.py:84
  42.1 25.5 %all-gather.4 = bf16[32,4,512]{2,1,0:T(4,128)(2,1)S(1)} all-gather(bf16[1,4,512]{2,1,0:T(4,128)(2,1)S(1)} %bitcast.273), channel_id=1, replica_groups=mesh['sib'=32,'ctx'=8,'tp'=2] {'sib'}, dimensions={0}, use_global_device_ids=true | all-gather | bytes 135168 | tf_op jit(solution)/shard_map/all_gather | solution.py:85
  67.8 0.4 reduce_sum.89
  68.2 44.5 %all-gather.2 = bf16[2,1024,4]{2,1,0:T(8,128)(2,1)S(1)} all-gather(bf16[2,128,4]{2,1,0:T(8,128)(2,1)S(1)} %reduce_sum.89), channel_id=4, replica_groups=mesh['sib'=32,'ctx'=8,'tp'=2] {'ctx'}, dimensions={1}, use_global_device_ids=true | all-gather | bytes 18432 | tf_op jit(solution)/shard_map/all_gather | solution.py:81
  112.8 2.6 slice_reduce_fusion.3
  116.7 1.5 fusion.102
  118.2 1.7 fusion.104
  123.7 42.3 %all-gather.1 = f32[32,2,1024]{2,1,0:T(2,128)S(1)} all-gather(f32[4,2,1024]{2,1,0:T(2,128)S(1)} %pad_maximum_fusion.4), channel_id=3, replica_groups=mesh['sib'=32,'ctx'=8,'tp'=2] {'ctx'}, dimensions={0}, use_global_device_ids=true | all-gather | bytes 294912 | tf_op jit(solution)/shard_map/all_gather | solution.py:12
  166.0 40.6 %all-gather = f32[32,2,1024]{2,1,0:T(2,128)S(1)} all-gather(f32[4,2,1024]{2,1,0:T(2,128)S(1)} %pad_maximum_fusion.3), channel_id=2, replica_groups=mesh['sib'=32,'ctx'=8,'tp'=2] {'ctx'}, dimensions={0}, use_global_device_ids=true | all-gather | bytes 294912 | tf_op jit(solution)/shard_map/all_gather | solution.py:12
  206.6 0.6 while.17
  207.2 0.6 slice_bitcast_fusion.43
  207.8 1.9 convolution_bitcast_fusion.3
  209.7 1.8 fusion.18
  211.5 1.7 fusion.19
  213.3 0.4 convolution_bitcast_fusion
  214.1 0.6 copy-done.16
  215.1 1.0 convolution_bitcast_fusion.1
  216.8 1.0 convolution_bitcast_fusion.2
  221.5 1.5 pad_maximum_fusion
  223.0 6.2 copy.264
  229.1 3.5 copy.271
  232.7 1.0 pad_maximum_fusion.2
  233.7 1.6 fusion.37
  235.3 1.4 fusion.34
  237.5 0.7 pad_maximum_fusion.1
  238.2 584.7 %all-reduce.8 = (bf16[128,512]{0,1:T(8,128)(2,1)}, bf16[128,512]{0,1:T(8,128)(2,1)S(1)}) all-reduce(f32[128,512]{0,1:T(8,128)} %pad_maximum_fusion.1, f32[128,512]{0,1:T(8,128)S(1)} %pad_maximum_fusion.2), channel_id=8, replica_groups=mesh['sib'=32,'ctx'=8,'tp'=2] {'sib','tp'}, use_global_device_ids=true, to_apply=%region_22.23.clone | all-reduce | flops 131072 | bytes 786432
  822.9 1.0 dynamic-slice_convert_fusion.1
  823.9 0.7 copy.198
  824.7 0.7 copy.199
  825.4 1.5 fusion.41
  826.9 1.4 fusion.38
  828.3 1.4 fusion.39
  830.1 0.7 maximum_bitcast_fusion
  830.8 1.1 copy.169
  832.0 1.7 convolution_bitcast_fusion.11
  833.7 1.6 convolution_bitcast_fusion.8
  835.3 0.4 convolution_bitcast_fusion.9
  836.3 375.8 %all-reduce.9 = (bf16[1,128,512]{2,0,1:T(2,128)(2,1)S(1)}, bf16[1,128,512]{2,0,1:T(2,128)(2,1)S(1)}) all-reduce(f32[1,128,512]{2,0,1:T(1,128)S(1)} %copy.169, f32[1,128,512]{2,0,1:T(1,128)S(1)} %copy.178), channel_id=6, replica_groups=mesh['sib'=32,'ctx'=8,'tp'=2] {'tp'}, use_global_device_ids=true, to_apply=%region_20.21.clone | all-reduce | flops 131072 | bytes 786432
  1212.2 0.6 copy.197
  1213.0 0.6 copy.196
  1213.6 1.1 reshape.292
  1214.8 0.7 copy.195
  (152 shorter events, 11.5 us)
Async XLA Ops:
  7.2 34.9 %copy-start.43 = (bf16[4,512]{1,0:T(4,128)(2,1)S(1)}, bf16[4,512]{1,0:T(4,128)(2,1)}, u32[]{:S(2)}) copy-start(bf16[4,512]{1,0:T(4,128)(2,1)} %param.16) | copy-start | bytes 12292
  7.2 109.5 %all-gather.8.cloned.1.call-start = ((), (), s32[]{:S(2)}) async-start(), calls=%async_computation.1 | async-start | bytes 2359296 | tf_op jit(solution)/shard_map/all_gather | solution.py:79
  7.9 199.9 %all-gather.10.cloned.1.call-start = ((), (), s32[]{:S(2)}) async-start(), calls=%async_computation.2 | async-start | bytes 2359296 | tf_op jit(solution)/shard_map/all_gather | solution.py:80
  11.8 1201.9 %reduce-scatter.6.cloned.1.call-start = ((), (), s32[]{:S(2)}) async-start(), calls=%async_computation.3 | async-start | bytes 2359296
  116.7 3.3 copy-start.1
  118.2 4.7 copy-start.6
  118.2 2.4 copy-start.38
  120.0 2.6 copy-start.4
  120.7 2.6 copy-start.8
  121.0 1.2 copy-start.9
  121.4 1.2 copy-start.12
  121.8 1.1 copy-start.15
  122.2 1.1 copy-start.17
  207.8 5.5 copy-start.35
  207.8 3.7 copy-start
  209.7 3.6 copy-start.7
  209.7 3.6 copy-start.33
  211.5 8.2 copy-start.18
  211.5 2.2 copy-start.42
  213.3 7.8 copy-start.26
  213.3 1.4 copy-start.16
  213.3 1.4 copy-start.37
  213.8 1.4 copy-start.5
  214.7 4.6 copy-start.20
  214.7 1.4 copy-start.41
  215.0 5.7 copy-start.28
  215.0 1.4 copy-start.13
  216.5 2.5 copy-start.22
  216.5 1.4 copy-start.40
  216.8 3.6 copy-start.30
  216.8 1.4 copy-start.10
  218.3 1.0 copy-start.24
  218.6 1.4 copy-start.31
  218.9 1.1 copy-start.39
  232.6 1.1 copy-start.19
  232.6 2.7 copy-start.21
  232.6 4.1 copy-start.2
  232.6 4.1 copy-start.23
  232.6 4.4 copy-start.25
  236.7 588.6 %copy-start.27 = (bf16[2,1024,128]{1,2,0:T(8,128)(2,1)S(1)}, bf16[2,1024,128]{1,2,0:T(8,128)(2,1)}, u32[]{:S(2)}) copy-start(bf16[2,1024,128]{1,2,0:T(8,128)(2,1)} %copy-done.26) | copy-start | bytes 1572868
  237.1 589.8 %copy-start.29 = (bf16[2,1024,128]{1,2,0:T(8,128)(2,1)S(1)}, bf16[2,1024,128]{1,2,0:T(8,128)(2,1)}, u32[]{:S(2)}) copy-start(bf16[2,1024,128]{1,2,0:T(8,128)(2,1)} %copy-done.28) | copy-start | bytes 1572868
  825.4 3.0 copy-start.3
  825.4 4.4 copy-start.32
  826.9 5.0 copy-start.36
  829.7 3.9 copy-start.34
  830.1 5.2 copy-start.14
  831.9 3.8 copy-start.11
Sparse Core Ops, SparseCore 0:
  10.1 72.4 all-gather.7
  85.2 69.6 all-gather.9
  232.7 85.9 reduce-scatter.5
where the time goes:
time: 1220 us
  blocking collectives  1140 us (93%)
  matrix products  30.2 us (2%)
  local copies, waits for them, and re-layouts  25 us (2%)
  between operations  16 us (1%)
    unnamed x2, blocking collectives  960 us
    all_gather x2, blocking collectives, merged(): gathered = jax.tree.map(lambda a: lax.all_gather(a, axis), part)  82.9 us
    all_gather x1, blocking collectives, on_device(): lax.all_gather(row_delta_term, 'ctx', axis=2, tiled=True)  44.5 us
    all_gather x1, blocking collectives, on_device(): lax.all_gather(prefix_keys, 'sib', axis=0, tiled=True)  27.5 us
    all_gather x1, blocking collectives, on_device(): lax.all_gather(prefix_value_matrix, 'sib', axis=0, tiled=True)  25.5 us
  transfers between devices with their start and end apart: 3, of which 0 were waited for; matrix products, arithmetic and copies ran while one was open for 3% of the time, Pallas kernels for 0%

commit v1 on v0

v1 whole, which is shorter than its diff:
```python
import functools
import math

import jax
import jax.numpy as jnp
from jax import lax
from jax.experimental import pallas as pl
from jax.experimental.pallas import tpu as pltpu
from jax.sharding import Mesh, PartitionSpec as P

HEADS = 4
LANES = 128
ROWS = 128
GROUPS = 2
LOG2E = math.log2(math.e)
NEG = -1e30
Z = ("cb", "cq", "tp")


def dot_nt(a, b):
    return lax.dot_general(a, b, (((1,), (1,)), ((), ())), preferred_element_type=jnp.float32)


def dot_nn(a, b):
    return lax.dot_general(a, b, (((1,), (0,)), ((), ())), preferred_element_type=jnp.float32)


def vmem(n):
    return [pl.BlockSpec(memory_space=pltpu.VMEM)] * n


def cost(flops, moved, exps=0):
    return pl.CostEstimate(flops=flops, bytes_accessed=moved, transcendentals=exps)


def pack_kernel(lengths, q, g, o, k, v, pk, pv, kvm, qg):
    ctx = lax.axis_index("cb") * HEADS + lax.axis_index("cq")
    length = lengths[lax.axis_index("sib")]
    row = lax.broadcasted_iota(jnp.int32, (ROWS, LANES), 0) + ctx * ROWS
    live = row < length
    ones = jnp.ones((8, LANES), jnp.bfloat16)
    for h in range(HEADS):
        cols = slice(h * LANES, (h + 1) * LANES)
        kvm[h, 0:ROWS, :] = k[:, cols]
        kvm[h, ROWS : 2 * ROWS, :] = v[:, cols]
        deltas = []
        for slot in range(GROUPS):
            rows = slice(slot * ROWS, (slot + 1) * ROWS)
            qg[h, rows, :] = q[slot, :, cols]
            grad = jnp.where(live, g[slot, :, cols].astype(jnp.float32), 0.0)
            qg[h, GROUPS * ROWS + slot * ROWS : GROUPS * ROWS + (slot + 1) * ROWS, :] = grad.astype(
                jnp.bfloat16
            )
            prod = grad * o[slot, :, cols].astype(jnp.float32)
            high = prod.astype(jnp.bfloat16)
            low = (prod - high.astype(jnp.float32)).astype(jnp.bfloat16)
            deltas.append((dot_nt(ones, high) + dot_nt(ones, low))[0:1])
        misc = jnp.concatenate(
            [pk[:, cols].astype(jnp.float32), pv[:, cols].astype(jnp.float32)]
            + deltas
            + [jnp.zeros((6, LANES), jnp.float32)],
            axis=0,
        )
        kvm[h, 2 * ROWS : 2 * ROWS + 16, :] = misc.astype(jnp.bfloat16)


def main_kernel(
    chunk, n_sib, qg, kvm, oth_lo, oth_hi, pref,
    dq, pgrad, keep, send8, plus, minus,
    keys, values, keys_t, scores, dk_acc, dv_acc,
):
    scale = 1.0 / math.sqrt(LANES)
    cb = lax.axis_index("cb")
    tp = lax.axis_index("tp")
    half = HEADS * ROWS
    pre = n_sib * 16
    total = 2 * pre + 2 * half
    for part, base in ((0, 0), (1, pre)):
        keys[base : base + pre, :] = pref[:, part * 32 : part * 32 + 16, :].reshape(pre, LANES)
        values[base : base + pre, :] = pref[:, part * 32 + 16 : part * 32 + 32, :].reshape(pre, LANES)
    base = 2 * pre
    for slot in range(HEADS):
        src = (oth_lo if slot < 2 else oth_hi).at[slot % 2]
        keys[base + slot * ROWS : base + (slot + 1) * ROWS, :] = src[0:ROWS, :]
        values[base + slot * ROWS : base + (slot + 1) * ROWS, :] = src[ROWS : 2 * ROWS, :]
    base = 2 * pre + half
    for slot in range(HEADS):
        keys[base + slot * ROWS : base + (slot + 1) * ROWS, :] = kvm[slot, 0:ROWS, :]
        values[base + slot * ROWS : base + (slot + 1) * ROWS, :] = kvm[slot, ROWS : 2 * ROWS, :]
    for at in range(0, total, chunk):
        keys_t[:, at : at + chunk] = keys[at : at + chunk, :].astype(jnp.float32).T.astype(jnp.bfloat16)
    dk_acc[...] = jnp.zeros_like(dk_acc)
    dv_acc[...] = jnp.zeros_like(dv_acc)
    wide = GROUPS * ROWS

    @pl.loop(0, HEADS)
    def _(tile):
        queries = qg[tile, 0:wide, :]
        grads = qg[tile, wide : 2 * wide, :]
        misc = kvm[tile, 2 * ROWS : 2 * ROWS + 16, :].astype(jnp.float32)
        delta = jnp.concatenate([misc[8 + s : 9 + s] for s in range(GROUPS)], axis=1)
        position = tile * ROWS + lax.rem(lax.broadcasted_iota(jnp.int32, (chunk, wide), 1), ROWS)
        key_at = lax.broadcasted_iota(jnp.int32, (chunk, wide), 0)
        top = jnp.full((1, wide), NEG, jnp.float32)
        for at in range(0, total, chunk):
            s = dot_nt(keys[at : at + chunk, :], queries) * (scale * LOG2E)
            if at >= 2 * pre + half:
                s = jnp.where(key_at + (at - 2 * pre - half) <= position, s, NEG)
            elif at >= 2 * pre:
                s = jnp.where(cb == 1, s, NEG)
            scores[at : at + chunk, :] = s
            top = jnp.maximum(top, jnp.max(s, axis=0, keepdims=True))
        norm = jnp.zeros((1, wide), jnp.float32)
        for at in range(0, total, chunk):
            e = jnp.exp2(scores[at : at + chunk, :] - top)
            scores[at : at + chunk, :] = e
            norm = norm + jnp.sum(e, axis=0, keepdims=True)
        inverse = 1.0 / norm
        dq_t = jnp.zeros((LANES, wide), jnp.float32)
        for at in range(0, total, chunk):
            p = scores[at : at + chunk, :] * inverse
            dp = dot_nt(values[at : at + chunk, :], grads)
            ds = (p * (dp - delta)).astype(jnp.bfloat16)
            dv_acc[at : at + chunk, :] += dot_nn(p.astype(jnp.bfloat16), grads)
            dk_acc[at : at + chunk, :] += dot_nn(ds, queries)
            dq_t = dq_t + dot_nn(keys_t[:, at : at + chunk], ds)
        dq[tile, :, :] = (dq_t.T * scale).astype(jnp.bfloat16)

    for part, base in ((0, 0), (1, pre)):
        pgrad[:, part * 32 : part * 32 + 16, :] = (
            (dk_acc[base : base + pre, :] * scale).astype(jnp.bfloat16).reshape(n_sib, 16, LANES)
        )
        pgrad[:, part * 32 + 16 : part * 32 + 32, :] = (
            dv_acc[base : base + pre, :].astype(jnp.bfloat16).reshape(n_sib, 16, LANES)
        )
    for out, base, which in (
        (minus, 2 * pre, tp),
        (plus, 2 * pre, 1 - tp),
        (keep, 2 * pre + half, tp),
        (send8, 2 * pre + half, 1 - tp),
    ):
        for slot in range(HEADS):
            rows = pl.ds(pl.multiple_of(base + slot * ROWS + which * (ROWS // 2), ROWS // 2), ROWS // 2)
            out[slot, 0 : ROWS // 2, :] = (dk_acc[rows, :] * scale).astype(jnp.bfloat16)
            out[slot, ROWS // 2 : ROWS, :] = dv_acc[rows, :].astype(jnp.bfloat16)


def unpack_kernel(dq, sib, dq_out, sk_out, sv_out):
    for h in range(HEADS):
        cols = slice(h * LANES, (h + 1) * LANES)
        for slot in range(GROUPS):
            dq_out[slot, :, cols] = dq[h, slot * ROWS : (slot + 1) * ROWS, :]
        sk_out[:, cols] = sib[h, 0 : ROWS // 2, :]
        sv_out[:, cols] = sib[h, ROWS // 2 : ROWS, :]


def ring_index(position):
    return (position % 8) * 2 + position // 8


def ring(shift, sources=range(16)):
    return [(ring_index(p), ring_index((p + shift) % 16)) for p in sources]


def on_device(n_sib, queries, gradient, forward, sib_k, sib_v, pre_k, pre_v, lengths):
    bf16 = jnp.bfloat16
    shape = jax.ShapeDtypeStruct
    cb, tp = lax.axis_index("cb"), lax.axis_index("tp")
    late = [p for p in range(16) if p % 8 >= 4]

    kvm, qg = pl.pallas_call(
        pack_kernel,
        out_shape=(shape((HEADS, 272, LANES), bf16), shape((HEADS, 512, LANES), bf16)),
        in_specs=[pl.BlockSpec(memory_space=pltpu.SMEM)] + vmem(7),
        out_specs=tuple(vmem(2)),
        cost_estimate=cost(1 << 20, 2 << 20),
        name="pack_heads",
    )(lengths, queries[0], gradient[0], forward[0], sib_k[0], sib_v[0], pre_k, pre_v)

    kvm = lax.all_to_all(kvm, "cq", 0, 0)
    qg = lax.all_to_all(qg, "cq", 0, 0)
    own_rows = jnp.concatenate(
        [kvm[:, 256:260].reshape(16, LANES), kvm[:, 260:264].reshape(16, LANES)], 0
    )
    other_rows = lax.ppermute(own_rows, "cb", [(0, 1), (1, 0)])
    own_kv = kvm[:, 0:256]
    oth_lo = lax.ppermute(own_kv[0:2], Z, ring(4, [p for p in range(16) if p % 8 < 4]))
    oth_hi = lax.ppermute(own_kv[2:4], Z, ring(-4, [p for p in range(16) if p % 8 < 4]))
    spread = jnp.broadcast_to(jnp.concatenate([own_rows, other_rows], 0)[None], (n_sib, 64, LANES))
    pref = lax.all_to_all(spread, "sib", 0, 0)

    total = 2 * n_sib * 16 + 2 * HEADS * ROWS
    wide = GROUPS * ROWS
    piece = shape((HEADS, ROWS, LANES), bf16)
    dq, pgrad, keep, send8, plus, minus = pl.pallas_call(
        functools.partial(main_kernel, min(256, n_sib * 16), n_sib),
        out_shape=(
            shape((HEADS, wide, LANES), bf16),
            shape((n_sib, 64, LANES), bf16),
            piece,
            piece,
            piece,
            piece,
        ),
        in_specs=vmem(5),
        out_specs=tuple(vmem(6)),
        scratch_shapes=[
            pltpu.VMEM((total, LANES), bf16),
            pltpu.VMEM((total, LANES), bf16),
            pltpu.VMEM((LANES, total), bf16),
            pltpu.VMEM((total, wide), jnp.float32),
            pltpu.VMEM((total, LANES), jnp.float32),
            pltpu.VMEM((total, LANES), jnp.float32),
        ],
        compiler_params=pltpu.CompilerParams(vmem_limit_bytes=32 << 20),
        cost_estimate=cost(10 * HEADS * wide * total * LANES, 4 << 20, HEADS * wide * total),
        name="attention_grads",
    )(qg, kvm, oth_lo, oth_hi, pref)

    got8 = lax.ppermute(send8, Z, ring(8))
    got_plus = lax.ppermute(plus, Z, ring(4, late))
    got_minus = lax.ppermute(minus, Z, ring(-4, late))

    pparts = lax.all_to_all(pgrad, "sib", 0, 0)
    psum = jnp.sum(pparts.astype(jnp.float32), 0).reshape(2, 2, HEADS, 2, 2, LANES)
    plus_tp = jnp.where(cb == 1, 1 - tp, tp)

    def rows_for(part, which):
        return lax.dynamic_index_in_dim(psum[part], which, 2, False).reshape(16, LANES)

    mine = (
        rows_for(0, tp)
        + lax.ppermute(rows_for(0, 1 - tp), Z, ring(8))
        + lax.ppermute(rows_for(1, plus_tp), Z, ring(4))
        + lax.ppermute(rows_for(1, 1 - plus_tp), Z, ring(-4))
    )

    f32 = jnp.float32
    sib = (
        keep.astype(f32) + got8.astype(f32) + got_plus.astype(f32) + got_minus.astype(f32)
    ).astype(bf16)
    back = lax.all_to_all(jnp.concatenate([dq, sib], 1), "cq", 0, 0)
    small = lax.all_to_all(mine.reshape(2, HEADS, 2, LANES).swapaxes(0, 1), "cq", 0, 0)
    out_k = small[:, 0].swapaxes(0, 1).reshape(2, HEADS * LANES).astype(bf16)
    out_v = small[:, 1].swapaxes(0, 1).reshape(2, HEADS * LANES).astype(bf16)

    dq_out, sk_out, sv_out = pl.pallas_call(
        unpack_kernel,
        out_shape=(
            shape((GROUPS, ROWS, HEADS * LANES), bf16),
            shape((ROWS // 2, HEADS * LANES), bf16),
            shape((ROWS // 2, HEADS * LANES), bf16),
        ),
        in_specs=vmem(2),
        out_specs=tuple(vmem(3)),
        cost_estimate=cost(1 << 10, 1 << 20),
        name="unpack_heads",
    )(back[:, 0:wide], back[:, wide:])
    return dq_out[None], sk_out[None], sv_out[None], out_k, out_v


def solution(mesh):
    n_sib, n_ctx, n_tp = mesh.shape["sib"], mesh.shape["ctx"], mesh.shape["tp"]
    fine = Mesh(
        mesh.devices.reshape(n_sib, n_ctx // HEADS, HEADS, n_tp), ("sib", "cb", "cq", "tp")
    )
    ctx = ("cb", "cq")
    heads = P("sib", "tp", ctx, None)
    return jax.shard_map(
        functools.partial(on_device, n_sib),
        mesh=fine,
        in_specs=(
            heads,
            heads,
            heads,
            P("sib", ctx, None),
            P("sib", ctx, None),
            P(("sib",) + ctx, None),
            P(("sib",) + ctx, None),
            P(),
        ),
        out_specs=(
            heads,
            P("sib", ctx + ("tp",), None),
            P("sib", ctx + ("tp",), None),
            P(("sib",) + ctx + ("tp",), None),
            P(("sib",) + ctx + ("tp",), None),
        ),
        check_vma=False,
    )
```

time: 1220 us -> 165 us (0.14)
  the two profiles are of different devices: /device:TPU:1 before, /device:TPU:2 now
where the time goes in v1:
time: 165 us; the launch traced here: 164 us
  starting transfers between devices  72.5 us (44%)
  waiting for transfers between devices  38.7 us (23%)
  blocking collectives  33 us (20%)
  Pallas kernels  15 us (9%)
  local copies, waits for them, and re-layouts  2.72 us (2%)
    all_to_all x1, blocking collectives, on_device(): pref = lax.all_to_all(spread, 'sib', 0, 0)  17.9 us
    ppermute x1, waiting for transfers between devices, on_device(): got_minus = lax.ppermute(minus, Z, ring(-4, late))  17.6 us
    all_to_all x1, blocking collectives, on_device(): kvm = lax.all_to_all(kvm, 'cq', 0, 0)  15.1 us
    ppermute x1, starting transfers between devices, on_device(): got8 = lax.ppermute(send8, Z, ring(8))  12.2 us
    pallas_call x1, Pallas kernels, on_device(): pl.pallas_call(functools.partial(main_kernel, min(256, n_sib * 16), n_sib...  10.7 us
    ppermute x1, starting transfers between devices, on_device(): other_rows = lax.ppermute(own_rows, 'cb', [(0, 1), (1, 0)])  9.1 us
    ppermute x1, starting transfers between devices, on_device(): lax.ppermute(own_kv[0:2], Z, ring(4, [p for p in range(16) if p % 8 < 4]))  7.72 us
    all_to_all x1, starting transfers between devices, on_device(): back = lax.all_to_all(jnp.concatenate([dq, sib], 1), 'cq', 0, 0)  7.61 us
  transfers between devices with their start and end apart: 13, of which 7 were waited for; matrix products, arithmetic and copies ran while one was open for 2% of the time, Pallas kernels for 0%

profile of v1, /device:TPU:2, one launch (start us, length us, event | category | flops | bytes accessed | tf_op | source)
XLA Modules:
  0.0 163.8 jit_solution(311660120315584342)
XLA Ops:
  0.6 2.5 %pack_heads.1 = (bf16[4,272,128]{2,1,0:T(8,128)(2,1)}, bf16[4,512,128]{2,1,0:T(8,128)(2,1)}) custom-call(s32[32]{0:T(128)} %lengths.1, bf16[2,128,512]{2,1,0:T(8,128)(2,1)} %bitcast.31, bf16[2,128,512]{2,1,0:T(8,128)(2,1)} %bitcast.32, bf16[2,128,512]{2,1,0:T(8,128)(2,1)} %bitcast.33, bf16[128,512]{1,0:T(8,128)(2,1)} %bitcast.34, bf16[128,512]{1,0:T(8,128)(2,1)} %bitcast.35, ...), custom_call_target="tpu_custom_call" | custom-call | flops 1048576 | bytes 2097152 | tf_op jit(solution)/shard_map/pack_heads/pallas_call | solution.py:171
  3.1 15.1 %all_to_all.30.kvm = bf16[4,272,128]{2,1,0:T(8,128)(2,1)S(1)} all-to-all(bf16[4,272,128]{2,1,0:T(8,128)(2,1)} %get-tuple-element.17), channel_id=1, replica_groups=mesh['sib'=32,'cb'=2,'cq'=4,'tp'=2] {'cq'}, dimensions={0} | all-to-all | bytes 557056 | tf_op jit(solution)/shard_map/all_to_all | solution.py:180
  18.3 9.1 %collective-permute-start.2 = (bf16[32,128]{1,0:T(8,128)(2,1)S(1)}, bf16[32,128]{1,0:T(8,128)(2,1)S(1)}, u32[]{:S(2)}, u32[]{:S(2)}) collective-permute-start(bf16[32,128]{1,0:T(8,128)(2,1)S(1)} %pad_maximum_fusion.2), channel_id=1, source_target_pairs={{0,8},{8,0},{1,9},{9,1},{2,10},{10,2},{3,11},{11,3},{4,12},{12,4},... | collective-permute-start | bytes 24584 | tf_op jit(solution)/shard_map/ppermute | solution.py:185
  27.4 1.7 %collective-permute-done.2 = bf16[32,128]{1,0:T(8,128)(2,1)S(1)} collective-permute-done((bf16[32,128]{1,0:T(8,128)(2,1)S(1)}, bf16[32,128]{1,0:T(8,128)(2,1)S(1)}, u32[]{:S(2)}, u32[]{:S(2)}) %collective-permute-start.2) | collective-permute-done | bytes 8224 | tf_op jit(solution)/shard_map/ppermute | solution.py:185
  29.1 0.1 broadcast_in_dim.15
  29.2 17.9 %all_to_all.31.pref = bf16[32,64,128]{2,1,0:T(8,128)(2,1)S(1)} all-to-all(bf16[32,64,128]{2,1,0:T(8,128)(2,1)S(1)} %broadcast_in_dim.15), channel_id=1, replica_groups=mesh['sib'=32,'cb'=2,'cq'=4,'tp'=2] {'sib'}, dimensions={0} | all-to-all | bytes 1048576 | tf_op jit(solution)/shard_map/all_to_all | solution.py:190
  47.1 3.5 %all-to-all-start = ((bf16[4,512,128]{2,1,0:T(8,128)(2,1)}), bf16[4,512,128]{2,1,0:T(8,128)(2,1)S(1)}, u32[]{:S(2)}, u32[]{:S(2)}) async-start(bf16[4,512,128]{2,1,0:T(8,128)(2,1)} %get-tuple-element.16), calls=%async_computation | async-start | bytes 1048576 | tf_op jit(solution)/shard_map/all_to_all | solution.py:181
  50.6 7.7 %collective-permute-start = (bf16[2,256,128]{2,1,0:T(8,128)(2,1)S(1)}, bf16[2,256,128]{2,1,0:T(8,128)(2,1)S(1)}, u32[]{:S(2)}, u32[]{:S(2)}) collective-permute-start(bf16[2,256,128]{2,1,0:T(8,128)(2,1)S(1)} %get-tuple-element.30), channel_id=1, source_target_pairs={{0,8},{2,10},{4,12},{6,14},{1,9},{3,11},{5,13},{7,15},{16,24},{18,... | collective-permute-start | bytes 393224 | tf_op jit(solution)/shard_map/ppermute | solution.py:187
  58.4 2.7 %collective-permute-start.1 = (bf16[2,256,128]{2,1,0:T(8,128)(2,1)S(1)}, bf16[2,256,128]{2,1,0:T(8,128)(2,1)S(1)}, u32[]{:S(2)}, u32[]{:S(2)}) collective-permute-start(bf16[2,256,128]{2,1,0:T(8,128)(2,1)S(1)} %get-tuple-element.29), channel_id=1, source_target_pairs={{0,9},{2,11},{4,13},{6,15},{1,8},{3,10},{5,12},{7,14},{16,25},{18,... | collective-permute-start | bytes 393224 | tf_op jit(solution)/shard_map/ppermute | solution.py:188
  61.1 1.8 %collective-permute-done.oth_lo = bf16[2,256,128]{2,1,0:T(8,128)(2,1)S(1)} collective-permute-done((bf16[2,256,128]{2,1,0:T(8,128)(2,1)S(1)}, bf16[2,256,128]{2,1,0:T(8,128)(2,1)S(1)}, u32[]{:S(2)}, u32[]{:S(2)}) %collective-permute-start) | collective-permute-done | bytes 131104 | tf_op jit(solution)/shard_map/ppermute | solution.py:187
  62.9 5.2 %collective-permute-done.1.oth_hi = bf16[2,256,128]{2,1,0:T(8,128)(2,1)S(1)} collective-permute-done((bf16[2,256,128]{2,1,0:T(8,128)(2,1)S(1)}, bf16[2,256,128]{2,1,0:T(8,128)(2,1)S(1)}, u32[]{:S(2)}, u32[]{:S(2)}) %collective-permute-start.1) | collective-permute-done | bytes 131104 | tf_op jit(solution)/shard_map/ppermute | solution.py:188
  68.1 1.2 all-to-all-done.qg
  69.4 10.7 %attention_grads.1 = (bf16[4,256,128]{2,1,0:T(8,128)(2,1)S(1)}, bf16[32,64,128]{2,1,0:T(8,128)(2,1)}, bf16[4,128,128]{2,1,0:T(8,128)(2,1)S(1)}, bf16[4,128,128]{...) custom-call(bf16[4,512,128]{2,1,0:T(8,128)(2,1)S(1)} %all-to-all-done.qg, ...), custom_call_target="tpu_custom_call" | custom-call | flops 2684354560 | bytes 4194304 | tf_op jit(solution)/shard_map/attention_grads/pallas_call | solution.py:195
  80.1 5.1 %all-to-all-start.4 = ((bf16[32,64,128]{2,1,0:T(8,128)(2,1)}), bf16[32,64,128]{2,1,0:T(8,128)(2,1)S(1)}, u32[]{:S(2)}, u32[]{:S(2)}) async-start(bf16[32,64,128]{2,1,0:T(8,128)(2,1)} %get-tuple-element.26), calls=%async_computation.4 | async-start | bytes 1048576 | tf_op jit(solution)/shard_map/all_to_all | solution.py:224
  85.1 1.3 collective-permute-start.5
  86.4 1.3 collective-permute-start.4
  87.7 12.2 %collective-permute-start.3 = (bf16[4,128,128]{2,1,0:T(8,128)(2,1)S(1)}, bf16[4,128,128]{2,1,0:T(8,128)(2,1)S(1)}, u32[]{:S(2)}, u32[]{:S(2)}) collective-permute-start(bf16[4,128,128]{2,1,0:T(8,128)(2,1)S(1)} %get-tuple-element.20), channel_id=1, source_target_pairs={{0,1},{2,3},{4,5},{6,7},{8,9},{10,11},{12,13},{14,15},{1,0},{3,2},... | collective-permute-start | bytes 393224 | tf_op jit(solution)/shard_map/ppermute | solution.py:220
  99.9 17.6 %collective-permute-done.5 = bf16[4,128,128]{2,1,0:T(8,128)(2,1)S(1)} collective-permute-done((bf16[4,128,128]{2,1,0:T(8,128)(2,1)S(1)}, bf16[4,128,128]{2,1,0:T(8,128)(2,1)S(1)}, u32[]{:S(2)}, u32[]{:S(2)}) %collective-permute-start.5) | collective-permute-done | bytes 131104 | tf_op jit(solution)/shard_map/ppermute | solution.py:222
  117.5 0.0 collective-permute-done.4
  117.5 0.0 collective-permute-done.3
  117.5 0.1 add_convert_fusion
  117.6 0.8 pad_maximum_fusion
  118.4 0.0 all-to-all-done.4
  118.4 7.6 %all-to-all-start.3 = ((bf16[4,384,128]{2,1,0:T(8,128)(2,1)}), bf16[4,384,128]{2,1,0:T(8,128)(2,1)S(1)}, u32[]{:S(2)}, u32[]{:S(2)}) async-start(bf16[4,384,128]{2,1,0:T(8,128)(2,1)} %pad_maximum_fusion), calls=%async_computation.3 | async-start | bytes 786432 | tf_op jit(solution)/shard_map/all_to_all | solution.py:242
  126.0 0.1 convert_reduce_fusion
  126.1 4.6 %collective-permute-start.8 = (f32[16,128]{1,0:T(8,128)S(1)}, f32[16,128]{1,0:T(8,128)S(1)}, u32[]{:S(2)}, u32[]{:S(2)}) collective-permute-start(f32[16,128]{1,0:T(8,128)S(1)} %bitcast.45), channel_id=1, source_target_pairs={{0,9},{2,11},{4,13},{6,15},{8,0},{10,2},{12,4},{14,6},{1,8},{3,10}... | collective-permute-start | bytes 24584 | tf_op jit(solution)/shard_map/ppermute | solution.py:235
  130.7 5.2 %collective-permute-start.7 = (f32[16,128]{1,0:T(8,128)S(1)}, f32[16,128]{1,0:T(8,128)S(1)}, u32[]{:S(2)}, u32[]{:S(2)}) collective-permute-start(f32[16,128]{1,0:T(8,128)S(1)} %bitcast.44), channel_id=1, source_target_pairs={{0,8},{2,10},{4,12},{6,14},{8,1},{10,3},{12,5},{14,7},{1,9},{3,11}... | collective-permute-start | bytes 24584 | tf_op jit(solution)/shard_map/ppermute | solution.py:234
  135.9 7.3 %collective-permute-start.6 = (f32[16,128]{1,0:T(8,128)S(1)}, f32[16,128]{1,0:T(8,128)S(1)}, u32[]{:S(2)}, u32[]{:S(2)}) collective-permute-start(f32[16,128]{1,0:T(8,128)S(1)} %bitcast.46), channel_id=1, source_target_pairs={{0,1},{2,3},{4,5},{6,7},{8,9},{10,11},{12,13},{14,15},{1,0},{3,2},... | collective-permute-start | bytes 24584 | tf_op jit(solution)/shard_map/ppermute | solution.py:233
  143.2 0.0 collective-permute-done.8
  143.2 0.0 collective-permute-done.7
  143.2 7.0 %collective-permute-done.6 = f32[16,128]{1,0:T(8,128)S(1)} collective-permute-done((f32[16,128]{1,0:T(8,128)S(1)}, f32[16,128]{1,0:T(8,128)S(1)}, u32[]{:S(2)}, u32[]{:S(2)}) %collective-permute-start.6) | collective-permute-done | bytes 8224 | tf_op jit(solution)/shard_map/ppermute | solution.py:233
  150.1 0.6 copy.13
  150.7 0.0 all-to-all-done.3
  150.7 5.1 %all-to-all-start.5 = ((bf16[4,2,2,128]{3,2,1,0:T(2,128)(2,1)}), bf16[4,2,2,128]{3,2,1,0:T(2,128)(2,1)S(1)}, u32[]{:S(2)}, u32[]{:S(2)}) async-start(bf16[4,2,2,128]{3,2,1,0:T(2,128)(2,1)} %copy.13), calls=%async_computation.5 | async-start | bytes 8192 | tf_op jit(solution)/shard_map/all_to_all | solution.py:243
  155.8 0.7 slice.53.dq
  156.5 0.6 slice.54.sib
  157.2 4.2 %all-to-all-done.5 = bf16[4,2,2,128]{3,2,1,0:T(2,128)(2,1)S(1)} async-done(((bf16[4,2,2,128]{3,2,1,0:T(2,128)(2,1)}), bf16[4,2,2,128]{3,2,1,0:T(2,128)(2,1)S(1)}, u32[]{:S(2)}, u32[]{:S(2)}) %all-to-all-start.5) | async-done | bytes 4128 | tf_op jit(solution)/shard_map/all_to_all | solution.py:243
  161.4 0.6 slice_bitcast_fusion
  162.0 1.8 %unpack_heads.1 = (bf16[2,128,512]{2,1,0:T(8,128)(2,1)}, bf16[64,512]{1,0:T(8,128)(2,1)}, bf16[64,512]{1,0:T(8,128)(2,1)}) custom-call(bf16[4,256,128]{2,1,0:T(8,128)(2,1)} %slice.53.dq, bf16[4,128,128]{2,1,0:T(8,128)(2,1)} %slice.54.sib), custom_call_target="tpu_custom_call" | custom-call | flops 1024 | bytes 1048576 | tf_op jit(solution)/shard_map/unpack_heads/pallas_call | solution.py:247
  (8 shorter events, 0.1 us)
Async XLA Ops:
  18.3 10.8 %collective-permute-start.2 = (bf16[32,128]{1,0:T(8,128)(2,1)S(1)}, bf16[32,128]{1,0:T(8,128)(2,1)S(1)}, u32[]{:S(2)}, u32[]{:S(2)}) collective-permute-start(bf16[32,128]{1,0:T(8,128)(2,1)S(1)} %pad_maximum_fusion.2), channel_id=1, source_target_pairs={{0,8},{8,0},{1,9},{9,1},{2,10},{10,2},{3,11},{11,3},{4,12},{12,4},... | collective-permute-start | bytes 24584 | tf_op jit(solution)/shard_map/ppermute | solution.py:185
  47.1 22.2 %all-to-all-start = ((bf16[4,512,128]{2,1,0:T(8,128)(2,1)}), bf16[4,512,128]{2,1,0:T(8,128)(2,1)S(1)}, u32[]{:S(2)}, u32[]{:S(2)}) async-start(bf16[4,512,128]{2,1,0:T(8,128)(2,1)} %get-tuple-element.16), calls=%async_computation | async-start | bytes 1048576 | tf_op jit(solution)/shard_map/all_to_all | solution.py:181
  50.6 12.3 %collective-permute-start = (bf16[2,256,128]{2,1,0:T(8,128)(2,1)S(1)}, bf16[2,256,128]{2,1,0:T(8,128)(2,1)S(1)}, u32[]{:S(2)}, u32[]{:S(2)}) collective-permute-start(bf16[2,256,128]{2,1,0:T(8,128)(2,1)S(1)} %get-tuple-element.30), channel_id=1, source_target_pairs={{0,8},{2,10},{4,12},{6,14},{1,9},{3,11},{5,13},{7,15},{16,24},{18,... | collective-permute-start | bytes 393224 | tf_op jit(solution)/shard_map/ppermute | solution.py:187
  58.4 9.7 %collective-permute-start.1 = (bf16[2,256,128]{2,1,0:T(8,128)(2,1)S(1)}, bf16[2,256,128]{2,1,0:T(8,128)(2,1)S(1)}, u32[]{:S(2)}, u32[]{:S(2)}) collective-permute-start(bf16[2,256,128]{2,1,0:T(8,128)(2,1)S(1)} %get-tuple-element.29), channel_id=1, source_target_pairs={{0,9},{2,11},{4,13},{6,15},{1,8},{3,10},{5,12},{7,14},{16,25},{18,... | collective-permute-start | bytes 393224 | tf_op jit(solution)/shard_map/ppermute | solution.py:188
  80.1 38.3 %all-to-all-start.4 = ((bf16[32,64,128]{2,1,0:T(8,128)(2,1)}), bf16[32,64,128]{2,1,0:T(8,128)(2,1)S(1)}, u32[]{:S(2)}, u32[]{:S(2)}) async-start(bf16[32,64,128]{2,1,0:T(8,128)(2,1)} %get-tuple-element.26), calls=%async_computation.4 | async-start | bytes 1048576 | tf_op jit(solution)/shard_map/all_to_all | solution.py:224
  85.1 32.3 %collective-permute-start.5 = (bf16[4,128,128]{2,1,0:T(8,128)(2,1)S(1)}, bf16[4,128,128]{2,1,0:T(8,128)(2,1)S(1)}, u32[]{:S(2)}, u32[]{:S(2)}) collective-permute-start(bf16[4,128,128]{2,1,0:T(8,128)(2,1)S(1)} %get-tuple-element.22), channel_id=1, source_target_pairs={{8,0},{10,2},{12,4},{14,6},{9,1},{11,3},{13,5},{15,7},{24,16},{26,... | collective-permute-start | bytes 393224 | tf_op jit(solution)/shard_map/ppermute | solution.py:222
  86.4 31.0 %collective-permute-start.4 = (bf16[4,128,128]{2,1,0:T(8,128)(2,1)S(1)}, bf16[4,128,128]{2,1,0:T(8,128)(2,1)S(1)}, u32[]{:S(2)}, u32[]{:S(2)}) collective-permute-start(bf16[4,128,128]{2,1,0:T(8,128)(2,1)S(1)} %get-tuple-element.21), channel_id=1, source_target_pairs={{8,1},{10,3},{12,5},{14,7},{9,0},{11,2},{13,4},{15,6},{24,17},{26,... | collective-permute-start | bytes 393224 | tf_op jit(solution)/shard_map/ppermute | solution.py:221
  87.7 29.7 %collective-permute-start.3 = (bf16[4,128,128]{2,1,0:T(8,128)(2,1)S(1)}, bf16[4,128,128]{2,1,0:T(8,128)(2,1)S(1)}, u32[]{:S(2)}, u32[]{:S(2)}) collective-permute-start(bf16[4,128,128]{2,1,0:T(8,128)(2,1)S(1)} %get-tuple-element.20), channel_id=1, source_target_pairs={{0,1},{2,3},{4,5},{6,7},{8,9},{10,11},{12,13},{14,15},{1,0},{3,2},... | collective-permute-start | bytes 393224 | tf_op jit(solution)/shard_map/ppermute | solution.py:220
  118.4 32.4 %all-to-all-start.3 = ((bf16[4,384,128]{2,1,0:T(8,128)(2,1)}), bf16[4,384,128]{2,1,0:T(8,128)(2,1)S(1)}, u32[]{:S(2)}, u32[]{:S(2)}) async-start(bf16[4,384,128]{2,1,0:T(8,128)(2,1)} %pad_maximum_fusion), calls=%async_computation.3 | async-start | bytes 786432 | tf_op jit(solution)/shard_map/all_to_all | solution.py:242
  126.1 17.1 %collective-permute-start.8 = (f32[16,128]{1,0:T(8,128)S(1)}, f32[16,128]{1,0:T(8,128)S(1)}, u32[]{:S(2)}, u32[]{:S(2)}) collective-permute-start(f32[16,128]{1,0:T(8,128)S(1)} %bitcast.45), channel_id=1, source_target_pairs={{0,9},{2,11},{4,13},{6,15},{8,0},{10,2},{12,4},{14,6},{1,8},{3,10}... | collective-permute-start | bytes 24584 | tf_op jit(solution)/shard_map/ppermute | solution.py:235
  130.7 12.5 %collective-permute-start.7 = (f32[16,128]{1,0:T(8,128)S(1)}, f32[16,128]{1,0:T(8,128)S(1)}, u32[]{:S(2)}, u32[]{:S(2)}) collective-permute-start(f32[16,128]{1,0:T(8,128)S(1)} %bitcast.44), channel_id=1, source_target_pairs={{0,8},{2,10},{4,12},{6,14},{8,1},{10,3},{12,5},{14,7},{1,9},{3,11}... | collective-permute-start | bytes 24584 | tf_op jit(solution)/shard_map/ppermute | solution.py:234
  135.9 14.3 %collective-permute-start.6 = (f32[16,128]{1,0:T(8,128)S(1)}, f32[16,128]{1,0:T(8,128)S(1)}, u32[]{:S(2)}, u32[]{:S(2)}) collective-permute-start(f32[16,128]{1,0:T(8,128)S(1)} %bitcast.46), channel_id=1, source_target_pairs={{0,1},{2,3},{4,5},{6,7},{8,9},{10,11},{12,13},{14,15},{1,0},{3,2},... | collective-permute-start | bytes 24584 | tf_op jit(solution)/shard_map/ppermute | solution.py:233
  150.7 10.7 %all-to-all-start.5 = ((bf16[4,2,2,128]{3,2,1,0:T(2,128)(2,1)}), bf16[4,2,2,128]{3,2,1,0:T(2,128)(2,1)S(1)}, u32[]{:S(2)}, u32[]{:S(2)}) async-start(bf16[4,2,2,128]{3,2,1,0:T(2,128)(2,1)} %copy.13), calls=%async_computation.5 | async-start | bytes 8192 | tf_op jit(solution)/shard_map/all_to_all | solution.py:243

commit v2 on v1

v2 whole, which is shorter than its diff:
```python
import functools
import math

import jax
import jax.numpy as jnp
from jax import lax
from jax.experimental import pallas as pl
from jax.experimental.pallas import tpu as pltpu
from jax.sharding import Mesh, PartitionSpec as P

HEADS = 4
LANES = 128
ROWS = 128
GROUPS = 2
LOG2E = math.log2(math.e)
NEG = -1e30
Z = ("cb", "cq", "tp")


def dot_nt(a, b):
    return lax.dot_general(a, b, (((1,), (1,)), ((), ())), preferred_element_type=jnp.float32)


def dot_nn(a, b):
    return lax.dot_general(a, b, (((1,), (0,)), ((), ())), preferred_element_type=jnp.float32)


def vmem(n):
    return [pl.BlockSpec(memory_space=pltpu.VMEM)] * n


def cost(flops, moved, exps=0):
    return pl.CostEstimate(flops=flops, bytes_accessed=moved, transcendentals=exps)


def pack_kernel(lengths, q, g, o, k, v, bulk):
    ctx = lax.axis_index("cb") * HEADS + lax.axis_index("cq")
    length = lengths[lax.axis_index("sib")]
    row = lax.broadcasted_iota(jnp.int32, (ROWS, LANES), 0) + ctx * ROWS
    live = row < length
    ones = jnp.ones((8, LANES), jnp.bfloat16)
    for h in range(HEADS):
        cols = slice(h * LANES, (h + 1) * LANES)
        bulk[h, 4 * ROWS : 5 * ROWS, :] = k[:, cols]
        bulk[h, 5 * ROWS : 6 * ROWS, :] = v[:, cols]
        deltas = []
        for slot in range(GROUPS):
            rows = slice(slot * ROWS, (slot + 1) * ROWS)
            bulk[h, rows, :] = q[slot, :, cols]
            grad = jnp.where(live, g[slot, :, cols].astype(jnp.float32), 0.0)
            bulk[h, GROUPS * ROWS + slot * ROWS : GROUPS * ROWS + (slot + 1) * ROWS, :] = grad.astype(
                jnp.bfloat16
            )
            prod = grad * o[slot, :, cols].astype(jnp.float32)
            high = prod.astype(jnp.bfloat16)
            low = (prod - high.astype(jnp.float32)).astype(jnp.bfloat16)
            deltas.append((dot_nt(ones, high) + dot_nt(ones, low))[0:1])
        rest = jnp.concatenate(deltas + [jnp.zeros((14, LANES), jnp.float32)], axis=0)
        bulk[h, 6 * ROWS : 6 * ROWS + 16, :] = rest.astype(jnp.bfloat16)


def pack_prefix_kernel(pk, pv, pre):
    for h in range(HEADS):
        cols = slice(h * LANES, (h + 1) * LANES)
        own = jnp.concatenate(
            [
                pk[:, cols].astype(jnp.float32),
                pv[:, cols].astype(jnp.float32),
                jnp.zeros((8, LANES), jnp.float32),
            ],
            axis=0,
        ).astype(jnp.bfloat16)
        for half in range(2):
            pre[half * HEADS + h] = own


def spread_kernel(pre, out):
    rows = [pre[at].astype(jnp.float32) for at in range(2 * HEADS)]
    block = []
    for half in range(2):
        mine = rows[half * HEADS : (half + 1) * HEADS]
        block += [r[0:4] for r in mine] + [r[4:8] for r in mine]
    block = jnp.concatenate(block, axis=0).astype(jnp.bfloat16)
    for at in range(out.shape[0]):
        out[at] = block


def load_keys(pref, keys, values):
    pre = pref.shape[0] * 16
    for part in range(2):
        rows = slice(part * pre, (part + 1) * pre)
        keys[rows, :] = pref[:, part * 32 : part * 32 + 16, :].reshape(pre, LANES)
        values[rows, :] = pref[:, part * 32 + 16 : part * 32 + 32, :].reshape(pre, LANES)


def tile_data(bulk, step):
    wide = GROUPS * ROWS
    rest = bulk[step, 6 * ROWS : 6 * ROWS + 16, :].astype(jnp.float32)
    delta = jnp.concatenate([rest[s : s + 1] for s in range(GROUPS)], axis=1)
    return bulk[step, 0:wide, :], bulk[step, wide : 2 * wide, :], delta


def gather_bulk(bulk, own, far1, far2, far3):
    bulk[0] = own[lax.axis_index("cq")]
    for step, received in ((1, far1), (2, far2), (3, far3)):
        bulk[step] = received[...]


def transpose_keys(keys, keys_t, start, stop, chunk):
    for at in range(start, stop, chunk):
        keys_t[:, at - start : at - start + chunk] = (
            keys[at : at + chunk, :].astype(jnp.float32).T.astype(jnp.bfloat16)
        )


def load_sibling(bulk, oth_lo, oth_hi, keys, values, base):
    cq = lax.axis_index("cq")
    half = HEADS * ROWS
    for step in range(HEADS):
        at = jnp.bitwise_xor(cq, step) * ROWS
        src = (oth_lo if step < 2 else oth_hi).at[step % 2]
        rows = pl.ds(pl.multiple_of(base + at, ROWS), ROWS)
        keys[rows, :] = src[0:ROWS, :]
        if values is not None:
            values[rows, :] = src[ROWS : 2 * ROWS, :]
        rows = pl.ds(pl.multiple_of(base + half + at, ROWS), ROWS)
        keys[rows, :] = bulk[step, 4 * ROWS : 5 * ROWS, :]
        if values is not None:
            values[rows, :] = bulk[step, 5 * ROWS : 6 * ROWS, :]


def sibling_scores(keys, queries, at, base, tile):
    half = HEADS * ROWS
    chunk = keys.shape[0]
    s = dot_nt(keys, queries) * (LOG2E / math.sqrt(LANES))
    if at >= base + half:
        position = tile * ROWS + lax.rem(lax.broadcasted_iota(jnp.int32, s.shape, 1), ROWS)
        key_at = lax.broadcasted_iota(jnp.int32, s.shape, 0) + (at - base - half)
        return jnp.where(key_at <= position, s, NEG)
    if at >= base:
        return jnp.where(lax.axis_index("cb") == 1, s, NEG)
    return s


def prefix_kernel(
    chunk, own, far1, far2, far3, oth_lo, oth_hi, pref,
    pgrad, norms, dq_part,
    keys, values, keys_t, scores, dk_acc, dv_acc, bulk,
):
    scale = 1.0 / math.sqrt(LANES)
    n_sib = pref.shape[0]
    pre = n_sib * 32
    total = keys.shape[0]
    wide = GROUPS * ROWS
    gather_bulk(bulk, own, far1, far2, far3)
    load_keys(pref, keys, values)
    load_sibling(bulk, oth_lo, oth_hi, keys, None, pre)
    transpose_keys(keys, keys_t, 0, pre, chunk)
    dk_acc[...] = jnp.zeros_like(dk_acc)
    dv_acc[...] = jnp.zeros_like(dv_acc)

    @pl.loop(0, HEADS)
    def _(step):
        tile = jnp.bitwise_xor(lax.axis_index("cq"), step)
        queries, grads, delta = tile_data(bulk, step)
        top = jnp.full((1, wide), NEG, jnp.float32)
        for at in range(0, total, chunk):
            s = sibling_scores(keys[at : at + chunk, :], queries, at, pre, tile)
            scores[at : at + chunk, :] = s
            top = jnp.maximum(top, jnp.max(s, axis=0, keepdims=True))
        norm = jnp.zeros((1, wide), jnp.float32)
        for at in range(0, total, chunk):
            e = jnp.exp2(scores[at : at + chunk, :] - top)
            if at < pre:
                scores[at : at + chunk, :] = e
            norm = norm + jnp.sum(e, axis=0, keepdims=True)
        norms[step] = jnp.broadcast_to(top + jnp.log2(norm), (8, wide))
        inverse = 1.0 / norm
        dq_t = jnp.zeros((LANES, wide), jnp.float32)
        for at in range(0, pre, chunk):
            rows = slice(at, at + chunk)
            p = scores[rows, :] * inverse
            dp = dot_nt(values[rows, :], grads)
            ds = (p * (dp - delta)).astype(jnp.bfloat16)
            dv_acc[rows, :] += dot_nn(p.astype(jnp.bfloat16), grads)
            dk_acc[rows, :] += dot_nn(ds, queries)
            dq_t = dq_t + dot_nn(keys_t[:, rows], ds)
        dq_part[step, :, :] = dq_t

    for part in range(2):
        rows = slice(part * pre // 2, (part + 1) * pre // 2)
        pgrad[:, part * 32 : part * 32 + 16, :] = (
            (dk_acc[rows, :] * scale).astype(jnp.bfloat16).reshape(n_sib, 16, LANES)
        )
        pgrad[:, part * 32 + 16 : part * 32 + 32, :] = (
            dv_acc[rows, :].astype(jnp.bfloat16).reshape(n_sib, 16, LANES)
        )


def sibling_kernel(
    chunk, own, far1, far2, far3, oth_lo, oth_hi, norms, dq_part,
    dq0, dq1, dq2, dq3, sgrad,
    keys, values, keys_t, dk_acc, dv_acc, bulk, dq,
):
    scale = 1.0 / math.sqrt(LANES)
    cb = lax.axis_index("cb")
    total = keys.shape[0]
    gather_bulk(bulk, own, far1, far2, far3)
    load_sibling(bulk, oth_lo, oth_hi, keys, values, 0)
    transpose_keys(keys, keys_t, 0, total, chunk)
    dk_acc[...] = jnp.zeros_like(dk_acc)
    dv_acc[...] = jnp.zeros_like(dv_acc)

    @pl.loop(0, HEADS)
    def _(step):
        tile = jnp.bitwise_xor(lax.axis_index("cq"), step)
        queries, grads, delta = tile_data(bulk, step)
        norm = norms[step][0:1]
        dq_t = dq_part[step]
        for at in range(0, total, chunk):
            rows = slice(at, at + chunk)
            p = jnp.exp2(sibling_scores(keys[rows, :], queries, at, 0, tile) - norm)
            dp = dot_nt(values[rows, :], grads)
            ds = (p * (dp - delta)).astype(jnp.bfloat16)
            dv_acc[rows, :] += dot_nn(p.astype(jnp.bfloat16), grads)
            dk_acc[rows, :] += dot_nn(ds, queries)
            dq_t = dq_t + dot_nn(keys_t[:, rows], ds)
        dq[step, :, :] = (dq_t.T * scale).astype(jnp.bfloat16)

    for step, out in enumerate((dq0, dq1, dq2, dq3)):
        out[...] = dq[step]
    for base, owner in ((0, 1 - cb), (HEADS * ROWS, cb)):
        for piece in range(2 * HEADS):
            rows = slice(base + piece * (ROWS // 2), base + (piece + 1) * (ROWS // 2))
            at = owner * 2 * HEADS + piece
            sgrad[at, 0 : ROWS // 2, :] = (dk_acc[rows, :] * scale).astype(jnp.bfloat16)
            sgrad[at, ROWS // 2 : ROWS, :] = dv_acc[rows, :].astype(jnp.bfloat16)


def prefix_sum_kernel(parts, sgrad, out):
    total = jnp.sum(parts[...].astype(jnp.float32), axis=0)
    for part in range(2):
        for piece in range(2 * HEADS):
            at = part * 32 + piece * 2
            rows = jnp.concatenate(
                [total[at : at + 2], total[at + 16 : at + 18], jnp.zeros((12, LANES), jnp.float32)],
                axis=0,
            )
            out[part * 2 * HEADS + piece, :, :] = rows.astype(jnp.bfloat16)


def unpack_kernel(dq0, dq1, dq2, dq3, parts, dq_out, sk_out, sv_out, pk_out, pv_out):
    cq = lax.axis_index("cq")
    half = ROWS // 2
    for step, dq in enumerate((dq0, dq1, dq2, dq3)):
        head = jnp.bitwise_xor(cq, step)
        cols = pl.ds(pl.multiple_of(head * LANES, LANES), LANES)
        for slot in range(GROUPS):
            dq_out[slot, :, cols] = dq[slot * ROWS : (slot + 1) * ROWS, :]
    for head in range(HEADS):
        cols = slice(head * LANES, (head + 1) * LANES)
        total = sum(
            parts[(b * HEADS + head) * 2 + t].astype(jnp.float32) for b in range(2) for t in range(2)
        ).astype(jnp.bfloat16)
        sk_out[:, cols] = total[0:half]
        sv_out[:, cols] = total[half:ROWS]
        pk_out[:, cols] = total[ROWS : ROWS + 2]
        pv_out[:, cols] = total[ROWS + 2 : ROWS + 4]


def ring_index(position):
    return (position % 8) * 2 + position // 8


def ring(shift, sources=range(16)):
    return [(ring_index(p), ring_index((p + shift) % 16)) for p in sources]


def on_device(n_sib, queries, gradient, forward, sib_k, sib_v, pre_k, pre_v, lengths):
    bf16 = jnp.bfloat16
    shape = jax.ShapeDtypeStruct

    pre = pl.pallas_call(
        pack_prefix_kernel,
        out_shape=shape((2 * HEADS, 16, LANES), bf16),
        in_specs=vmem(2),
        out_specs=vmem(1)[0],
        cost_estimate=cost(1 << 10, 1 << 16),
        name="pack_prefix",
    )(pre_k, pre_v)
    bulk = pl.pallas_call(
        pack_kernel,
        out_shape=shape((HEADS, 784, LANES), bf16),
        in_specs=[pl.BlockSpec(memory_space=pltpu.SMEM)] + vmem(5),
        out_specs=vmem(1)[0],
        cost_estimate=cost(1 << 20, 2 << 20),
        name="pack_heads",
    )(lengths, queries[0], gradient[0], forward[0], sib_k[0], sib_v[0])
    cq = lax.axis_index("cq")

    def swap(array, step):
        return lax.ppermute(array, "cq", [(i, i ^ step) for i in range(HEADS)])

    def slot(array, step):
        return lax.dynamic_index_in_dim(array, jnp.bitwise_xor(cq, step), 0, False)

    far = [swap(slot(bulk, d), d) for d in (1, 2, 3)]
    pre = lax.all_to_all(pre, ("cb", "cq"), 0, 0)
    early = [p for p in range(16) if p % 8 < 4]
    pairs = [a[4 * ROWS : 6 * ROWS] for a in [slot(bulk, 0)] + far]
    oth_lo = lax.ppermute(jnp.stack(pairs[0:2]), Z, ring(4, early))
    oth_hi = lax.ppermute(jnp.stack(pairs[2:4]), Z, ring(-4, early))
    spread = pl.pallas_call(
        spread_kernel,
        out_shape=shape((n_sib, 64, LANES), bf16),
        in_specs=vmem(1),
        out_specs=vmem(1)[0],
        cost_estimate=cost(1 << 18, 1 << 19),
        name="spread_prefix",
    )(pre)
    pref = lax.all_to_all(spread, "sib", 0, 0)

    chunk = min(256, n_sib * 16)
    pre_rows, sib_rows = 32 * n_sib, 2 * HEADS * ROWS
    wide = GROUPS * ROWS
    pgrad, norms, dq_part = pl.pallas_call(
        functools.partial(prefix_kernel, chunk),
        out_shape=(
            shape((n_sib, 64, LANES), bf16),
            shape((HEADS, 8, wide), jnp.float32),
            shape((HEADS, LANES, wide), jnp.float32),
        ),
        in_specs=vmem(7),
        out_specs=tuple(vmem(3)),
        scratch_shapes=[
            pltpu.VMEM((pre_rows + sib_rows, LANES), bf16),
            pltpu.VMEM((pre_rows, LANES), bf16),
            pltpu.VMEM((LANES, pre_rows), bf16),
            pltpu.VMEM((pre_rows + sib_rows, wide), jnp.float32),
            pltpu.VMEM((pre_rows, LANES), jnp.float32),
            pltpu.VMEM((pre_rows, LANES), jnp.float32),
            pltpu.VMEM((HEADS, 784, LANES), bf16),
        ],
        compiler_params=pltpu.CompilerParams(vmem_limit_bytes=32 << 20),
        cost_estimate=cost(6 * HEADS * wide * 2048 * LANES, 4 << 20, HEADS * wide * 2048),
        name="prefix_grads",
    )(bulk, *far, oth_lo, oth_hi, pref)
    *dq, sgrad = pl.pallas_call(
        functools.partial(sibling_kernel, chunk),
        out_shape=(shape((wide, LANES), bf16),) * 4 + (shape((16, ROWS + 16, LANES), bf16),),
        in_specs=vmem(8),
        out_specs=tuple(vmem(5)),
        scratch_shapes=[
            pltpu.VMEM((sib_rows, LANES), bf16),
            pltpu.VMEM((sib_rows, LANES), bf16),
            pltpu.VMEM((LANES, sib_rows), bf16),
            pltpu.VMEM((sib_rows, LANES), jnp.float32),
            pltpu.VMEM((sib_rows, LANES), jnp.float32),
            pltpu.VMEM((HEADS, 784, LANES), bf16),
            pltpu.VMEM((HEADS, wide, LANES), bf16),
        ],
        compiler_params=pltpu.CompilerParams(vmem_limit_bytes=32 << 20),
        cost_estimate=cost(10 * HEADS * wide * 1024 * LANES, 4 << 20, HEADS * wide * 1024),
        name="sibling_grads",
    )(bulk, *far, oth_lo, oth_hi, norms, dq_part)
    dq = [dq[0]] + [swap(dq[d], d) for d in (1, 2, 3)]

    parts = lax.all_to_all(pgrad, "sib", 0, 0)
    owners = pl.pallas_call(
        prefix_sum_kernel,
        out_shape=shape((16, ROWS + 16, LANES), bf16),
        grid=(1,),
        in_specs=[
            pl.BlockSpec((n_sib, 64, LANES), lambda i: (0, 0, 0)),
            pl.BlockSpec(memory_space=pl.ANY),
        ],
        out_specs=pl.BlockSpec((16, 16, LANES), lambda i: (0, ROWS // 16, 0)),
        input_output_aliases={1: 0},
        cost_estimate=cost(1 << 18, 1 << 19),
        name="prefix_sums",
    )(parts, sgrad)
    owners = lax.all_to_all(owners, Z, 0, 0)

    dq_out, sk_out, sv_out, pk_out, pv_out = pl.pallas_call(
        unpack_kernel,
        out_shape=(
            shape((GROUPS, ROWS, HEADS * LANES), bf16),
            shape((ROWS // 2, HEADS * LANES), bf16),
            shape((ROWS // 2, HEADS * LANES), bf16),
            shape((2, HEADS * LANES), bf16),
            shape((2, HEADS * LANES), bf16),
        ),
        in_specs=vmem(5),
        out_specs=tuple(vmem(5)),
        cost_estimate=cost(1 << 18, 1 << 20),
        name="unpack_heads",
    )(*dq, owners)
    return dq_out[None], sk_out[None], sv_out[None], pk_out, pv_out


def solution(mesh):
    n_sib, n_ctx, n_tp = mesh.shape["sib"], mesh.shape["ctx"], mesh.shape["tp"]
    fine = Mesh(
        mesh.devices.reshape(n_sib, n_ctx // HEADS, HEADS, n_tp), ("sib", "cb", "cq", "tp")
    )
    ctx = ("cb", "cq")
    heads = P("sib", "tp", ctx, None)
    return jax.shard_map(
        functools.partial(on_device, n_sib),
        mesh=fine,
        in_specs=(
            heads,
            heads,
            heads,
            P("sib", ctx, None),
            P("sib", ctx, None),
            P(("sib",) + ctx, None),
            P(("sib",) + ctx, None),
            P(),
        ),
        out_specs=(
            heads,
            P("sib", ctx + ("tp",), None),
            P("sib", ctx + ("tp",), None),
            P(("sib",) + ctx + ("tp",), None),
            P(("sib",) + ctx + ("tp",), None),
        ),
        check_vma=False,
    )
```

time: 165 us -> 139 us (0.84)
  the two profiles are of different devices: /device:TPU:2 before, /device:TPU:32 now
where the time goes in v2:
time: 139 us; the launch traced here: 138 us
  starting transfers between devices  67.3 us (48%)
  waiting for transfers between devices  42.8 us (31%)
  Pallas kernels  22 us (16%)
  local copies, waits for them, and re-layouts  5.01 us (4%)
    ppermute x6, waiting for transfers between devices, swap(): return lax.ppermute(array, 'cq', [(i, i ^ step) for i in range(HEADS)])  23 us
    ppermute x6, starting transfers between devices, swap(): return lax.ppermute(array, 'cq', [(i, i ^ step) for i in range(HEADS)])  19.8 us
    all_to_all x1, starting transfers between devices, on_device(): owners = lax.all_to_all(owners, Z, 0, 0)  13.2 us
    all_to_all x1, starting transfers between devices, on_device(): pre = lax.all_to_all(pre, ('cb', 'cq'), 0, 0)  11.3 us
    pallas_call x1, Pallas kernels, on_device(): pl.pallas_call(functools.partial(prefix_kernel, chunk), out_shape=(shape(...  7.85 us
    ppermute x1, waiting for transfers between devices, on_device(): oth_hi = lax.ppermute(jnp.stack(pairs[2:4]), Z, ring(-4, early))  7.49 us
    all_to_all x1, starting transfers between devices, on_device(): pref = lax.all_to_all(spread, 'sib', 0, 0)  7.32 us
    all_to_all x1, starting transfers between devices, on_device(): parts = lax.all_to_all(pgrad, 'sib', 0, 0)  7.26 us
  transfers between devices with their start and end apart: 12, of which 7 were waited for; matrix products, arithmetic and copies ran while one was open for 0% of the time, Pallas kernels for 6%

profile of v2, /device:TPU:32, one launch (start us, length us, event | category | flops | bytes accessed | tf_op | source)
XLA Modules:
  0.0 138.0 jit_solution(11520887276913016687)
XLA Ops:
  0.7 2.5 %pack_heads.1.own = bf16[4,784,128]{2,1,0:T(8,128)(2,1)} custom-call(s32[32]{0:T(128)} %lengths.1, bf16[2,128,512]{2,1,0:T(8,128)(2,1)} %bitcast.20, bf16[2,128,512]{2,1,0:T(8,128)(2,1)} %bitcast.21, bf16[2,128,512]{2,1,0:T(8,128)(2,1)} %bitcast.22, bf16[128,512]{1,0:T(8,128)(2,1)} %bitcast.23, bf16[128,512]{1,0:T(8,128)(2,1)} %bitcast.24), custom_call_target="tpu_custom_call" | custom-call | flops 1048576 | bytes 2097152 | tf_op jit(solution)/shard_map/pack_heads/pallas_call | solution.py:291
  3.2 0.0 copy-start
  3.2 1.2 dynamic-slice_bitcast_fusion
  4.4 3.8 %collective-permute-start.2 = (bf16[784,128]{1,0:T(8,128)(2,1)S(1)}, bf16[784,128]{1,0:T(8,128)(2,1)S(1)}, u32[]{:S(2)}, u32[]{:S(2)}) collective-permute-start(bf16[784,128]{1,0:T(8,128)(2,1)S(1)} %get-tuple-element.31), channel_id=1, source_target_pairs={{0,6},{2,4},{4,2},{6,0},{1,7},{3,5},{5,3},{7,1},{8,14},{10,12},{12... | collective-permute-start | bytes 602120 | tf_op jit(solution)/shard_map/ppermute | solution.py:302
  8.3 1.3 pack_prefix.1
  9.6 11.3 %all-to-all-start = ((bf16[8,16,128]{2,1,0:T(8,128)(2,1)}), bf16[8,16,128]{2,1,0:T(8,128)(2,1)S(1)}, u32[]{:S(2)}, u32[]{:S(2)}) async-start(bf16[8,16,128]{2,1,0:T(8,128)(2,1)} %pack_prefix.1), calls=%async_computation | async-start | bytes 65536 | tf_op jit(solution)/shard_map/all_to_all | solution.py:308
  20.9 4.3 %collective-permute-start.1 = (bf16[784,128]{1,0:T(8,128)(2,1)S(1)}, bf16[784,128]{1,0:T(8,128)(2,1)S(1)}, u32[]{:S(2)}, u32[]{:S(2)}) collective-permute-start(bf16[784,128]{1,0:T(8,128)(2,1)S(1)} %get-tuple-element.32), channel_id=1, source_target_pairs={{0,4},{2,6},{4,0},{6,2},{1,5},{3,7},{5,1},{7,3},{8,12},{10,14},{12... | collective-permute-start | bytes 602120 | tf_op jit(solution)/shard_map/ppermute | solution.py:302
  25.1 2.5 %collective-permute-start = (bf16[784,128]{1,0:T(8,128)(2,1)S(1)}, bf16[784,128]{1,0:T(8,128)(2,1)S(1)}, u32[]{:S(2)}, u32[]{:S(2)}) collective-permute-start(bf16[784,128]{1,0:T(8,128)(2,1)S(1)} %get-tuple-element.33), channel_id=1, source_target_pairs={{0,2},{2,0},{4,6},{6,4},{1,3},{3,1},{5,7},{7,5},{8,10},{10,8},{12,... | collective-permute-start | bytes 602120 | tf_op jit(solution)/shard_map/ppermute | solution.py:302
  27.6 0.0 copy-done
  27.6 2.4 %all-to-all-done.pre = bf16[8,16,128]{2,1,0:T(8,128)(2,1)S(1)} async-done(((bf16[8,16,128]{2,1,0:T(8,128)(2,1)}), bf16[8,16,128]{2,1,0:T(8,128)(2,1)S(1)}, u32[]{:S(2)}, u32[]{:S(2)}) %all-to-all-start) | async-done | bytes 32800 | tf_op jit(solution)/shard_map/all_to_all | solution.py:308
  30.1 0.0 copy-start.5
  30.1 0.6 copy-done.5
  30.7 1.6 %spread_prefix.1 = bf16[32,64,128]{2,1,0:T(8,128)(2,1)} custom-call(bf16[8,16,128]{2,1,0:T(8,128)(2,1)} %copy-done.5), custom_call_target="tpu_custom_call" | custom-call | flops 262144 | bytes 524288 | tf_op jit(solution)/shard_map/spread_prefix/pallas_call | solution.py:313
  32.3 7.3 %all-to-all-start.1 = ((bf16[32,64,128]{2,1,0:T(8,128)(2,1)}), bf16[32,64,128]{2,1,0:T(8,128)(2,1)S(1)}, u32[]{:S(2)}, u32[]{:S(2)}) async-start(bf16[32,64,128]{2,1,0:T(8,128)(2,1)} %spread_prefix.1), calls=%async_computation.1 | async-start | bytes 1048576 | tf_op jit(solution)/shard_map/all_to_all | solution.py:321
  39.6 0.0 collective-permute-done.2.far3
  39.7 0.0 collective-permute-done.1.far2
  39.7 7.2 %collective-permute-start.4 = (bf16[2,256,128]{2,1,0:T(8,128)(2,1)S(1)}, bf16[2,256,128]{2,1,0:T(8,128)(2,1)S(1)}, u32[]{:S(2)}, u32[]{:S(2)}) collective-permute-start(bf16[2,256,128]{2,1,0:T(8,128)(2,1)S(1)} %pad_maximum_fusion.1), channel_id=1, source_target_pairs={{0,9},{2,11},{4,13},{6,15},{1,8},{3,10},{5,12},{7,14},{16,25},{18,... | collective-permute-start | bytes 393224 | tf_op jit(solution)/shard_map/ppermute | solution.py:312
  46.9 0.0 collective-permute-done.far1
  46.9 1.3 collective-permute-start.3
  48.2 7.5 %collective-permute-done.4.oth_hi = bf16[2,256,128]{2,1,0:T(8,128)(2,1)S(1)} collective-permute-done((bf16[2,256,128]{2,1,0:T(8,128)(2,1)S(1)}, bf16[2,256,128]{2,1,0:T(8,128)(2,1)S(1)}, u32[]{:S(2)}, u32[]{:S(2)}) %collective-permute-start.4) | collective-permute-done | bytes 131104 | tf_op jit(solution)/shard_map/ppermute | solution.py:312
  55.7 0.0 collective-permute-done.3.oth_lo
  55.7 0.0 all-to-all-done.1.pref
  55.7 7.8 %prefix_grads.1 = (bf16[32,64,128]{2,1,0:T(8,128)(2,1)}, f32[4,8,256]{2,1,0:T(8,128)S(1)}, f32[4,128,256]{2,1,0:T(8,128)S(1)}) custom-call(bf16[4,784,128]{2,1,0:T(8,128)(2,1)S(1)} %copy-done, bf16[784,128]{1,0:T(8,128)(2,1)S(1)} %collective-permute-done.far1, bf16[784,128]{1,0:T(8,128)(2,1)S(1)} %collective-permute-done.1.far2, ...), custom_call_target="tpu_custom_call" | custom-call | flops 1610612736 | bytes 4194304 | tf_op jit(solution)/shard_map/prefix_grads/pallas_call | solution.py:326
  63.6 7.3 %all-to-all-start.2 = ((bf16[32,64,128]{2,1,0:T(8,128)(2,1)}), bf16[32,64,128]{2,1,0:T(8,128)(2,1)S(1)}, u32[]{:S(2)}, u32[]{:S(2)}) async-start(bf16[32,64,128]{2,1,0:T(8,128)(2,1)} %get-tuple-element.24), calls=%async_computation.2 | async-start | bytes 1048576 | tf_op jit(solution)/shard_map/all_to_all | solution.py:368
  70.8 4.9 %sibling_grads.1 = (bf16[256,128]{1,0:T(8,128)(2,1)S(1)}, bf16[256,128]{1,0:T(8,128)(2,1)S(1)}, bf16[256,128]{1,0:T(8,128)(2,1)S(1)}, bf16[256,128]{1,0:T(8,128)(2,1)S(1)}, bf16[16,144,128]{2,1,0:T(8,128)(2,1)S(1)}) custom-call(bf16[4,784,128]{2,1,0:T(8,128)(2,1)S(1)} %copy-done, bf16[784,128]{1,0:T(8,128)(2,1)S(1)} %collective-permute-done.far1, ...), custom_call_target="tpu_custom_call" | custom-call | flops 1342177280 | bytes 4194304 | tf_op jit(solution)/shard_map/sibling_grads/pallas_call | solution.py:348
  75.7 0.0 copy-start.1
  75.7 0.8 copy-done.1
  76.6 0.0 copy-start.2
  76.6 0.6 copy-done.2
  77.2 5.4 %all-to-all-done.2.parts = bf16[32,64,128]{2,1,0:T(8,128)(2,1)S(1)} async-done(((bf16[32,64,128]{2,1,0:T(8,128)(2,1)}), bf16[32,64,128]{2,1,0:T(8,128)(2,1)S(1)}, u32[]{:S(2)}, u32[]{:S(2)}) %all-to-all-start.2) | async-done | bytes 524320 | tf_op jit(solution)/shard_map/all_to_all | solution.py:368
  82.6 0.0 copy-start.4
  82.6 0.8 copy-done.4
  83.4 1.8 %prefix_sums.1 = bf16[16,144,128]{2,1,0:T(8,128)(2,1)} custom-call(bf16[32,64,128]{2,1,0:T(8,128)(2,1)} %copy-done.4, bf16[16,144,128]{2,1,0:T(8,128)(2,1)} %copy-done.1), custom_call_target="tpu_custom_call", output_to_operand_aliasing={{}: (1, {})} | custom-call | flops 262144 | bytes 524288 | tf_op jit(solution)/shard_map/prefix_sums/pallas_call | solution.py:369
  85.2 13.2 %all-to-all-start.3 = ((bf16[16,144,128]{2,1,0:T(8,128)(2,1)}), bf16[16,144,128]{2,1,0:T(8,128)(2,1)S(1)}, u32[]{:S(2)}, u32[]{:S(2)}) async-start(bf16[16,144,128]{2,1,0:T(8,128)(2,1)} %prefix_sums.1), calls=%async_computation.3 | async-start | bytes 1179648 | tf_op jit(solution)/shard_map/all_to_all | solution.py:382
  98.4 2.0 %collective-permute-start.5 = (bf16[256,128]{1,0:T(8,128)(2,1)S(1)}, bf16[256,128]{1,0:T(8,128)(2,1)S(1)}, u32[]{:S(2)}, u32[]{:S(2)}) collective-permute-start(bf16[256,128]{1,0:T(8,128)(2,1)S(1)} %get-tuple-element.21), channel_id=1, source_target_pairs={{0,2},{2,0},{4,6},{6,4},{1,3},{3,1},{5,7},{7,5},{8,10},{10,8},{12,... | collective-permute-start | bytes 196616 | tf_op jit(solution)/shard_map/ppermute | solution.py:302
  100.4 4.7 %collective-permute-start.6 = (bf16[256,128]{1,0:T(8,128)(2,1)S(1)}, bf16[256,128]{1,0:T(8,128)(2,1)S(1)}, u32[]{:S(2)}, u32[]{:S(2)}) collective-permute-start(bf16[256,128]{1,0:T(8,128)(2,1)S(1)} %get-tuple-element.22), channel_id=1, source_target_pairs={{0,4},{2,6},{4,0},{6,2},{1,5},{3,7},{5,1},{7,3},{8,12},{10,14},{12... | collective-permute-start | bytes 196616 | tf_op jit(solution)/shard_map/ppermute | solution.py:302
  105.2 2.5 %collective-permute-start.7 = (bf16[256,128]{1,0:T(8,128)(2,1)S(1)}, bf16[256,128]{1,0:T(8,128)(2,1)S(1)}, u32[]{:S(2)}, u32[]{:S(2)}) collective-permute-start(bf16[256,128]{1,0:T(8,128)(2,1)S(1)} %get-tuple-element.23), channel_id=1, source_target_pairs={{0,6},{2,4},{4,2},{6,0},{1,7},{3,5},{5,3},{7,1},{8,14},{10,12},{12... | collective-permute-start | bytes 196616 | tf_op jit(solution)/shard_map/ppermute | solution.py:302
  107.6 17.8 %collective-permute-done.5.dq1 = bf16[256,128]{1,0:T(8,128)(2,1)S(1)} collective-permute-done((bf16[256,128]{1,0:T(8,128)(2,1)S(1)}, bf16[256,128]{1,0:T(8,128)(2,1)S(1)}, u32[]{:S(2)}, u32[]{:S(2)}) %collective-permute-start.5) | collective-permute-done | bytes 65568 | tf_op jit(solution)/shard_map/ppermute | solution.py:302
  125.4 0.0 copy-start.6
  125.4 2.2 %collective-permute-done.6.dq2 = bf16[256,128]{1,0:T(8,128)(2,1)S(1)} collective-permute-done((bf16[256,128]{1,0:T(8,128)(2,1)S(1)}, bf16[256,128]{1,0:T(8,128)(2,1)S(1)}, u32[]{:S(2)}, u32[]{:S(2)}) %collective-permute-start.6) | collective-permute-done | bytes 65568 | tf_op jit(solution)/shard_map/ppermute | solution.py:302
  127.6 0.0 copy-start.7
  127.6 3.0 %collective-permute-done.7.dq3 = bf16[256,128]{1,0:T(8,128)(2,1)S(1)} collective-permute-done((bf16[256,128]{1,0:T(8,128)(2,1)S(1)}, bf16[256,128]{1,0:T(8,128)(2,1)S(1)}, u32[]{:S(2)}, u32[]{:S(2)}) %collective-permute-start.7) | collective-permute-done | bytes 65568 | tf_op jit(solution)/shard_map/ppermute | solution.py:302
  130.6 4.5 %all-to-all-done.3.parts = bf16[16,144,128]{2,1,0:T(8,128)(2,1)S(1)} async-done(((bf16[16,144,128]{2,1,0:T(8,128)(2,1)}), bf16[16,144,128]{2,1,0:T(8,128)(2,1)S(1)}, u32[]{:S(2)}, u32[]{:S(2)}) %all-to-all-start.3) | async-done | bytes 589856 | tf_op jit(solution)/shard_map/all_to_all | solution.py:382
  135.1 0.0 copy-done.6
  135.1 0.0 copy-done.7
  135.1 0.0 copy-done.8
  135.1 0.8 copy-done.3
  135.9 2.0 %unpack_heads.1 = (bf16[2,128,512]{2,1,0:T(8,128)(2,1)}, bf16[64,512]{1,0:T(8,128)(2,1)}, bf16[64,512]{1,0:T(8,128)(2,1)}, bf16[2,512]{1,0:T(2,128)(2,1)}, bf16[2,512]{1,0:T(2,128)(2,1)}) custom-call(bf16[256,128]{1,0:T(8,128)(2,1)} %copy-done.2, bf16[256,128]{1,0:T(8,128)(2,1)} %copy-done.6, bf16[256,128]{1,0:T(8,128)(2,1)} %copy-done.7, ...), custom_call_target="tpu_custom_call" | custom-call | flops 262144 | bytes 1048576 | tf_op jit(solution)/shard_map/unpack_heads/pallas_call | solution.py:384
  (8 shorter events, 0.1 us)
Async XLA Ops:
  3.2 24.4 %copy-start = (bf16[4,784,128]{2,1,0:T(8,128)(2,1)S(1)}, bf16[4,784,128]{2,1,0:T(8,128)(2,1)}, u32[]{:S(2)}) copy-start(bf16[4,784,128]{2,1,0:T(8,128)(2,1)} %pack_heads.1.own) | copy-start | bytes 2408452
  4.4 35.2 %collective-permute-start.2 = (bf16[784,128]{1,0:T(8,128)(2,1)S(1)}, bf16[784,128]{1,0:T(8,128)(2,1)S(1)}, u32[]{:S(2)}, u32[]{:S(2)}) collective-permute-start(bf16[784,128]{1,0:T(8,128)(2,1)S(1)} %get-tuple-element.31), channel_id=1, source_target_pairs={{0,6},{2,4},{4,2},{6,0},{1,7},{3,5},{5,3},{7,1},{8,14},{10,12},{12... | collective-permute-start | bytes 602120 | tf_op jit(solution)/shard_map/ppermute | solution.py:302
  9.6 20.5 %all-to-all-start = ((bf16[8,16,128]{2,1,0:T(8,128)(2,1)}), bf16[8,16,128]{2,1,0:T(8,128)(2,1)S(1)}, u32[]{:S(2)}, u32[]{:S(2)}) async-start(bf16[8,16,128]{2,1,0:T(8,128)(2,1)} %pack_prefix.1), calls=%async_computation | async-start | bytes 65536 | tf_op jit(solution)/shard_map/all_to_all | solution.py:308
  20.9 18.8 %collective-permute-start.1 = (bf16[784,128]{1,0:T(8,128)(2,1)S(1)}, bf16[784,128]{1,0:T(8,128)(2,1)S(1)}, u32[]{:S(2)}, u32[]{:S(2)}) collective-permute-start(bf16[784,128]{1,0:T(8,128)(2,1)S(1)} %get-tuple-element.32), channel_id=1, source_target_pairs={{0,4},{2,6},{4,0},{6,2},{1,5},{3,7},{5,1},{7,3},{8,12},{10,14},{12... | collective-permute-start | bytes 602120 | tf_op jit(solution)/shard_map/ppermute | solution.py:302
  25.1 21.7 %collective-permute-start = (bf16[784,128]{1,0:T(8,128)(2,1)S(1)}, bf16[784,128]{1,0:T(8,128)(2,1)S(1)}, u32[]{:S(2)}, u32[]{:S(2)}) collective-permute-start(bf16[784,128]{1,0:T(8,128)(2,1)S(1)} %get-tuple-element.33), channel_id=1, source_target_pairs={{0,2},{2,0},{4,6},{6,4},{1,3},{3,1},{5,7},{7,5},{8,10},{10,8},{12,... | collective-permute-start | bytes 602120 | tf_op jit(solution)/shard_map/ppermute | solution.py:302
  30.1 0.6 copy-start.5
  32.3 23.4 %all-to-all-start.1 = ((bf16[32,64,128]{2,1,0:T(8,128)(2,1)}), bf16[32,64,128]{2,1,0:T(8,128)(2,1)S(1)}, u32[]{:S(2)}, u32[]{:S(2)}) async-start(bf16[32,64,128]{2,1,0:T(8,128)(2,1)} %spread_prefix.1), calls=%async_computation.1 | async-start | bytes 1048576 | tf_op jit(solution)/shard_map/all_to_all | solution.py:321
  39.7 16.0 %collective-permute-start.4 = (bf16[2,256,128]{2,1,0:T(8,128)(2,1)S(1)}, bf16[2,256,128]{2,1,0:T(8,128)(2,1)S(1)}, u32[]{:S(2)}, u32[]{:S(2)}) collective-permute-start(bf16[2,256,128]{2,1,0:T(8,128)(2,1)S(1)} %pad_maximum_fusion.1), channel_id=1, source_target_pairs={{0,9},{2,11},{4,13},{6,15},{1,8},{3,10},{5,12},{7,14},{16,25},{18,... | collective-permute-start | bytes 393224 | tf_op jit(solution)/shard_map/ppermute | solution.py:312
  46.9 8.8 %collective-permute-start.3 = (bf16[2,256,128]{2,1,0:T(8,128)(2,1)S(1)}, bf16[2,256,128]{2,1,0:T(8,128)(2,1)S(1)}, u32[]{:S(2)}, u32[]{:S(2)}) collective-permute-start(bf16[2,256,128]{2,1,0:T(8,128)(2,1)S(1)} %pad_maximum_fusion), channel_id=1, source_target_pairs={{0,8},{2,10},{4,12},{6,14},{1,9},{3,11},{5,13},{7,15},{16,24},{18,... | collective-permute-start | bytes 393224 | tf_op jit(solution)/shard_map/ppermute | solution.py:311
  63.6 19.0 %all-to-all-start.2 = ((bf16[32,64,128]{2,1,0:T(8,128)(2,1)}), bf16[32,64,128]{2,1,0:T(8,128)(2,1)S(1)}, u32[]{:S(2)}, u32[]{:S(2)}) async-start(bf16[32,64,128]{2,1,0:T(8,128)(2,1)} %get-tuple-element.24), calls=%async_computation.2 | async-start | bytes 1048576 | tf_op jit(solution)/shard_map/all_to_all | solution.py:368
  75.7 0.8 copy-start.1
  76.6 0.6 copy-start.2
  82.6 0.8 copy-start.4
  85.2 49.9 %all-to-all-start.3 = ((bf16[16,144,128]{2,1,0:T(8,128)(2,1)}), bf16[16,144,128]{2,1,0:T(8,128)(2,1)S(1)}, u32[]{:S(2)}, u32[]{:S(2)}) async-start(bf16[16,144,128]{2,1,0:T(8,128)(2,1)} %prefix_sums.1), calls=%async_computation.3 | async-start | bytes 1179648 | tf_op jit(solution)/shard_map/all_to_all | solution.py:382
  98.4 27.0 %collective-permute-start.5 = (bf16[256,128]{1,0:T(8,128)(2,1)S(1)}, bf16[256,128]{1,0:T(8,128)(2,1)S(1)}, u32[]{:S(2)}, u32[]{:S(2)}) collective-permute-start(bf16[256,128]{1,0:T(8,128)(2,1)S(1)} %get-tuple-element.21), channel_id=1, source_target_pairs={{0,2},{2,0},{4,6},{6,4},{1,3},{3,1},{5,7},{7,5},{8,10},{10,8},{12,... | collective-permute-start | bytes 196616 | tf_op jit(solution)/shard_map/ppermute | solution.py:302
  100.4 27.2 %collective-permute-start.6 = (bf16[256,128]{1,0:T(8,128)(2,1)S(1)}, bf16[256,128]{1,0:T(8,128)(2,1)S(1)}, u32[]{:S(2)}, u32[]{:S(2)}) collective-permute-start(bf16[256,128]{1,0:T(8,128)(2,1)S(1)} %get-tuple-element.22), channel_id=1, source_target_pairs={{0,4},{2,6},{4,0},{6,2},{1,5},{3,7},{5,1},{7,3},{8,12},{10,14},{12... | collective-permute-start | bytes 196616 | tf_op jit(solution)/shard_map/ppermute | solution.py:302
  105.2 25.4 %collective-permute-start.7 = (bf16[256,128]{1,0:T(8,128)(2,1)S(1)}, bf16[256,128]{1,0:T(8,128)(2,1)S(1)}, u32[]{:S(2)}, u32[]{:S(2)}) collective-permute-start(bf16[256,128]{1,0:T(8,128)(2,1)S(1)} %get-tuple-element.23), channel_id=1, source_target_pairs={{0,6},{2,4},{4,2},{6,0},{1,7},{3,5},{5,3},{7,1},{8,14},{10,12},{12... | collective-permute-start | bytes 196616 | tf_op jit(solution)/shard_map/ppermute | solution.py:302
  125.4 9.7 %copy-start.6 = (bf16[256,128]{1,0:T(8,128)(2,1)}, bf16[256,128]{1,0:T(8,128)(2,1)S(1)}, u32[]{:S(2)}) copy-start(bf16[256,128]{1,0:T(8,128)(2,1)S(1)} %collective-permute-done.5.dq1) | copy-start | bytes 196612
  127.6 7.5 %copy-start.7 = (bf16[256,128]{1,0:T(8,128)(2,1)}, bf16[256,128]{1,0:T(8,128)(2,1)S(1)}, u32[]{:S(2)}) copy-start(bf16[256,128]{1,0:T(8,128)(2,1)S(1)} %collective-permute-done.6.dq2) | copy-start | bytes 196612
  130.6 4.5 %copy-start.8 = (bf16[256,128]{1,0:T(8,128)(2,1)}, bf16[256,128]{1,0:T(8,128)(2,1)S(1)}, u32[]{:S(2)}) copy-start(bf16[256,128]{1,0:T(8,128)(2,1)S(1)} %collective-permute-done.7.dq3) | copy-start | bytes 196612
  135.1 0.8 copy-start.3

commit v3 on v2

v3 whole, which is shorter than its diff:
```python
import functools
import math

import jax
import jax.numpy as jnp
from jax import lax
from jax.experimental import pallas as pl
from jax.experimental.pallas import tpu as pltpu
from jax.sharding import Mesh, PartitionSpec as P

HEADS = 4
LANES = 128
ROWS = 128
GROUPS = 2
LOG2E = math.log2(math.e)
NEG = -1e30
Z = ("cb", "cq", "tp")
NORMS_COST = 1 << 33
PACK_COST = 1 << 33
GRADS_COST = 1 << 36
MERGE_COST = 1 << 36
SPREAD_COST = 1 << 18


def dot_nt(a, b):
    return lax.dot_general(a, b, (((1,), (1,)), ((), ())), preferred_element_type=jnp.float32)


def dot_nn(a, b):
    return lax.dot_general(a, b, (((1,), (0,)), ((), ())), preferred_element_type=jnp.float32)


def vmem(n):
    return [pl.BlockSpec(memory_space=pltpu.VMEM)] * n


def cost(flops, moved, exps=0):
    return pl.CostEstimate(flops=flops, bytes_accessed=moved, transcendentals=exps)


def pack_kernel(lengths, q, g, o, k, v, pre, own, far1, far2, far3):
    cq = lax.axis_index("cq")
    ctx = lax.axis_index("cb") * HEADS + cq
    length = lengths[lax.axis_index("sib")]
    row = lax.broadcasted_iota(jnp.int32, (ROWS, LANES), 0) + ctx * ROWS
    live = row < length
    ones = jnp.ones((8, LANES), jnp.bfloat16)
    for step, out in enumerate((own, far1, far2, far3)):
        head = jnp.bitwise_xor(cq, step)
        cols = pl.ds(pl.multiple_of(head * LANES, LANES), LANES)
        out[4 * ROWS : 5 * ROWS, :] = k[:, cols]
        out[5 * ROWS : 6 * ROWS, :] = v[:, cols]
        deltas = []
        for slot in range(GROUPS):
            rows = slice(slot * ROWS, (slot + 1) * ROWS)
            out[rows, :] = q[slot, :, cols]
            grad = jnp.where(live, g[slot, :, cols].astype(jnp.float32), 0.0)
            rows = slice((GROUPS + slot) * ROWS, (GROUPS + slot + 1) * ROWS)
            out[rows, :] = grad.astype(jnp.bfloat16)
            prod = grad * o[slot, :, cols].astype(jnp.float32)
            high = prod.astype(jnp.bfloat16)
            low = (prod - high.astype(jnp.float32)).astype(jnp.bfloat16)
            deltas.append((dot_nt(ones, high) + dot_nt(ones, low))[0:1])
        rest = jnp.concatenate(deltas + [jnp.zeros((14, LANES), jnp.float32)], axis=0)
        out[6 * ROWS : 6 * ROWS + 16, :] = rest.astype(jnp.bfloat16)


def pack_prefix_kernel(pk, pv, pre):
    for head in range(HEADS):
        cols = slice(head * LANES, (head + 1) * LANES)
        rows = jnp.concatenate(
            [
                pk[:, cols].astype(jnp.float32),
                pv[:, cols].astype(jnp.float32),
                jnp.zeros((8, LANES), jnp.float32),
            ],
            axis=0,
        ).astype(jnp.bfloat16)
        for half in range(2):
            pre[half * HEADS + head] = rows


def spread_kernel(pre, out):
    rows = [pre[at].astype(jnp.float32) for at in range(2 * HEADS)]
    block = []
    for half in range(2):
        mine = rows[half * HEADS : (half + 1) * HEADS]
        block += [r[0:4] for r in mine] + [r[4:8] for r in mine]
    block = jnp.concatenate(block, axis=0).astype(jnp.bfloat16)
    for at in range(out.shape[0]):
        out[at] = block


def load_keys(pref, keys, values):
    pre = pref.shape[0] * 16
    for part in range(2):
        rows = slice(part * pre, (part + 1) * pre)
        keys[rows, :] = pref[:, part * 32 : part * 32 + 16, :].reshape(pre, LANES)
        values[rows, :] = pref[:, part * 32 + 16 : part * 32 + 32, :].reshape(pre, LANES)


def tile_data(bulk, step):
    wide = GROUPS * ROWS
    rest = bulk[step, 6 * ROWS : 6 * ROWS + 16, :].astype(jnp.float32)
    delta = jnp.concatenate([rest[s : s + 1] for s in range(GROUPS)], axis=1)
    return bulk[step, 0:wide, :], bulk[step, wide : 2 * wide, :], delta


def gather_bulk(bulk, own, far1, far2, far3):
    for step, received in enumerate((own, far1, far2, far3)):
        bulk[step] = received[...]


def transpose_keys(keys, keys_t, start, stop, chunk):
    for at in range(start, stop, chunk):
        keys_t[:, at - start : at - start + chunk] = (
            keys[at : at + chunk, :].astype(jnp.float32).T.astype(jnp.bfloat16)
        )


def load_sibling(bulk, oth_lo, oth_hi, keys, values, base):
    cq = lax.axis_index("cq")
    half = HEADS * ROWS
    for step in range(HEADS):
        at = jnp.bitwise_xor(cq, step) * ROWS
        src = (oth_lo if step < 2 else oth_hi).at[step % 2]
        rows = pl.ds(pl.multiple_of(base + at, ROWS), ROWS)
        keys[rows, :] = src[0:ROWS, :]
        if values is not None:
            values[rows, :] = src[ROWS : 2 * ROWS, :]
        rows = pl.ds(pl.multiple_of(base + half + at, ROWS), ROWS)
        keys[rows, :] = bulk[step, 4 * ROWS : 5 * ROWS, :]
        if values is not None:
            values[rows, :] = bulk[step, 5 * ROWS : 6 * ROWS, :]


def sibling_scores(keys, queries, at, tile):
    half = HEADS * ROWS
    s = dot_nt(keys, queries) * (LOG2E / math.sqrt(LANES))
    if at >= half:
        position = tile * ROWS + lax.rem(lax.broadcasted_iota(jnp.int32, s.shape, 1), ROWS)
        key_at = lax.broadcasted_iota(jnp.int32, s.shape, 0) + (at - half)
        return jnp.where(key_at <= position, s, NEG)
    return jnp.where(lax.axis_index("cb") == 1, s, NEG)


def norms_kernel(chunk, own, far1, far2, far3, pref, norms, keys, bulk):
    n_sib = pref.shape[0]
    pre = n_sib * 32
    wide = GROUPS * ROWS
    gather_bulk(bulk, own, far1, far2, far3)
    for part in range(2):
        rows = slice(part * pre // 2, (part + 1) * pre // 2)
        keys[rows, :] = pref[:, part * 32 : part * 32 + 16, :].reshape(pre // 2, LANES)

    @pl.loop(0, HEADS)
    def _(step):
        queries, grads, delta = tile_data(bulk, step)
        top = jnp.full((1, wide), NEG, jnp.float32)
        norm = jnp.zeros((1, wide), jnp.float32)
        for at in range(0, pre, chunk):
            s = dot_nt(keys[at : at + chunk, :], queries) * (LOG2E / math.sqrt(LANES))
            top, norm = online(s, top, norm)
        norms[step] = jnp.broadcast_to(top + jnp.log2(norm), (8, wide))


def online(s, top, norm):
    higher = jnp.maximum(top, jnp.max(s, axis=0, keepdims=True))
    added = jnp.sum(jnp.exp2(s - higher), axis=0, keepdims=True)
    return higher, norm * jnp.exp2(top - higher) + added


def sibling_kernel(
    chunk, own, far1, far2, far3, oth_lo, oth_hi, pre_norms,
    keep, send8, plus, minus, norms, dq_part,
    keys, values, keys_t, scores, dk_acc, dv_acc, bulk,
):
    scale = 1.0 / math.sqrt(LANES)
    total = keys.shape[0]
    half = HEADS * ROWS
    wide = GROUPS * ROWS
    gather_bulk(bulk, own, far1, far2, far3)
    load_sibling(bulk, oth_lo, oth_hi, keys, values, 0)
    transpose_keys(keys, keys_t, 0, total, chunk)
    dk_acc[...] = jnp.zeros_like(dk_acc)
    dv_acc[...] = jnp.zeros_like(dv_acc)

    @pl.loop(0, HEADS)
    def _(step):
        tile = jnp.bitwise_xor(lax.axis_index("cq"), step)
        queries, grads, delta = tile_data(bulk, step)
        top = pre_norms[step][0:1]
        norm = jnp.ones((1, wide), jnp.float32)
        tops = []
        for at in range(0, total, chunk):
            s = sibling_scores(keys[at : at + chunk, :], queries, at, tile)
            higher = jnp.maximum(top, jnp.max(s, axis=0, keepdims=True))
            e = jnp.exp2(s - higher)
            scores[at : at + chunk, :] = e
            norm = norm * jnp.exp2(top - higher) + jnp.sum(e, axis=0, keepdims=True)
            top = higher
            tops.append(top)
        log_norm = top + jnp.log2(norm)
        norms[step] = jnp.broadcast_to(log_norm, (8, wide))
        dq_t = jnp.zeros((LANES, wide), jnp.float32)
        for at in range(0, total, chunk):
            rows = slice(at, at + chunk)
            p = scores[rows, :] * jnp.exp2(tops[at // chunk] - log_norm)
            dp = dot_nt(values[rows, :], grads)
            ds = (p * (dp - delta)).astype(jnp.bfloat16)
            dv_acc[rows, :] += dot_nn(p.astype(jnp.bfloat16), grads)
            dk_acc[rows, :] += dot_nn(ds, queries)
            dq_t = dq_t + dot_nn(keys_t[:, rows], ds)
        dq_part[step, :, :] = dq_t

    tp = lax.axis_index("tp")
    for out, base, which in (
        (minus, 0, tp),
        (plus, 0, 1 - tp),
        (keep, half, tp),
        (send8, half, 1 - tp),
    ):
        for slot in range(HEADS):
            rows = pl.ds(pl.multiple_of(base + slot * ROWS + which * (ROWS // 2), ROWS // 2), ROWS // 2)
            out[slot, 0 : ROWS // 2, :] = (dk_acc[rows, :] * scale).astype(jnp.bfloat16)
            out[slot, ROWS // 2 : ROWS, :] = dv_acc[rows, :].astype(jnp.bfloat16)


def prefix_kernel(
    chunk, own, far1, far2, far3, pref, norms, dq_part,
    pgrad, dq,
    keys, values, keys_t, dk_acc, dv_acc, bulk,
):
    scale = 1.0 / math.sqrt(LANES)
    n_sib = pref.shape[0]
    pre = n_sib * 32
    gather_bulk(bulk, own, far1, far2, far3)
    load_keys(pref, keys, values)
    transpose_keys(keys, keys_t, 0, pre, chunk)
    dk_acc[...] = jnp.zeros_like(dk_acc)
    dv_acc[...] = jnp.zeros_like(dv_acc)

    @pl.loop(0, HEADS)
    def _(step):
        queries, grads, delta = tile_data(bulk, step)
        norm = norms[step][0:1]
        dq_t = dq_part[step]
        for at in range(0, pre, chunk):
            rows = slice(at, at + chunk)
            p = jnp.exp2(dot_nt(keys[rows, :], queries) * (scale * LOG2E) - norm)
            dp = dot_nt(values[rows, :], grads)
            ds = (p * (dp - delta)).astype(jnp.bfloat16)
            dv_acc[rows, :] += dot_nn(p.astype(jnp.bfloat16), grads)
            dk_acc[rows, :] += dot_nn(ds, queries)
            dq_t = dq_t + dot_nn(keys_t[:, rows], ds)
        dq[step, :, :] = (dq_t.T * scale).astype(jnp.bfloat16)

    for part in range(2):
        rows = slice(part * pre // 2, (part + 1) * pre // 2)
        pgrad[:, part * 32 : part * 32 + 16, :] = (
            (dk_acc[rows, :] * scale).astype(jnp.bfloat16).reshape(n_sib, 16, LANES)
        )
        pgrad[:, part * 32 + 16 : part * 32 + 32, :] = (
            dv_acc[rows, :].astype(jnp.bfloat16).reshape(n_sib, 16, LANES)
        )


def near_kernel(keep, got_plus, got_minus, out):
    for slot in range(HEADS):
        out[slot] = sum(a[slot].astype(jnp.float32) for a in (keep, got_plus, got_minus))


def merge_kernel(near, got8, dq, out0, out1, out2, out3):
    cq = lax.axis_index("cq")
    wide = GROUPS * ROWS
    for step, out in enumerate((out0, out1, out2, out3)):
        slot = jnp.bitwise_xor(cq, step)
        out[0:wide, :] = dq[step]
        total = near[slot] + got8[slot].astype(jnp.float32)
        out[wide : wide + ROWS, :] = total.astype(jnp.bfloat16)


def prefix_sum_kernel(parts, out):
    total = jnp.sum(parts[...].astype(jnp.float32), axis=0)
    for part in range(2):
        for piece in range(2 * HEADS):
            at = part * 32 + piece * 2
            rows = jnp.concatenate(
                [total[at : at + 2], total[at + 16 : at + 18], jnp.zeros((4, LANES), jnp.float32)],
                axis=0,
            )
            out[part * 2 * HEADS + piece, :, :] = rows


def unpack_kernel(back0, back1, back2, back3, small, dq_out, sk_out, sv_out, pk_out, pv_out):
    cq = lax.axis_index("cq")
    half = ROWS // 2
    wide = GROUPS * ROWS
    for step, back in enumerate((back0, back1, back2, back3)):
        head = jnp.bitwise_xor(cq, step)
        cols = pl.ds(pl.multiple_of(head * LANES, LANES), LANES)
        for slot in range(GROUPS):
            dq_out[slot, :, cols] = back[slot * ROWS : (slot + 1) * ROWS, :]
        sk_out[:, cols] = back[wide : wide + half, :]
        sv_out[:, cols] = back[wide + half : wide + ROWS, :]
    for head in range(HEADS):
        cols = slice(head * LANES, (head + 1) * LANES)
        total = sum(small[(b * HEADS + head) * 2 + t] for b in range(2) for t in range(2))
        pk_out[:, cols] = total[0:2].astype(jnp.bfloat16)
        pv_out[:, cols] = total[2:4].astype(jnp.bfloat16)


def ring_index(position):
    return (position % 8) * 2 + position // 8


def ring(shift, sources=range(16)):
    return [(ring_index(p), ring_index((p + shift) % 16)) for p in sources]


def on_device(n_sib, queries, gradient, forward, sib_k, sib_v, pre_k, pre_v, lengths):
    bf16 = jnp.bfloat16
    shape = jax.ShapeDtypeStruct

    pre = pl.pallas_call(
        pack_prefix_kernel,
        out_shape=shape((2 * HEADS, 16, LANES), bf16),
        in_specs=vmem(2),
        out_specs=vmem(1)[0],
        cost_estimate=cost(1 << 10, 1 << 16),
        name="pack_prefix",
    )(pre_k, pre_v)
    bulk = pl.pallas_call(
        pack_kernel,
        out_shape=(shape((784, LANES), bf16),) * 4,
        in_specs=[pl.BlockSpec(memory_space=pltpu.SMEM)]
        + vmem(5)
        + [pl.BlockSpec(memory_space=pl.ANY)],
        out_specs=tuple(vmem(4)),
        cost_estimate=cost(PACK_COST, 2 << 20),
        name="pack_heads",
    )(lengths, queries[0], gradient[0], forward[0], sib_k[0], sib_v[0], pre)

    def swap(array, step):
        return lax.ppermute(array, "cq", [(i, i ^ step) for i in range(HEADS)])

    bulk = [bulk[0]] + [swap(bulk[d], d) for d in (1, 2, 3)]
    pre = lax.all_to_all(pre, ("cb", "cq"), 0, 0)
    early = [p for p in range(16) if p % 8 < 4]
    pairs = [a[4 * ROWS : 6 * ROWS] for a in bulk]
    oth_lo = lax.ppermute(jnp.stack(pairs[0:2]), Z, ring(4, early))
    oth_hi = lax.ppermute(jnp.stack(pairs[2:4]), Z, ring(-4, early))
    spread = pl.pallas_call(
        spread_kernel,
        out_shape=shape((n_sib, 64, LANES), bf16),
        in_specs=vmem(1),
        out_specs=vmem(1)[0],
        cost_estimate=cost(SPREAD_COST, 1 << 19),
        name="spread_prefix",
    )(pre)
    pref = lax.all_to_all(spread, "sib", 0, 0)

    chunk = min(512, n_sib * 16)
    pre_rows, sib_rows = 32 * n_sib, 2 * HEADS * ROWS
    wide = GROUPS * ROWS
    norm_rows = shape((HEADS, 8, wide), jnp.float32)
    pre_norms = pl.pallas_call(
        functools.partial(norms_kernel, chunk),
        out_shape=norm_rows,
        in_specs=vmem(5),
        out_specs=vmem(1)[0],
        scratch_shapes=[
            pltpu.VMEM((pre_rows, LANES), bf16),
            pltpu.VMEM((HEADS, 784, LANES), bf16),
        ],
        compiler_params=pltpu.CompilerParams(vmem_limit_bytes=32 << 20),
        cost_estimate=cost(NORMS_COST, 1 << 20, HEADS * wide * 1024),
        name="prefix_norms",
    )(*bulk, pref)
    piece = shape((HEADS, ROWS, LANES), bf16)
    keep, send8, plus, minus, norms, dq_part = pl.pallas_call(
        functools.partial(sibling_kernel, chunk),
        out_shape=(piece,) * 4 + (norm_rows, shape((HEADS, LANES, wide), jnp.float32)),
        in_specs=vmem(7),
        out_specs=tuple(vmem(6)),
        scratch_shapes=[
            pltpu.VMEM((sib_rows, LANES), bf16),
            pltpu.VMEM((sib_rows, LANES), bf16),
            pltpu.VMEM((LANES, sib_rows), bf16),
            pltpu.VMEM((sib_rows, wide), jnp.float32),
            pltpu.VMEM((sib_rows, LANES), jnp.float32),
            pltpu.VMEM((sib_rows, LANES), jnp.float32),
            pltpu.VMEM((HEADS, 784, LANES), bf16),
        ],
        compiler_params=pltpu.CompilerParams(vmem_limit_bytes=32 << 20),
        cost_estimate=cost(10 * HEADS * wide * 1024 * LANES, 4 << 20, HEADS * wide * 1024),
        name="sibling_grads",
    )(*bulk, oth_lo, oth_hi, pre_norms)
    late = [p for p in range(16) if p % 8 >= 4]
    got8 = lax.ppermute(send8, Z, ring(8))
    got_plus = lax.ppermute(plus, Z, ring(4, late))
    got_minus = lax.ppermute(minus, Z, ring(-4, late))

    pgrad, dq = pl.pallas_call(
        functools.partial(prefix_kernel, chunk),
        out_shape=(shape((n_sib, 64, LANES), bf16), shape((HEADS, wide, LANES), bf16)),
        in_specs=vmem(7),
        out_specs=tuple(vmem(2)),
        scratch_shapes=[
            pltpu.VMEM((pre_rows, LANES), bf16),
            pltpu.VMEM((pre_rows, LANES), bf16),
            pltpu.VMEM((LANES, pre_rows), bf16),
            pltpu.VMEM((pre_rows, LANES), jnp.float32),
            pltpu.VMEM((pre_rows, LANES), jnp.float32),
            pltpu.VMEM((HEADS, 784, LANES), bf16),
        ],
        compiler_params=pltpu.CompilerParams(vmem_limit_bytes=32 << 20),
        cost_estimate=cost(GRADS_COST, 4 << 20, HEADS * wide * 1024),
        name="prefix_grads",
    )(*bulk, pref, norms, dq_part)

    parts = lax.all_to_all(pgrad, "sib", 0, 0)
    near = pl.pallas_call(
        near_kernel,
        out_shape=shape((HEADS, ROWS, LANES), jnp.float32),
        in_specs=vmem(3),
        out_specs=vmem(1)[0],
        cost_estimate=cost(MERGE_COST, 1 << 20),
        name="near_sums",
    )(keep, got_plus, got_minus)
    parts, near = lax.optimization_barrier((parts, near))
    back = pl.pallas_call(
        merge_kernel,
        out_shape=(shape((wide + ROWS, LANES), bf16),) * 4,
        in_specs=vmem(3),
        out_specs=tuple(vmem(4)),
        cost_estimate=cost(MERGE_COST, 1 << 20),
        name="merge_grads",
    )(near, got8, dq)
    small = pl.pallas_call(
        prefix_sum_kernel,
        out_shape=shape((16, 8, LANES), jnp.float32),
        in_specs=vmem(1),
        out_specs=vmem(1)[0],
        cost_estimate=cost(1 << 18, 1 << 19),
        name="prefix_sums",
    )(parts)
    small = lax.all_to_all(small, Z, 0, 0)
    back = [back[0]] + [swap(back[d], d) for d in (1, 2, 3)]

    dq_out, sk_out, sv_out, pk_out, pv_out = pl.pallas_call(
        unpack_kernel,
        out_shape=(
            shape((GROUPS, ROWS, HEADS * LANES), bf16),
            shape((ROWS // 2, HEADS * LANES), bf16),
            shape((ROWS // 2, HEADS * LANES), bf16),
            shape((2, HEADS * LANES), bf16),
            shape((2, HEADS * LANES), bf16),
        ),
        in_specs=vmem(5),
        out_specs=tuple(vmem(5)),
        cost_estimate=cost(1 << 18, 1 << 20),
        name="unpack_heads",
    )(*back, small)
    return dq_out[None], sk_out[None], sv_out[None], pk_out, pv_out


def solution(mesh):
    n_sib, n_ctx, n_tp = mesh.shape["sib"], mesh.shape["ctx"], mesh.shape["tp"]
    fine = Mesh(
        mesh.devices.reshape(n_sib, n_ctx // HEADS, HEADS, n_tp), ("sib", "cb", "cq", "tp")
    )
    ctx = ("cb", "cq")
    heads = P("sib", "tp", ctx, None)
    return jax.shard_map(
        functools.partial(on_device, n_sib),
        mesh=fine,
        in_specs=(
            heads,
            heads,
            heads,
            P("sib", ctx, None),
            P("sib", ctx, None),
            P(("sib",) + ctx, None),
            P(("sib",) + ctx, None),
            P(),
        ),
        out_specs=(
            heads,
            P("sib", ctx + ("tp",), None),
            P("sib", ctx + ("tp",), None),
            P(("sib",) + ctx + ("tp",), None),
            P(("sib",) + ctx + ("tp",), None),
        ),
        check_vma=False,
    )
```

time: 139 us -> 127 us (0.914)
  the two profiles are of different devices: /device:TPU:32 before, /device:TPU:2 now
where the time goes in v3:
time: 127 us; the launch traced here: 126 us
  starting transfers between devices  77.2 us (61%)
  Pallas kernels  24.8 us (20%)
  waiting for transfers between devices  18.3 us (14%)
  local copies, waits for them, and re-layouts  4.91 us (4%)
    ppermute x6, starting transfers between devices, swap(): return lax.ppermute(array, 'cq', [(i, i ^ step) for i in range(HEADS)])  20.2 us
    all_to_all x1, starting transfers between devices, on_device(): pre = lax.all_to_all(pre, ('cb', 'cq'), 0, 0)  12.5 us
    all_to_all x1, starting transfers between devices, on_device(): small = lax.all_to_all(small, Z, 0, 0)  11.1 us
    ppermute x6, waiting for transfers between devices, swap(): return lax.ppermute(array, 'cq', [(i, i ^ step) for i in range(HEADS)])  9.16 us
    ppermute x1, starting transfers between devices, on_device(): oth_hi = lax.ppermute(jnp.stack(pairs[2:4]), Z, ring(-4, early))  7.96 us
    all_to_all x1, starting transfers between devices, on_device(): parts = lax.all_to_all(pgrad, 'sib', 0, 0)  7.62 us
    all_to_all x1, starting transfers between devices, on_device(): pref = lax.all_to_all(spread, 'sib', 0, 0)  7.62 us
    ppermute x1, waiting for transfers between devices, on_device(): oth_hi = lax.ppermute(jnp.stack(pairs[2:4]), Z, ring(-4, early))  7.46 us
  transfers between devices with their start and end apart: 15, of which 5 were waited for; matrix products, arithmetic and copies ran while one was open for 1% of the time, Pallas kernels for 13%

profile of v3, /device:TPU:2, one launch (start us, length us, event | category | flops | bytes accessed | tf_op | source)
XLA Modules:
  0.0 126.2 jit_solution(17951142332229097369)
XLA Ops:
  0.6 1.3 %pack_prefix.1.pre = bf16[8,16,128]{2,1,0:T(8,128)(2,1)} custom-call(bf16[4,512]{1,0:T(4,128)(2,1)} %pk.1, bf16[4,512]{1,0:T(4,128)(2,1)} %pv.1), custom_call_target="tpu_custom_call" | custom-call | flops 1024 | bytes 65536 | tf_op jit(solution)/shard_map/pack_prefix/pallas_call | solution.py:325
  2.0 12.5 %all-to-all-start = ((bf16[8,16,128]{2,1,0:T(8,128)(2,1)}), bf16[8,16,128]{2,1,0:T(8,128)(2,1)S(1)}, u32[]{:S(2)}, u32[]{:S(2)}) async-start(bf16[8,16,128]{2,1,0:T(8,128)(2,1)} %pack_prefix.1.pre), calls=%async_computation | async-start | bytes 65536 | tf_op jit(solution)/shard_map/all_to_all | solution.py:348
  14.5 2.4 %pack_heads.1 = (bf16[784,128]{1,0:T(8,128)(2,1)}, bf16[784,128]{1,0:T(8,128)(2,1)}, bf16[784,128]{1,0:T(8,128)(2,1)}, bf16[784,128]{1,0:T(8,128)(2,1)}) custom-call(s32[32]{0:T(128)} %lengths.1, bf16[2,128,512]{2,1,0:T(8,128)(2,1)} %bitcast.16, bf16[2,128,512]{2,1,0:T(8,128)(2,1)} %bitcast.17, bf16[2,128,512]{2,1,0:T(8,128)(2,1)} %bitcast.18, ...), custom_call_target="tpu_custom_call" | custom-call | flops 8589934592 | bytes 2097152 | tf_op jit(solution)/shard_map/pack_heads/pallas_call | solution.py:333
  16.9 3.9 %collective-permute-start = (bf16[784,128]{1,0:T(8,128)(2,1)}, bf16[784,128]{1,0:T(8,128)(2,1)S(1)}, u32[]{:S(2)}, u32[]{:S(2)}) collective-permute-start(bf16[784,128]{1,0:T(8,128)(2,1)} %get-tuple-element.29), channel_id=1, source_target_pairs={{0,2},{2,0},{4,6},{6,4},{1,3},{3,1},{5,7},{7,5},{8,10},{10,8},{12,... | collective-permute-start | bytes 602120 | tf_op jit(solution)/shard_map/ppermute | solution.py:345
  20.8 4.3 %collective-permute-start.1 = (bf16[784,128]{1,0:T(8,128)(2,1)}, bf16[784,128]{1,0:T(8,128)(2,1)S(1)}, u32[]{:S(2)}, u32[]{:S(2)}) collective-permute-start(bf16[784,128]{1,0:T(8,128)(2,1)} %get-tuple-element.30), channel_id=1, source_target_pairs={{0,4},{2,6},{4,0},{6,2},{1,5},{3,7},{5,1},{7,3},{8,12},{10,14},{12... | collective-permute-start | bytes 602120 | tf_op jit(solution)/shard_map/ppermute | solution.py:345
  25.1 1.9 %collective-permute-start.2 = (bf16[784,128]{1,0:T(8,128)(2,1)}, bf16[784,128]{1,0:T(8,128)(2,1)S(1)}, u32[]{:S(2)}, u32[]{:S(2)}) collective-permute-start(bf16[784,128]{1,0:T(8,128)(2,1)} %get-tuple-element.31), channel_id=1, source_target_pairs={{0,6},{2,4},{4,2},{6,0},{1,7},{3,5},{5,3},{7,1},{8,14},{10,12},{12... | collective-permute-start | bytes 602120 | tf_op jit(solution)/shard_map/ppermute | solution.py:345
  27.0 0.8 slice_bitcast_fusion.3
  27.9 0.0 all-to-all-done.pre
  27.9 0.6 copy-done.5
  28.5 1.6 %spread_prefix.1 = bf16[32,64,128]{2,1,0:T(8,128)(2,1)} custom-call(bf16[8,16,128]{2,1,0:T(8,128)(2,1)} %copy-done.5), custom_call_target="tpu_custom_call" | custom-call | flops 262144 | bytes 524288 | tf_op jit(solution)/shard_map/spread_prefix/pallas_call | solution.py:353
  30.1 7.6 %all-to-all-start.1 = ((bf16[32,64,128]{2,1,0:T(8,128)(2,1)}), bf16[32,64,128]{2,1,0:T(8,128)(2,1)S(1)}, u32[]{:S(2)}, u32[]{:S(2)}) async-start(bf16[32,64,128]{2,1,0:T(8,128)(2,1)} %spread_prefix.1), calls=%async_computation.1 | async-start | bytes 1048576 | tf_op jit(solution)/shard_map/all_to_all | solution.py:361
  37.7 0.0 collective-permute-done.2.far3
  37.8 2.2 %collective-permute-done.1.far2 = bf16[784,128]{1,0:T(8,128)(2,1)S(1)} collective-permute-done((bf16[784,128]{1,0:T(8,128)(2,1)}, bf16[784,128]{1,0:T(8,128)(2,1)S(1)}, u32[]{:S(2)}, u32[]{:S(2)}) %collective-permute-start.1) | collective-permute-done | bytes 200736 | tf_op jit(solution)/shard_map/ppermute | solution.py:345
  40.0 0.0 copy-start
  40.0 8.0 %collective-permute-start.4 = (bf16[2,256,128]{2,1,0:T(8,128)(2,1)S(1)}, bf16[2,256,128]{2,1,0:T(8,128)(2,1)S(1)}, u32[]{:S(2)}, u32[]{:S(2)}) collective-permute-start(bf16[2,256,128]{2,1,0:T(8,128)(2,1)S(1)} %pad_maximum_fusion.1), channel_id=1, source_target_pairs={{0,9},{2,11},{4,13},{6,15},{1,8},{3,10},{5,12},{7,14},{16,25},{18,... | collective-permute-start | bytes 393224 | tf_op jit(solution)/shard_map/ppermute | solution.py:352
  47.9 0.0 collective-permute-done.far1
  48.0 1.3 %collective-permute-start.3 = (bf16[2,256,128]{2,1,0:T(8,128)(2,1)S(1)}, bf16[2,256,128]{2,1,0:T(8,128)(2,1)S(1)}, u32[]{:S(2)}, u32[]{:S(2)}) collective-permute-start(bf16[2,256,128]{2,1,0:T(8,128)(2,1)S(1)} %pad_maximum_fusion), channel_id=1, source_target_pairs={{0,8},{2,10},{4,12},{6,14},{1,9},{3,11},{5,13},{7,15},{16,24},{18,... | collective-permute-start | bytes 393224 | tf_op jit(solution)/shard_map/ppermute | solution.py:351
  49.3 0.0 all-to-all-done.1.pref
  49.3 2.1 %prefix_norms.1.pre_norms = f32[4,8,256]{2,1,0:T(8,128)S(1)} custom-call(bf16[784,128]{1,0:T(8,128)(2,1)S(1)} %copy-done, bf16[784,128]{1,0:T(8,128)(2,1)S(1)} %collective-permute-done.far1, bf16[784,128]{1,0:T(8,128)(2,1)S(1)} %collective-permute-done.1.far2, bf16[784,128]{1,0:T(8,128)(2,1)S(1)} %collective-permute-done.2.far3, ...), custom_call_target="tpu_custom_call" | custom-call | flops 8589934592 | bytes 1048576 | tf_op jit(solution)/shard_map/prefix_norms/pallas_call | solution.py:367
  51.4 7.5 %collective-permute-done.4.oth_hi = bf16[2,256,128]{2,1,0:T(8,128)(2,1)S(1)} collective-permute-done((bf16[2,256,128]{2,1,0:T(8,128)(2,1)S(1)}, bf16[2,256,128]{2,1,0:T(8,128)(2,1)S(1)}, u32[]{:S(2)}, u32[]{:S(2)}) %collective-permute-start.4) | collective-permute-done | bytes 131104 | tf_op jit(solution)/shard_map/ppermute | solution.py:352
  58.9 0.0 collective-permute-done.3.oth_lo
  58.9 5.2 %sibling_grads.1 = (bf16[4,128,128]{2,1,0:T(8,128)(2,1)S(1)}, bf16[4,128,128]{2,1,0:T(8,128)(2,1)S(1)}, bf16[4,128,128]{2,1,0:T(8,128)(2,1)S(1)}, bf16[4,128,128...) custom-call(bf16[784,128]{1,0:T(8,128)(2,1)S(1)} %copy-done, ...), custom_call_target="tpu_custom_call" | custom-call | flops 1342177280 | bytes 4194304 | tf_op jit(solution)/shard_map/sibling_grads/pallas_call | solution.py:381
  64.1 1.3 %collective-permute-start.5 = (bf16[4,128,128]{2,1,0:T(8,128)(2,1)S(1)}, bf16[4,128,128]{2,1,0:T(8,128)(2,1)S(1)}, u32[]{:S(2)}, u32[]{:S(2)}) collective-permute-start(bf16[4,128,128]{2,1,0:T(8,128)(2,1)S(1)} %get-tuple-element.36), channel_id=1, source_target_pairs={{8,1},{10,3},{12,5},{14,7},{9,0},{11,2},{13,4},{15,6},{24,17},{26,... | collective-permute-start | bytes 393224 | tf_op jit(solution)/shard_map/ppermute | solution.py:401
  65.4 1.3 %collective-permute-start.6 = (bf16[4,128,128]{2,1,0:T(8,128)(2,1)S(1)}, bf16[4,128,128]{2,1,0:T(8,128)(2,1)S(1)}, u32[]{:S(2)}, u32[]{:S(2)}) collective-permute-start(bf16[4,128,128]{2,1,0:T(8,128)(2,1)S(1)} %get-tuple-element.37), channel_id=1, source_target_pairs={{8,0},{10,2},{12,4},{14,6},{9,1},{11,3},{13,5},{15,7},{24,16},{26,... | collective-permute-start | bytes 393224 | tf_op jit(solution)/shard_map/ppermute | solution.py:402
  66.7 4.9 %prefix_grads.1 = (bf16[32,64,128]{2,1,0:T(8,128)(2,1)}, bf16[4,256,128]{2,1,0:T(8,128)(2,1)S(1)}) custom-call(bf16[784,128]{1,0:T(8,128)(2,1)S(1)} %copy-done, bf16[784,128]{1,0:T(8,128)(2,1)S(1)} %collective-permute-done.far1, bf16[784,128]{1,0:T(8,128)(2,1)S(1)} %collective-permute-done.1.far2, bf16[784,128]{1,0:T(8,128)(2,1)S(1)} %collective-permute-done.2.far3, ...), custom_call_target="tpu_custom_call" | custom-call | flops 68719476736 | bytes 4194304 | tf_op jit(solution)/shard_map/prefix_grads/pallas_call | solution.py:404
  71.6 0.7 copy-done.2
  72.3 7.6 %all-to-all-start.2 = ((bf16[32,64,128]{2,1,0:T(8,128)(2,1)}), bf16[32,64,128]{2,1,0:T(8,128)(2,1)S(1)}, u32[]{:S(2)}, u32[]{:S(2)}) async-start(bf16[32,64,128]{2,1,0:T(8,128)(2,1)} %get-tuple-element.34), calls=%async_computation.2 | async-start | bytes 1048576 | tf_op jit(solution)/shard_map/all_to_all | solution.py:422
  79.9 6.3 %collective-permute-start.7 = (bf16[4,128,128]{2,1,0:T(8,128)(2,1)S(1)}, bf16[4,128,128]{2,1,0:T(8,128)(2,1)S(1)}, u32[]{:S(2)}, u32[]{:S(2)}) collective-permute-start(bf16[4,128,128]{2,1,0:T(8,128)(2,1)S(1)} %get-tuple-element.39), channel_id=1, source_target_pairs={{0,1},{2,3},{4,5},{6,7},{8,9},{10,11},{12,13},{14,15},{1,0},{3,2},... | collective-permute-start | bytes 393224 | tf_op jit(solution)/shard_map/ppermute | solution.py:400
  86.3 0.0 collective-permute-done.5.got_plus
  86.3 0.0 collective-permute-done.6.got_minus
  86.3 0.6 copy-done.10
  86.9 0.0 copy-done.11
  87.0 1.8 %near_sums.1.near = f32[4,128,128]{2,1,0:T(8,128)} custom-call(bf16[4,128,128]{2,1,0:T(8,128)(2,1)} %copy-done.1, bf16[4,128,128]{2,1,0:T(8,128)(2,1)} %copy-done.10, bf16[4,128,128]{2,1,0:T(8,128)(2,1)} %copy-done.11), custom_call_target="tpu_custom_call" | custom-call | flops 68719476736 | bytes 1048576 | tf_op jit(solution)/shard_map/near_sums/pallas_call | solution.py:423
  88.7 1.7 %all-to-all-done.2.parts = bf16[32,64,128]{2,1,0:T(8,128)(2,1)S(1)} async-done(((bf16[32,64,128]{2,1,0:T(8,128)(2,1)}), bf16[32,64,128]{2,1,0:T(8,128)(2,1)S(1)}, u32[]{:S(2)}, u32[]{:S(2)}) %all-to-all-start.2) | async-done | bytes 524320 | tf_op jit(solution)/shard_map/all_to_all | solution.py:422
  90.4 0.8 copy-done.3
  91.2 1.8 %prefix_sums.1 = f32[16,8,128]{2,1,0:T(8,128)} custom-call(bf16[32,64,128]{2,1,0:T(8,128)(2,1)} %copy-done.3), custom_call_target="tpu_custom_call" | custom-call | flops 262144 | bytes 524288 | tf_op jit(solution)/shard_map/prefix_sums/pallas_call | solution.py:440
  93.0 11.1 %all-to-all-start.3 = ((f32[16,8,128]{2,1,0:T(8,128)}), f32[16,8,128]{2,1,0:T(8,128)S(1)}, u32[]{:S(2)}, u32[]{:S(2)}) async-start(f32[16,8,128]{2,1,0:T(8,128)} %prefix_sums.1), calls=%async_computation.3 | async-start | bytes 131072 | tf_op jit(solution)/shard_map/all_to_all | solution.py:448
  104.1 0.6 copy-done.9
  104.7 1.9 %merge_grads.1 = (bf16[384,128]{1,0:T(8,128)(2,1)}, bf16[384,128]{1,0:T(8,128)(2,1)}, bf16[384,128]{1,0:T(8,128)(2,1)}, bf16[384,128]{1,0:T(8,128)(2,1)}) custom-call(f32[4,128,128]{2,1,0:T(8,128)} %near_sums.1.near, bf16[4,128,128]{2,1,0:T(8,128)(2,1)} %copy-done.9, bf16[4,256,128]{2,1,0:T(8,128)(2,1)} %copy-done.2), custom_call_target="tpu_custom_call" | custom-call | flops 68719476736 | bytes 1048576 | tf_op jit(solution)/shard_map/merge_grads/pallas_call | solution.py:432
  106.6 5.6 %collective-permute-start.10 = (bf16[384,128]{1,0:T(8,128)(2,1)}, bf16[384,128]{1,0:T(8,128)(2,1)S(1)}, u32[]{:S(2)}, u32[]{:S(2)}) collective-permute-start(bf16[384,128]{1,0:T(8,128)(2,1)} %get-tuple-element.44), channel_id=1, source_target_pairs={{0,6},{2,4},{4,2},{6,0},{1,7},{3,5},{5,3},{7,1},{8,14},{10,12},{12... | collective-permute-start | bytes 294920 | tf_op jit(solution)/shard_map/ppermute | solution.py:345
  112.2 1.9 %collective-permute-start.8 = (bf16[384,128]{1,0:T(8,128)(2,1)}, bf16[384,128]{1,0:T(8,128)(2,1)S(1)}, u32[]{:S(2)}, u32[]{:S(2)}) collective-permute-start(bf16[384,128]{1,0:T(8,128)(2,1)} %get-tuple-element.42), channel_id=1, source_target_pairs={{0,2},{2,0},{4,6},{6,4},{1,3},{3,1},{5,7},{7,5},{8,10},{10,8},{12,... | collective-permute-start | bytes 294920 | tf_op jit(solution)/shard_map/ppermute | solution.py:345
  114.1 2.6 %collective-permute-start.9 = (bf16[384,128]{1,0:T(8,128)(2,1)}, bf16[384,128]{1,0:T(8,128)(2,1)S(1)}, u32[]{:S(2)}, u32[]{:S(2)}) collective-permute-start(bf16[384,128]{1,0:T(8,128)(2,1)} %get-tuple-element.43), channel_id=1, source_target_pairs={{0,4},{2,6},{4,0},{6,2},{1,5},{3,7},{5,1},{7,3},{8,12},{10,14},{12... | collective-permute-start | bytes 294920 | tf_op jit(solution)/shard_map/ppermute | solution.py:345
  116.7 2.2 %collective-permute-done.8.back1 = bf16[384,128]{1,0:T(8,128)(2,1)S(1)} collective-permute-done((bf16[384,128]{1,0:T(8,128)(2,1)}, bf16[384,128]{1,0:T(8,128)(2,1)S(1)}, u32[]{:S(2)}, u32[]{:S(2)}) %collective-permute-start.8) | collective-permute-done | bytes 98336 | tf_op jit(solution)/shard_map/ppermute | solution.py:345
  118.9 4.8 %collective-permute-done.9.back2 = bf16[384,128]{1,0:T(8,128)(2,1)S(1)} collective-permute-done((bf16[384,128]{1,0:T(8,128)(2,1)}, bf16[384,128]{1,0:T(8,128)(2,1)S(1)}, u32[]{:S(2)}, u32[]{:S(2)}) %collective-permute-start.9) | collective-permute-done | bytes 98336 | tf_op jit(solution)/shard_map/ppermute | solution.py:345
  123.7 0.0 all-to-all-done.3.small
  123.7 0.6 copy-done.8
  124.3 0.0 copy-done.4
  124.4 1.8 %unpack_heads.1 = (bf16[2,128,512]{2,1,0:T(8,128)(2,1)}, bf16[64,512]{1,0:T(8,128)(2,1)}, bf16[64,512]{1,0:T(8,128)(2,1)}, bf16[2,512]{1,0:T(2,128)(2,1)}, bf16[2,512]{1,0:T(2,128)(2,1)}) custom-call(bf16[384,128]{1,0:T(8,128)(2,1)} %get-tuple-element.41.back0, bf16[384,128]{1,0:T(8,128)(2,1)} %copy-done.7, bf16[384,128]{1,0:T(8,128)(2,1)} %copy-done.8, ...), custom_call_target="tpu_custom_call" | custom-call | flops 262144 | bytes 1048576 | tf_op jit(solution)/shard_map/unpack_heads/pallas_call | solution.py:451
  (22 shorter events, 0.1 us)
Async XLA Ops:
  2.0 25.9 %all-to-all-start = ((bf16[8,16,128]{2,1,0:T(8,128)(2,1)}), bf16[8,16,128]{2,1,0:T(8,128)(2,1)S(1)}, u32[]{:S(2)}, u32[]{:S(2)}) async-start(bf16[8,16,128]{2,1,0:T(8,128)(2,1)} %pack_prefix.1.pre), calls=%async_computation | async-start | bytes 65536 | tf_op jit(solution)/shard_map/all_to_all | solution.py:348
  16.9 31.0 %collective-permute-start = (bf16[784,128]{1,0:T(8,128)(2,1)}, bf16[784,128]{1,0:T(8,128)(2,1)S(1)}, u32[]{:S(2)}, u32[]{:S(2)}) collective-permute-start(bf16[784,128]{1,0:T(8,128)(2,1)} %get-tuple-element.29), channel_id=1, source_target_pairs={{0,2},{2,0},{4,6},{6,4},{1,3},{3,1},{5,7},{7,5},{8,10},{10,8},{12,... | collective-permute-start | bytes 602120 | tf_op jit(solution)/shard_map/ppermute | solution.py:345
  20.8 19.1 %collective-permute-start.1 = (bf16[784,128]{1,0:T(8,128)(2,1)}, bf16[784,128]{1,0:T(8,128)(2,1)S(1)}, u32[]{:S(2)}, u32[]{:S(2)}) collective-permute-start(bf16[784,128]{1,0:T(8,128)(2,1)} %get-tuple-element.30), channel_id=1, source_target_pairs={{0,4},{2,6},{4,0},{6,2},{1,5},{3,7},{5,1},{7,3},{8,12},{10,14},{12... | collective-permute-start | bytes 602120 | tf_op jit(solution)/shard_map/ppermute | solution.py:345
  25.1 12.6 %collective-permute-start.2 = (bf16[784,128]{1,0:T(8,128)(2,1)}, bf16[784,128]{1,0:T(8,128)(2,1)S(1)}, u32[]{:S(2)}, u32[]{:S(2)}) collective-permute-start(bf16[784,128]{1,0:T(8,128)(2,1)} %get-tuple-element.31), channel_id=1, source_target_pairs={{0,6},{2,4},{4,2},{6,0},{1,7},{3,5},{5,3},{7,1},{8,14},{10,12},{12... | collective-permute-start | bytes 602120 | tf_op jit(solution)/shard_map/ppermute | solution.py:345
  27.9 0.6 copy-start.5
  30.1 19.2 %all-to-all-start.1 = ((bf16[32,64,128]{2,1,0:T(8,128)(2,1)}), bf16[32,64,128]{2,1,0:T(8,128)(2,1)S(1)}, u32[]{:S(2)}, u32[]{:S(2)}) async-start(bf16[32,64,128]{2,1,0:T(8,128)(2,1)} %spread_prefix.1), calls=%async_computation.1 | async-start | bytes 1048576 | tf_op jit(solution)/shard_map/all_to_all | solution.py:361
  40.0 9.3 %copy-start = (bf16[784,128]{1,0:T(8,128)(2,1)S(1)}, bf16[784,128]{1,0:T(8,128)(2,1)}, u32[]{:S(2)}) copy-start(bf16[784,128]{1,0:T(8,128)(2,1)} %get-tuple-element.28.own) | copy-start | bytes 602116
  40.0 18.9 %collective-permute-start.4 = (bf16[2,256,128]{2,1,0:T(8,128)(2,1)S(1)}, bf16[2,256,128]{2,1,0:T(8,128)(2,1)S(1)}, u32[]{:S(2)}, u32[]{:S(2)}) collective-permute-start(bf16[2,256,128]{2,1,0:T(8,128)(2,1)S(1)} %pad_maximum_fusion.1), channel_id=1, source_target_pairs={{0,9},{2,11},{4,13},{6,15},{1,8},{3,10},{5,12},{7,14},{16,25},{18,... | collective-permute-start | bytes 393224 | tf_op jit(solution)/shard_map/ppermute | solution.py:352
  48.0 10.9 %collective-permute-start.3 = (bf16[2,256,128]{2,1,0:T(8,128)(2,1)S(1)}, bf16[2,256,128]{2,1,0:T(8,128)(2,1)S(1)}, u32[]{:S(2)}, u32[]{:S(2)}) collective-permute-start(bf16[2,256,128]{2,1,0:T(8,128)(2,1)S(1)} %pad_maximum_fusion), channel_id=1, source_target_pairs={{0,8},{2,10},{4,12},{6,14},{1,9},{3,11},{5,13},{7,15},{16,24},{18,... | collective-permute-start | bytes 393224 | tf_op jit(solution)/shard_map/ppermute | solution.py:351
  64.1 7.5 %copy-start.1 = (bf16[4,128,128]{2,1,0:T(8,128)(2,1)}, bf16[4,128,128]{2,1,0:T(8,128)(2,1)S(1)}, u32[]{:S(2)}) copy-start(bf16[4,128,128]{2,1,0:T(8,128)(2,1)S(1)} %get-tuple-element.35.keep) | copy-start | bytes 393220
  64.1 22.1 %collective-permute-start.5 = (bf16[4,128,128]{2,1,0:T(8,128)(2,1)S(1)}, bf16[4,128,128]{2,1,0:T(8,128)(2,1)S(1)}, u32[]{:S(2)}, u32[]{:S(2)}) collective-permute-start(bf16[4,128,128]{2,1,0:T(8,128)(2,1)S(1)} %get-tuple-element.36), channel_id=1, source_target_pairs={{8,1},{10,3},{12,5},{14,7},{9,0},{11,2},{13,4},{15,6},{24,17},{26,... | collective-permute-start | bytes 393224 | tf_op jit(solution)/shard_map/ppermute | solution.py:401
  65.4 20.9 %collective-permute-start.6 = (bf16[4,128,128]{2,1,0:T(8,128)(2,1)S(1)}, bf16[4,128,128]{2,1,0:T(8,128)(2,1)S(1)}, u32[]{:S(2)}, u32[]{:S(2)}) collective-permute-start(bf16[4,128,128]{2,1,0:T(8,128)(2,1)S(1)} %get-tuple-element.37), channel_id=1, source_target_pairs={{8,0},{10,2},{12,4},{14,6},{9,1},{11,3},{13,5},{15,7},{24,16},{26,... | collective-permute-start | bytes 393224 | tf_op jit(solution)/shard_map/ppermute | solution.py:402
  71.6 0.7 copy-start.2
  72.3 18.1 %all-to-all-start.2 = ((bf16[32,64,128]{2,1,0:T(8,128)(2,1)}), bf16[32,64,128]{2,1,0:T(8,128)(2,1)S(1)}, u32[]{:S(2)}, u32[]{:S(2)}) async-start(bf16[32,64,128]{2,1,0:T(8,128)(2,1)} %get-tuple-element.34), calls=%async_computation.2 | async-start | bytes 1048576 | tf_op jit(solution)/shard_map/all_to_all | solution.py:422
  79.9 24.1 %collective-permute-start.7 = (bf16[4,128,128]{2,1,0:T(8,128)(2,1)S(1)}, bf16[4,128,128]{2,1,0:T(8,128)(2,1)S(1)}, u32[]{:S(2)}, u32[]{:S(2)}) collective-permute-start(bf16[4,128,128]{2,1,0:T(8,128)(2,1)S(1)} %get-tuple-element.39), channel_id=1, source_target_pairs={{0,1},{2,3},{4,5},{6,7},{8,9},{10,11},{12,13},{14,15},{1,0},{3,2},... | collective-permute-start | bytes 393224 | tf_op jit(solution)/shard_map/ppermute | solution.py:400
  86.3 0.6 copy-start.10
  86.3 0.7 copy-start.11
  90.4 0.8 copy-start.3
  93.0 30.7 %all-to-all-start.3 = ((f32[16,8,128]{2,1,0:T(8,128)}), f32[16,8,128]{2,1,0:T(8,128)S(1)}, u32[]{:S(2)}, u32[]{:S(2)}) async-start(f32[16,8,128]{2,1,0:T(8,128)} %prefix_sums.1), calls=%async_computation.3 | async-start | bytes 131072 | tf_op jit(solution)/shard_map/all_to_all | solution.py:448
  104.1 0.6 copy-start.9
  106.6 10.1 %collective-permute-start.10 = (bf16[384,128]{1,0:T(8,128)(2,1)}, bf16[384,128]{1,0:T(8,128)(2,1)S(1)}, u32[]{:S(2)}, u32[]{:S(2)}) collective-permute-start(bf16[384,128]{1,0:T(8,128)(2,1)} %get-tuple-element.44), channel_id=1, source_target_pairs={{0,6},{2,4},{4,2},{6,0},{1,7},{3,5},{5,3},{7,1},{8,14},{10,12},{12... | collective-permute-start | bytes 294920 | tf_op jit(solution)/shard_map/ppermute | solution.py:345
  112.2 6.7 %collective-permute-start.8 = (bf16[384,128]{1,0:T(8,128)(2,1)}, bf16[384,128]{1,0:T(8,128)(2,1)S(1)}, u32[]{:S(2)}, u32[]{:S(2)}) collective-permute-start(bf16[384,128]{1,0:T(8,128)(2,1)} %get-tuple-element.42), channel_id=1, source_target_pairs={{0,2},{2,0},{4,6},{6,4},{1,3},{3,1},{5,7},{7,5},{8,10},{10,8},{12,... | collective-permute-start | bytes 294920 | tf_op jit(solution)/shard_map/ppermute | solution.py:345
  114.1 9.6 %collective-permute-start.9 = (bf16[384,128]{1,0:T(8,128)(2,1)}, bf16[384,128]{1,0:T(8,128)(2,1)S(1)}, u32[]{:S(2)}, u32[]{:S(2)}) collective-permute-start(bf16[384,128]{1,0:T(8,128)(2,1)} %get-tuple-element.43), channel_id=1, source_target_pairs={{0,4},{2,6},{4,0},{6,2},{1,5},{3,7},{5,1},{7,3},{8,12},{10,14},{12... | collective-permute-start | bytes 294920 | tf_op jit(solution)/shard_map/ppermute | solution.py:345
  116.7 7.0 %copy-start.6 = (bf16[384,128]{1,0:T(8,128)(2,1)}, bf16[384,128]{1,0:T(8,128)(2,1)S(1)}, u32[]{:S(2)}) copy-start(bf16[384,128]{1,0:T(8,128)(2,1)S(1)} %collective-permute-done.10.back3) | copy-start | bytes 294916
  118.9 4.8 %copy-start.7 = (bf16[384,128]{1,0:T(8,128)(2,1)}, bf16[384,128]{1,0:T(8,128)(2,1)S(1)}, u32[]{:S(2)}) copy-start(bf16[384,128]{1,0:T(8,128)(2,1)S(1)} %collective-permute-done.8.back1) | copy-start | bytes 294916
  123.7 0.6 copy-start.8
  123.7 0.7 copy-start.4

commit v4 on v3

--- a/solution.py
+++ b/solution.py
@@ -99,16 +99,16 @@
         values[rows, :] = pref[:, part * 32 + 16 : part * 32 + 32, :].reshape(pre, LANES)
 
 
-def tile_data(bulk, step):
+def tile_data(bulk):
     wide = GROUPS * ROWS
-    rest = bulk[step, 6 * ROWS : 6 * ROWS + 16, :].astype(jnp.float32)
-    delta = jnp.concatenate([rest[s : s + 1] for s in range(GROUPS)], axis=1)
-    return bulk[step, 0:wide, :], bulk[step, wide : 2 * wide, :], delta
-
-
-def gather_bulk(bulk, own, far1, far2, far3):
-    for step, received in enumerate((own, far1, far2, far3)):
-        bulk[step] = received[...]
+    steps = range(HEADS)
+    deltas = []
+    for step in steps:
+        rest = bulk[step][6 * ROWS : 6 * ROWS + 16, :].astype(jnp.float32)
+        deltas += [rest[s : s + 1] for s in range(GROUPS)]
+    queries = jnp.concatenate([bulk[step][0:wide, :] for step in steps], axis=0)
+    grads = jnp.concatenate([bulk[step][wide : 2 * wide, :] for step in steps], axis=0)
+    return queries, grads, jnp.concatenate(deltas, axis=1)
 
 
 def transpose_keys(keys, keys_t, start, stop, chunk):
@@ -129,39 +129,40 @@
         if values is not None:
             values[rows, :] = src[ROWS : 2 * ROWS, :]
         rows = pl.ds(pl.multiple_of(base + half + at, ROWS), ROWS)
-        keys[rows, :] = bulk[step, 4 * ROWS : 5 * ROWS, :]
+        keys[rows, :] = bulk[step][4 * ROWS : 5 * ROWS, :]
         if values is not None:
-            values[rows, :] = bulk[step, 5 * ROWS : 6 * ROWS, :]
-
-
-def sibling_scores(keys, queries, at, tile):
+            values[rows, :] = bulk[step][5 * ROWS : 6 * ROWS, :]
+
+
+def sibling_scores(keys, queries, at):
     half = HEADS * ROWS
     s = dot_nt(keys, queries) * (LOG2E / math.sqrt(LANES))
     if at >= half:
-        position = tile * ROWS + lax.rem(lax.broadcasted_iota(jnp.int32, s.shape, 1), ROWS)
+        cq = lax.axis_index("cq")
+        lane = lax.broadcasted_iota(jnp.int32, (1, s.shape[1]), 1)
+        tile = jnp.bitwise_xor(cq, lane // (GROUPS * ROWS))
+        position = tile * ROWS + lax.rem(lane, ROWS)
         key_at = lax.broadcasted_iota(jnp.int32, s.shape, 0) + (at - half)
         return jnp.where(key_at <= position, s, NEG)
     return jnp.where(lax.axis_index("cb") == 1, s, NEG)
 
 
-def norms_kernel(chunk, own, far1, far2, far3, pref, norms, keys, bulk):
+def norms_kernel(chunk, own, far1, far2, far3, pref, norms, keys):
     n_sib = pref.shape[0]
     pre = n_sib * 32
-    wide = GROUPS * ROWS
-    gather_bulk(bulk, own, far1, far2, far3)
+    wide = HEADS * GROUPS * ROWS
+    bulk = (own, far1, far2, far3)
     for part in range(2):
         rows = slice(part * pre // 2, (part + 1) * pre // 2)
         keys[rows, :] = pref[:, part * 32 : part * 32 + 16, :].reshape(pre // 2, LANES)
 
-    @pl.loop(0, HEADS)
-    def _(step):
-        queries, grads, delta = tile_data(bulk, step)
-        top = jnp.full((1, wide), NEG, jnp.float32)
-        norm = jnp.zeros((1, wide), jnp.float32)
-        for at in range(0, pre, chunk):
-            s = dot_nt(keys[at : at + chunk, :], queries) * (LOG2E / math.sqrt(LANES))
-            top, norm = online(s, top, norm)
-        norms[step] = jnp.broadcast_to(top + jnp.log2(norm), (8, wide))
+    queries, grads, delta = tile_data(bulk)
+    top = jnp.full((1, wide), NEG, jnp.float32)
+    norm = jnp.zeros((1, wide), jnp.float32)
+    for at in range(0, pre, chunk):
+        s = dot_nt(keys[at : at + chunk, :], queries) * (LOG2E / math.sqrt(LANES))
+        top, norm = online(s, top, norm)
+    norms[...] = jnp.broadcast_to(top + jnp.log2(norm), (8, wide))
 
 
 def online(s, top, norm):
@@ -173,45 +174,40 @@
 def sibling_kernel(
     chunk, own, far1, far2, far3, oth_lo, oth_hi, pre_norms,
     keep, send8, plus, minus, norms, dq_part,
-    keys, values, keys_t, scores, dk_acc, dv_acc, bulk,
+    keys, values, keys_t, scores, dk_acc, dv_acc,
 ):
     scale = 1.0 / math.sqrt(LANES)
     total = keys.shape[0]
     half = HEADS * ROWS
-    wide = GROUPS * ROWS
-    gather_bulk(bulk, own, far1, far2, far3)
+    wide = HEADS * GROUPS * ROWS
+    bulk = (own, far1, far2, far3)
     load_sibling(bulk, oth_lo, oth_hi, keys, values, 0)
     transpose_keys(keys, keys_t, 0, total, chunk)
-    dk_acc[...] = jnp.zeros_like(dk_acc)
-    dv_acc[...] = jnp.zeros_like(dv_acc)
-
-    @pl.loop(0, HEADS)
-    def _(step):
-        tile = jnp.bitwise_xor(lax.axis_index("cq"), step)
-        queries, grads, delta = tile_data(bulk, step)
-        top = pre_norms[step][0:1]
-        norm = jnp.ones((1, wide), jnp.float32)
-        tops = []
-        for at in range(0, total, chunk):
-            s = sibling_scores(keys[at : at + chunk, :], queries, at, tile)
-            higher = jnp.maximum(top, jnp.max(s, axis=0, keepdims=True))
-            e = jnp.exp2(s - higher)
-            scores[at : at + chunk, :] = e
-            norm = norm * jnp.exp2(top - higher) + jnp.sum(e, axis=0, keepdims=True)
-            top = higher
-            tops.append(top)
-        log_norm = top + jnp.log2(norm)
-        norms[step] = jnp.broadcast_to(log_norm, (8, wide))
-        dq_t = jnp.zeros((LANES, wide), jnp.float32)
-        for at in range(0, total, chunk):
-            rows = slice(at, at + chunk)
-            p = scores[rows, :] * jnp.exp2(tops[at // chunk] - log_norm)
-            dp = dot_nt(values[rows, :], grads)
-            ds = (p * (dp - delta)).astype(jnp.bfloat16)
-            dv_acc[rows, :] += dot_nn(p.astype(jnp.bfloat16), grads)
-            dk_acc[rows, :] += dot_nn(ds, queries)
-            dq_t = dq_t + dot_nn(keys_t[:, rows], ds)
-        dq_part[step, :, :] = dq_t
+
+    queries, grads, delta = tile_data(bulk)
+    top = pre_norms[0:1]
+    norm = jnp.ones((1, wide), jnp.float32)
+    tops = []
+    for at in range(0, total, chunk):
+        s = sibling_scores(keys[at : at + chunk, :], queries, at)
+        higher = jnp.maximum(top, jnp.max(s, axis=0, keepdims=True))
+        e = jnp.exp2(s - higher)
+        scores[at : at + chunk, :] = e
+        norm = norm * jnp.exp2(top - higher) + jnp.sum(e, axis=0, keepdims=True)
+        top = higher
+        tops.append(top)
+    log_norm = top + jnp.log2(norm)
+    norms[...] = jnp.broadcast_to(log_norm, (8, wide))
+    dq_t = jnp.zeros((LANES, wide), jnp.float32)
+    for at in range(0, total, chunk):
+        rows = slice(at, at + chunk)
+        p = scores[rows, :] * jnp.exp2(tops[at // chunk] - log_norm)
+        dp = dot_nt(values[rows, :], grads)
+        ds = (p * (dp - delta)).astype(jnp.bfloat16)
+        dv_acc[rows, :] = dot_nn(p.astype(jnp.bfloat16), grads)
+        dk_acc[rows, :] = dot_nn(ds, queries)
+        dq_t = dq_t + dot_nn(keys_t[:, rows], ds)
+    dq_part[...] = dq_t
 
     tp = lax.axis_index("tp")
     for out, base, which in (
@@ -229,31 +225,29 @@
 def prefix_kernel(
     chunk, own, far1, far2, far3, pref, norms, dq_part,
     pgrad, dq,
-    keys, values, keys_t, dk_acc, dv_acc, bulk,
+    keys, values, keys_t, dk_acc, dv_acc,
 ):
     scale = 1.0 / math.sqrt(LANES)
     n_sib = pref.shape[0]
     pre = n_sib * 32
-    gather_bulk(bulk, own, far1, far2, far3)
+    bulk = (own, far1, far2, far3)
     load_keys(pref, keys, values)
     transpose_keys(keys, keys_t, 0, pre, chunk)
-    dk_acc[...] = jnp.zeros_like(dk_acc)
-    dv_acc[...] = jnp.zeros_like(dv_acc)
-
-    @pl.loop(0, HEADS)
-    def _(step):
-        queries, grads, delta = tile_data(bulk, step)
-        norm = norms[step][0:1]
-        dq_t = dq_part[step]
-        for at in range(0, pre, chunk):
-            rows = slice(at, at + chunk)
-            p = jnp.exp2(dot_nt(keys[rows, :], queries) * (scale * LOG2E) - norm)
-            dp = dot_nt(values[rows, :], grads)
-            ds = (p * (dp - delta)).astype(jnp.bfloat16)
-            dv_acc[rows, :] += dot_nn(p.astype(jnp.bfloat16), grads)
-            dk_acc[rows, :] += dot_nn(ds, queries)
-            dq_t = dq_t + dot_nn(keys_t[:, rows], ds)
-        dq[step, :, :] = (dq_t.T * scale).astype(jnp.bfloat16)
+
+    queries, grads, delta = tile_data(bulk)
+    norm = norms[0:1]
+    dq_t = dq_part[...]
+    for at in range(0, pre, chunk):
+        rows = slice(at, at + chunk)
+        p = jnp.exp2(dot_nt(keys[rows, :], queries) * (scale * LOG2E) - norm)
+        dp = dot_nt(values[rows, :], grads)
+        ds = (p * (dp - delta)).astype(jnp.bfloat16)
+        dv_acc[rows, :] = dot_nn(p.astype(jnp.bfloat16), grads)
+        dk_acc[rows, :] = dot_nn(ds, queries)
+        dq_t = dq_t + dot_nn(keys_t[:, rows], ds)
+    total = (dq_t.T * scale).astype(jnp.bfloat16)
+    for step in range(HEADS):
+        dq[step, :, :] = total[step * GROUPS * ROWS : (step + 1) * GROUPS * ROWS]
 
     for part in range(2):
         rows = slice(part * pre // 2, (part + 1) * pre // 2)
@@ -363,15 +357,14 @@
     chunk = min(512, n_sib * 16)
     pre_rows, sib_rows = 32 * n_sib, 2 * HEADS * ROWS
     wide = GROUPS * ROWS
-    norm_rows = shape((HEADS, 8, wide), jnp.float32)
+    norm_rows = shape((8, HEADS * wide), jnp.float32)
     pre_norms = pl.pallas_call(
-        functools.partial(norms_kernel, chunk),
+        functools.partial(norms_kernel, min(512, n_sib * 32)),
         out_shape=norm_rows,
         in_specs=vmem(5),
         out_specs=vmem(1)[0],
         scratch_shapes=[
             pltpu.VMEM((pre_rows, LANES), bf16),
-            pltpu.VMEM((HEADS, 784, LANES), bf16),
         ],
         compiler_params=pltpu.CompilerParams(vmem_limit_bytes=32 << 20),
         cost_estimate=cost(NORMS_COST, 1 << 20, HEADS * wide * 1024),
@@ -380,17 +373,16 @@
     piece = shape((HEADS, ROWS, LANES), bf16)
     keep, send8, plus, minus, norms, dq_part = pl.pallas_call(
         functools.partial(sibling_kernel, chunk),
-        out_shape=(piece,) * 4 + (norm_rows, shape((HEADS, LANES, wide), jnp.float32)),
+        out_shape=(piece,) * 4 + (norm_rows, shape((LANES, HEADS * wide), jnp.float32)),
         in_specs=vmem(7),
         out_specs=tuple(vmem(6)),
         scratch_shapes=[
             pltpu.VMEM((sib_rows, LANES), bf16),
             pltpu.VMEM((sib_rows, LANES), bf16),
             pltpu.VMEM((LANES, sib_rows), bf16),
-            pltpu.VMEM((sib_rows, wide), jnp.float32),
+            pltpu.VMEM((sib_rows, HEADS * wide), jnp.float32),
             pltpu.VMEM((sib_rows, LANES), jnp.float32),
             pltpu.VMEM((sib_rows, LANES), jnp.float32),
-            pltpu.VMEM((HEADS, 784, LANES), bf16),
         ],
         compiler_params=pltpu.CompilerParams(vmem_limit_bytes=32 << 20),
         cost_estimate=cost(10 * HEADS * wide * 1024 * LANES, 4 << 20, HEADS * wide * 1024),
@@ -402,7 +394,7 @@
     got_minus = lax.ppermute(minus, Z, ring(-4, late))
 
     pgrad, dq = pl.pallas_call(
-        functools.partial(prefix_kernel, chunk),
+        functools.partial(prefix_kernel, min(512, n_sib * 32)),
         out_shape=(shape((n_sib, 64, LANES), bf16), shape((HEADS, wide, LANES), bf16)),
         in_specs=vmem(7),
         out_specs=tuple(vmem(2)),
@@ -412,7 +404,6 @@
             pltpu.VMEM((LANES, pre_rows), bf16),
             pltpu.VMEM((pre_rows, LANES), jnp.float32),
             pltpu.VMEM((pre_rows, LANES), jnp.float32),
-            pltpu.VMEM((HEADS, 784, LANES), bf16),
         ],
         compiler_params=pltpu.CompilerParams(vmem_limit_bytes=32 << 20),
         cost_estimate=cost(GRADS_COST, 4 << 20, HEADS * wide * 1024),

time: 127 us -> 124 us (0.976)
  Pallas kernels: 24.8 us -> 21.2 us
    pallas_call x2, Pallas kernels: 6.95 us -> 4.65 us  [the longest x1 3.3 us: on_device(): pl.pallas_call(functools.partial(prefix_kernel, min(512, n_sib * 32)), ou...]
  transfers between devices with their start and end apart: 15 -> 15, of which waited for: 5 -> 5; matrix products, arithmetic and copies ran while one was open for 1% -> 1% of each run, Pallas kernels for 13% -> 11%
where the time goes in v4:
time: 124 us; the launch traced here: 123 us
  starting transfers between devices  77.3 us (62%)
  Pallas kernels  21.2 us (17%)
  waiting for transfers between devices  19 us (15%)
  local copies, waits for them, and re-layouts  4.91 us (4%)
    ppermute x6, starting transfers between devices, swap(): return lax.ppermute(array, 'cq', [(i, i ^ step) for i in range(HEADS)])  20.2 us
    all_to_all x1, starting transfers between devices, on_device(): pre = lax.all_to_all(pre, ('cb', 'cq'), 0, 0)  12.5 us
    all_to_all x1, starting transfers between devices, on_device(): small = lax.all_to_all(small, Z, 0, 0)  11.1 us
    ppermute x6, waiting for transfers between devices, swap(): return lax.ppermute(array, 'cq', [(i, i ^ step) for i in range(HEADS)])  9.14 us
    ppermute x1, waiting for transfers between devices, on_device(): oth_hi = lax.ppermute(jnp.stack(pairs[2:4]), Z, ring(-4, early))  8.2 us
    ppermute x1, starting transfers between devices, on_device(): oth_hi = lax.ppermute(jnp.stack(pairs[2:4]), Z, ring(-4, early))  7.96 us
    all_to_all x1, starting transfers between devices, on_device(): parts = lax.all_to_all(pgrad, 'sib', 0, 0)  7.62 us
    all_to_all x1, starting transfers between devices, on_device(): pref = lax.all_to_all(spread, 'sib', 0, 0)  7.62 us
  transfers between devices with their start and end apart: 15, of which 5 were waited for; matrix products, arithmetic and copies ran while one was open for 1% of the time, Pallas kernels for 11%

profile of v4, /device:TPU:2, one launch (start us, length us, event | category | flops | bytes accessed | tf_op | source)
XLA Modules:
  0.0 123.4 jit_solution(16010799497007595954)
XLA Ops:
  0.6 1.3 %pack_prefix.1.pre = bf16[8,16,128]{2,1,0:T(8,128)(2,1)} custom-call(bf16[4,512]{1,0:T(4,128)(2,1)} %pk.1, bf16[4,512]{1,0:T(4,128)(2,1)} %pv.1), custom_call_target="tpu_custom_call" | custom-call | flops 1024 | bytes 65536 | tf_op jit(solution)/shard_map/pack_prefix/pallas_call | solution.py:319
  2.0 12.5 %all-to-all-start = ((bf16[8,16,128]{2,1,0:T(8,128)(2,1)}), bf16[8,16,128]{2,1,0:T(8,128)(2,1)S(1)}, u32[]{:S(2)}, u32[]{:S(2)}) async-start(bf16[8,16,128]{2,1,0:T(8,128)(2,1)} %pack_prefix.1.pre), calls=%async_computation | async-start | bytes 65536 | tf_op jit(solution)/shard_map/all_to_all | solution.py:342
  14.5 2.4 %pack_heads.1 = (bf16[784,128]{1,0:T(8,128)(2,1)}, bf16[784,128]{1,0:T(8,128)(2,1)}, bf16[784,128]{1,0:T(8,128)(2,1)}, bf16[784,128]{1,0:T(8,128)(2,1)}) custom-call(s32[32]{0:T(128)} %lengths.1, bf16[2,128,512]{2,1,0:T(8,128)(2,1)} %bitcast.16, bf16[2,128,512]{2,1,0:T(8,128)(2,1)} %bitcast.17, bf16[2,128,512]{2,1,0:T(8,128)(2,1)} %bitcast.18, ...), custom_call_target="tpu_custom_call" | custom-call | flops 8589934592 | bytes 2097152 | tf_op jit(solution)/shard_map/pack_heads/pallas_call | solution.py:327
  16.9 3.9 %collective-permute-start = (bf16[784,128]{1,0:T(8,128)(2,1)}, bf16[784,128]{1,0:T(8,128)(2,1)S(1)}, u32[]{:S(2)}, u32[]{:S(2)}) collective-permute-start(bf16[784,128]{1,0:T(8,128)(2,1)} %get-tuple-element.29), channel_id=1, source_target_pairs={{0,2},{2,0},{4,6},{6,4},{1,3},{3,1},{5,7},{7,5},{8,10},{10,8},{12,... | collective-permute-start | bytes 602120 | tf_op jit(solution)/shard_map/ppermute | solution.py:339
  20.8 4.3 %collective-permute-start.1 = (bf16[784,128]{1,0:T(8,128)(2,1)}, bf16[784,128]{1,0:T(8,128)(2,1)S(1)}, u32[]{:S(2)}, u32[]{:S(2)}) collective-permute-start(bf16[784,128]{1,0:T(8,128)(2,1)} %get-tuple-element.30), channel_id=1, source_target_pairs={{0,4},{2,6},{4,0},{6,2},{1,5},{3,7},{5,1},{7,3},{8,12},{10,14},{12... | collective-permute-start | bytes 602120 | tf_op jit(solution)/shard_map/ppermute | solution.py:339
  25.1 1.9 %collective-permute-start.2 = (bf16[784,128]{1,0:T(8,128)(2,1)}, bf16[784,128]{1,0:T(8,128)(2,1)S(1)}, u32[]{:S(2)}, u32[]{:S(2)}) collective-permute-start(bf16[784,128]{1,0:T(8,128)(2,1)} %get-tuple-element.31), channel_id=1, source_target_pairs={{0,6},{2,4},{4,2},{6,0},{1,7},{3,5},{5,3},{7,1},{8,14},{10,12},{12... | collective-permute-start | bytes 602120 | tf_op jit(solution)/shard_map/ppermute | solution.py:339
  27.0 0.8 slice_bitcast_fusion.3
  27.9 0.0 all-to-all-done.pre
  27.9 0.6 copy-done.5
  28.5 1.6 %spread_prefix.1 = bf16[32,64,128]{2,1,0:T(8,128)(2,1)} custom-call(bf16[8,16,128]{2,1,0:T(8,128)(2,1)} %copy-done.5), custom_call_target="tpu_custom_call" | custom-call | flops 262144 | bytes 524288 | tf_op jit(solution)/shard_map/spread_prefix/pallas_call | solution.py:347
  30.1 7.6 %all-to-all-start.1 = ((bf16[32,64,128]{2,1,0:T(8,128)(2,1)}), bf16[32,64,128]{2,1,0:T(8,128)(2,1)S(1)}, u32[]{:S(2)}, u32[]{:S(2)}) async-start(bf16[32,64,128]{2,1,0:T(8,128)(2,1)} %spread_prefix.1), calls=%async_computation.1 | async-start | bytes 1048576 | tf_op jit(solution)/shard_map/all_to_all | solution.py:355
  37.7 0.0 collective-permute-done.2.far3
  37.8 2.2 %collective-permute-done.1.far2 = bf16[784,128]{1,0:T(8,128)(2,1)S(1)} collective-permute-done((bf16[784,128]{1,0:T(8,128)(2,1)}, bf16[784,128]{1,0:T(8,128)(2,1)S(1)}, u32[]{:S(2)}, u32[]{:S(2)}) %collective-permute-start.1) | collective-permute-done | bytes 200736 | tf_op jit(solution)/shard_map/ppermute | solution.py:339
  40.0 0.0 copy-start
  40.0 8.0 %collective-permute-start.4 = (bf16[2,256,128]{2,1,0:T(8,128)(2,1)S(1)}, bf16[2,256,128]{2,1,0:T(8,128)(2,1)S(1)}, u32[]{:S(2)}, u32[]{:S(2)}) collective-permute-start(bf16[2,256,128]{2,1,0:T(8,128)(2,1)S(1)} %pad_maximum_fusion.1), channel_id=1, source_target_pairs={{0,9},{2,11},{4,13},{6,15},{1,8},{3,10},{5,12},{7,14},{16,25},{18,... | collective-permute-start | bytes 393224 | tf_op jit(solution)/shard_map/ppermute | solution.py:346
  47.9 0.0 collective-permute-done.far1
  48.0 1.3 %collective-permute-start.3 = (bf16[2,256,128]{2,1,0:T(8,128)(2,1)S(1)}, bf16[2,256,128]{2,1,0:T(8,128)(2,1)S(1)}, u32[]{:S(2)}, u32[]{:S(2)}) collective-permute-start(bf16[2,256,128]{2,1,0:T(8,128)(2,1)S(1)} %pad_maximum_fusion), channel_id=1, source_target_pairs={{0,8},{2,10},{4,12},{6,14},{1,9},{3,11},{5,13},{7,15},{16,24},{18,... | collective-permute-start | bytes 393224 | tf_op jit(solution)/shard_map/ppermute | solution.py:345
  49.3 0.0 all-to-all-done.1.pref
  49.3 1.3 %prefix_norms.1.pre_norms = f32[8,1024]{1,0:T(8,128)S(1)} custom-call(bf16[784,128]{1,0:T(8,128)(2,1)S(1)} %copy-done, bf16[784,128]{1,0:T(8,128)(2,1)S(1)} %collective-permute-done.far1, bf16[784,128]{1,0:T(8,128)(2,1)S(1)} %collective-permute-done.1.far2, bf16[784,128]{1,0:T(8,128)(2,1)S(1)} %collective-permute-done.2.far3, ...), custom_call_target="tpu_custom_call" | custom-call | flops 8589934592 | bytes 1048576 | tf_op jit(solution)/shard_map/prefix_norms/pallas_call | solution.py:361
  50.7 8.2 %collective-permute-done.4.oth_hi = bf16[2,256,128]{2,1,0:T(8,128)(2,1)S(1)} collective-permute-done((bf16[2,256,128]{2,1,0:T(8,128)(2,1)S(1)}, bf16[2,256,128]{2,1,0:T(8,128)(2,1)S(1)}, u32[]{:S(2)}, u32[]{:S(2)}) %collective-permute-start.4) | collective-permute-done | bytes 131104 | tf_op jit(solution)/shard_map/ppermute | solution.py:346
  58.9 0.0 collective-permute-done.3.oth_lo
  58.9 4.0 %sibling_grads.1 = (bf16[4,128,128]{2,1,0:T(8,128)(2,1)S(1)}, bf16[4,128,128]{2,1,0:T(8,128)(2,1)S(1)}, bf16[4,128,128]{2,1,0:T(8,128)(2,1)S(1)}, bf16[4,128,128...) custom-call(bf16[784,128]{1,0:T(8,128)(2,1)S(1)} %copy-done, ...), custom_call_target="tpu_custom_call" | custom-call | flops 1342177280 | bytes 4194304 | tf_op jit(solution)/shard_map/sibling_grads/pallas_call | solution.py:374
  62.9 1.3 %collective-permute-start.5 = (bf16[4,128,128]{2,1,0:T(8,128)(2,1)S(1)}, bf16[4,128,128]{2,1,0:T(8,128)(2,1)S(1)}, u32[]{:S(2)}, u32[]{:S(2)}) collective-permute-start(bf16[4,128,128]{2,1,0:T(8,128)(2,1)S(1)} %get-tuple-element.36), channel_id=1, source_target_pairs={{8,1},{10,3},{12,5},{14,7},{9,0},{11,2},{13,4},{15,6},{24,17},{26,... | collective-permute-start | bytes 393224 | tf_op jit(solution)/shard_map/ppermute | solution.py:393
  64.2 1.3 %collective-permute-start.6 = (bf16[4,128,128]{2,1,0:T(8,128)(2,1)S(1)}, bf16[4,128,128]{2,1,0:T(8,128)(2,1)S(1)}, u32[]{:S(2)}, u32[]{:S(2)}) collective-permute-start(bf16[4,128,128]{2,1,0:T(8,128)(2,1)S(1)} %get-tuple-element.37), channel_id=1, source_target_pairs={{8,0},{10,2},{12,4},{14,6},{9,1},{11,3},{13,5},{15,7},{24,16},{26,... | collective-permute-start | bytes 393224 | tf_op jit(solution)/shard_map/ppermute | solution.py:394
  65.5 3.3 %prefix_grads.1 = (bf16[32,64,128]{2,1,0:T(8,128)(2,1)}, bf16[4,256,128]{2,1,0:T(8,128)(2,1)S(1)}) custom-call(bf16[784,128]{1,0:T(8,128)(2,1)S(1)} %copy-done, bf16[784,128]{1,0:T(8,128)(2,1)S(1)} %collective-permute-done.far1, bf16[784,128]{1,0:T(8,128)(2,1)S(1)} %collective-permute-done.1.far2, bf16[784,128]{1,0:T(8,128)(2,1)S(1)} %collective-permute-done.2.far3, ...), custom_call_target="tpu_custom_call" | custom-call | flops 68719476736 | bytes 4194304 | tf_op jit(solution)/shard_map/prefix_grads/pallas_call | solution.py:396
  68.8 0.7 copy-done.2
  69.5 7.6 %all-to-all-start.2 = ((bf16[32,64,128]{2,1,0:T(8,128)(2,1)}), bf16[32,64,128]{2,1,0:T(8,128)(2,1)S(1)}, u32[]{:S(2)}, u32[]{:S(2)}) async-start(bf16[32,64,128]{2,1,0:T(8,128)(2,1)} %get-tuple-element.34), calls=%async_computation.2 | async-start | bytes 1048576 | tf_op jit(solution)/shard_map/all_to_all | solution.py:413
  77.1 6.4 %collective-permute-start.7 = (bf16[4,128,128]{2,1,0:T(8,128)(2,1)S(1)}, bf16[4,128,128]{2,1,0:T(8,128)(2,1)S(1)}, u32[]{:S(2)}, u32[]{:S(2)}) collective-permute-start(bf16[4,128,128]{2,1,0:T(8,128)(2,1)S(1)} %get-tuple-element.39), channel_id=1, source_target_pairs={{0,1},{2,3},{4,5},{6,7},{8,9},{10,11},{12,13},{14,15},{1,0},{3,2},... | collective-permute-start | bytes 393224 | tf_op jit(solution)/shard_map/ppermute | solution.py:392
  83.5 0.0 collective-permute-done.5.got_plus
  83.5 0.0 collective-permute-done.6.got_minus
  83.5 0.6 copy-done.10
  84.1 0.0 copy-done.11
  84.2 1.8 %near_sums.1.near = f32[4,128,128]{2,1,0:T(8,128)} custom-call(bf16[4,128,128]{2,1,0:T(8,128)(2,1)} %copy-done.1, bf16[4,128,128]{2,1,0:T(8,128)(2,1)} %copy-done.10, bf16[4,128,128]{2,1,0:T(8,128)(2,1)} %copy-done.11), custom_call_target="tpu_custom_call" | custom-call | flops 68719476736 | bytes 1048576 | tf_op jit(solution)/shard_map/near_sums/pallas_call | solution.py:414
  85.9 1.6 %all-to-all-done.2.parts = bf16[32,64,128]{2,1,0:T(8,128)(2,1)S(1)} async-done(((bf16[32,64,128]{2,1,0:T(8,128)(2,1)}), bf16[32,64,128]{2,1,0:T(8,128)(2,1)S(1)}, u32[]{:S(2)}, u32[]{:S(2)}) %all-to-all-start.2) | async-done | bytes 524320 | tf_op jit(solution)/shard_map/all_to_all | solution.py:413
  87.6 0.8 copy-done.3
  88.4 1.8 %prefix_sums.1 = f32[16,8,128]{2,1,0:T(8,128)} custom-call(bf16[32,64,128]{2,1,0:T(8,128)(2,1)} %copy-done.3), custom_call_target="tpu_custom_call" | custom-call | flops 262144 | bytes 524288 | tf_op jit(solution)/shard_map/prefix_sums/pallas_call | solution.py:431
  90.1 11.1 %all-to-all-start.3 = ((f32[16,8,128]{2,1,0:T(8,128)}), f32[16,8,128]{2,1,0:T(8,128)S(1)}, u32[]{:S(2)}, u32[]{:S(2)}) async-start(f32[16,8,128]{2,1,0:T(8,128)} %prefix_sums.1), calls=%async_computation.3 | async-start | bytes 131072 | tf_op jit(solution)/shard_map/all_to_all | solution.py:439
  101.3 0.0 collective-permute-done.7.got8
  101.3 0.6 copy-done.9
  101.9 1.9 %merge_grads.1 = (bf16[384,128]{1,0:T(8,128)(2,1)}, bf16[384,128]{1,0:T(8,128)(2,1)}, bf16[384,128]{1,0:T(8,128)(2,1)}, bf16[384,128]{1,0:T(8,128)(2,1)}) custom-call(f32[4,128,128]{2,1,0:T(8,128)} %near_sums.1.near, bf16[4,128,128]{2,1,0:T(8,128)(2,1)} %copy-done.9, bf16[4,256,128]{2,1,0:T(8,128)(2,1)} %copy-done.2), custom_call_target="tpu_custom_call" | custom-call | flops 68719476736 | bytes 1048576 | tf_op jit(solution)/shard_map/merge_grads/pallas_call | solution.py:423
  103.8 5.6 %collective-permute-start.10 = (bf16[384,128]{1,0:T(8,128)(2,1)}, bf16[384,128]{1,0:T(8,128)(2,1)S(1)}, u32[]{:S(2)}, u32[]{:S(2)}) collective-permute-start(bf16[384,128]{1,0:T(8,128)(2,1)} %get-tuple-element.44), channel_id=1, source_target_pairs={{0,6},{2,4},{4,2},{6,0},{1,7},{3,5},{5,3},{7,1},{8,14},{10,12},{12... | collective-permute-start | bytes 294920 | tf_op jit(solution)/shard_map/ppermute | solution.py:339
  109.4 1.9 %collective-permute-start.8 = (bf16[384,128]{1,0:T(8,128)(2,1)}, bf16[384,128]{1,0:T(8,128)(2,1)S(1)}, u32[]{:S(2)}, u32[]{:S(2)}) collective-permute-start(bf16[384,128]{1,0:T(8,128)(2,1)} %get-tuple-element.42), channel_id=1, source_target_pairs={{0,2},{2,0},{4,6},{6,4},{1,3},{3,1},{5,7},{7,5},{8,10},{10,8},{12,... | collective-permute-start | bytes 294920 | tf_op jit(solution)/shard_map/ppermute | solution.py:339
  111.3 2.6 %collective-permute-start.9 = (bf16[384,128]{1,0:T(8,128)(2,1)}, bf16[384,128]{1,0:T(8,128)(2,1)S(1)}, u32[]{:S(2)}, u32[]{:S(2)}) collective-permute-start(bf16[384,128]{1,0:T(8,128)(2,1)} %get-tuple-element.43), channel_id=1, source_target_pairs={{0,4},{2,6},{4,0},{6,2},{1,5},{3,7},{5,1},{7,3},{8,12},{10,14},{12... | collective-permute-start | bytes 294920 | tf_op jit(solution)/shard_map/ppermute | solution.py:339
  113.9 2.2 %collective-permute-done.8.back1 = bf16[384,128]{1,0:T(8,128)(2,1)S(1)} collective-permute-done((bf16[384,128]{1,0:T(8,128)(2,1)}, bf16[384,128]{1,0:T(8,128)(2,1)S(1)}, u32[]{:S(2)}, u32[]{:S(2)}) %collective-permute-start.8) | collective-permute-done | bytes 98336 | tf_op jit(solution)/shard_map/ppermute | solution.py:339
  116.1 4.7 %collective-permute-done.9.back2 = bf16[384,128]{1,0:T(8,128)(2,1)S(1)} collective-permute-done((bf16[384,128]{1,0:T(8,128)(2,1)}, bf16[384,128]{1,0:T(8,128)(2,1)S(1)}, u32[]{:S(2)}, u32[]{:S(2)}) %collective-permute-start.9) | collective-permute-done | bytes 98336 | tf_op jit(solution)/shard_map/ppermute | solution.py:339
  120.9 0.6 copy-done.8
  121.5 0.0 copy-done.4
  121.5 1.8 %unpack_heads.1 = (bf16[2,128,512]{2,1,0:T(8,128)(2,1)}, bf16[64,512]{1,0:T(8,128)(2,1)}, bf16[64,512]{1,0:T(8,128)(2,1)}, bf16[2,512]{1,0:T(2,128)(2,1)}, bf16[2,512]{1,0:T(2,128)(2,1)}) custom-call(bf16[384,128]{1,0:T(8,128)(2,1)} %get-tuple-element.41.back0, bf16[384,128]{1,0:T(8,128)(2,1)} %copy-done.7, bf16[384,128]{1,0:T(8,128)(2,1)} %copy-done.8, ...), custom_call_target="tpu_custom_call" | custom-call | flops 262144 | bytes 1048576 | tf_op jit(solution)/shard_map/unpack_heads/pallas_call | solution.py:442
  (22 shorter events, 0.1 us)
Async XLA Ops:
  2.0 25.9 %all-to-all-start = ((bf16[8,16,128]{2,1,0:T(8,128)(2,1)}), bf16[8,16,128]{2,1,0:T(8,128)(2,1)S(1)}, u32[]{:S(2)}, u32[]{:S(2)}) async-start(bf16[8,16,128]{2,1,0:T(8,128)(2,1)} %pack_prefix.1.pre), calls=%async_computation | async-start | bytes 65536 | tf_op jit(solution)/shard_map/all_to_all | solution.py:342
  16.9 31.0 %collective-permute-start = (bf16[784,128]{1,0:T(8,128)(2,1)}, bf16[784,128]{1,0:T(8,128)(2,1)S(1)}, u32[]{:S(2)}, u32[]{:S(2)}) collective-permute-start(bf16[784,128]{1,0:T(8,128)(2,1)} %get-tuple-element.29), channel_id=1, source_target_pairs={{0,2},{2,0},{4,6},{6,4},{1,3},{3,1},{5,7},{7,5},{8,10},{10,8},{12,... | collective-permute-start | bytes 602120 | tf_op jit(solution)/shard_map/ppermute | solution.py:339
  20.8 19.1 %collective-permute-start.1 = (bf16[784,128]{1,0:T(8,128)(2,1)}, bf16[784,128]{1,0:T(8,128)(2,1)S(1)}, u32[]{:S(2)}, u32[]{:S(2)}) collective-permute-start(bf16[784,128]{1,0:T(8,128)(2,1)} %get-tuple-element.30), channel_id=1, source_target_pairs={{0,4},{2,6},{4,0},{6,2},{1,5},{3,7},{5,1},{7,3},{8,12},{10,14},{12... | collective-permute-start | bytes 602120 | tf_op jit(solution)/shard_map/ppermute | solution.py:339
  25.1 12.6 %collective-permute-start.2 = (bf16[784,128]{1,0:T(8,128)(2,1)}, bf16[784,128]{1,0:T(8,128)(2,1)S(1)}, u32[]{:S(2)}, u32[]{:S(2)}) collective-permute-start(bf16[784,128]{1,0:T(8,128)(2,1)} %get-tuple-element.31), channel_id=1, source_target_pairs={{0,6},{2,4},{4,2},{6,0},{1,7},{3,5},{5,3},{7,1},{8,14},{10,12},{12... | collective-permute-start | bytes 602120 | tf_op jit(solution)/shard_map/ppermute | solution.py:339
  27.9 0.6 copy-start.5
  30.1 19.2 %all-to-all-start.1 = ((bf16[32,64,128]{2,1,0:T(8,128)(2,1)}), bf16[32,64,128]{2,1,0:T(8,128)(2,1)S(1)}, u32[]{:S(2)}, u32[]{:S(2)}) async-start(bf16[32,64,128]{2,1,0:T(8,128)(2,1)} %spread_prefix.1), calls=%async_computation.1 | async-start | bytes 1048576 | tf_op jit(solution)/shard_map/all_to_all | solution.py:355
  40.0 9.3 %copy-start = (bf16[784,128]{1,0:T(8,128)(2,1)S(1)}, bf16[784,128]{1,0:T(8,128)(2,1)}, u32[]{:S(2)}) copy-start(bf16[784,128]{1,0:T(8,128)(2,1)} %get-tuple-element.28.own) | copy-start | bytes 602116
  40.0 18.9 %collective-permute-start.4 = (bf16[2,256,128]{2,1,0:T(8,128)(2,1)S(1)}, bf16[2,256,128]{2,1,0:T(8,128)(2,1)S(1)}, u32[]{:S(2)}, u32[]{:S(2)}) collective-permute-start(bf16[2,256,128]{2,1,0:T(8,128)(2,1)S(1)} %pad_maximum_fusion.1), channel_id=1, source_target_pairs={{0,9},{2,11},{4,13},{6,15},{1,8},{3,10},{5,12},{7,14},{16,25},{18,... | collective-permute-start | bytes 393224 | tf_op jit(solution)/shard_map/ppermute | solution.py:346
  48.0 10.9 %collective-permute-start.3 = (bf16[2,256,128]{2,1,0:T(8,128)(2,1)S(1)}, bf16[2,256,128]{2,1,0:T(8,128)(2,1)S(1)}, u32[]{:S(2)}, u32[]{:S(2)}) collective-permute-start(bf16[2,256,128]{2,1,0:T(8,128)(2,1)S(1)} %pad_maximum_fusion), channel_id=1, source_target_pairs={{0,8},{2,10},{4,12},{6,14},{1,9},{3,11},{5,13},{7,15},{16,24},{18,... | collective-permute-start | bytes 393224 | tf_op jit(solution)/shard_map/ppermute | solution.py:345
  62.9 5.9 %copy-start.1 = (bf16[4,128,128]{2,1,0:T(8,128)(2,1)}, bf16[4,128,128]{2,1,0:T(8,128)(2,1)S(1)}, u32[]{:S(2)}) copy-start(bf16[4,128,128]{2,1,0:T(8,128)(2,1)S(1)} %get-tuple-element.35.keep) | copy-start | bytes 393220
  62.9 20.6 %collective-permute-start.5 = (bf16[4,128,128]{2,1,0:T(8,128)(2,1)S(1)}, bf16[4,128,128]{2,1,0:T(8,128)(2,1)S(1)}, u32[]{:S(2)}, u32[]{:S(2)}) collective-permute-start(bf16[4,128,128]{2,1,0:T(8,128)(2,1)S(1)} %get-tuple-element.36), channel_id=1, source_target_pairs={{8,1},{10,3},{12,5},{14,7},{9,0},{11,2},{13,4},{15,6},{24,17},{26,... | collective-permute-start | bytes 393224 | tf_op jit(solution)/shard_map/ppermute | solution.py:393
  64.2 19.3 %collective-permute-start.6 = (bf16[4,128,128]{2,1,0:T(8,128)(2,1)S(1)}, bf16[4,128,128]{2,1,0:T(8,128)(2,1)S(1)}, u32[]{:S(2)}, u32[]{:S(2)}) collective-permute-start(bf16[4,128,128]{2,1,0:T(8,128)(2,1)S(1)} %get-tuple-element.37), channel_id=1, source_target_pairs={{8,0},{10,2},{12,4},{14,6},{9,1},{11,3},{13,5},{15,7},{24,16},{26,... | collective-permute-start | bytes 393224 | tf_op jit(solution)/shard_map/ppermute | solution.py:394
  68.8 0.7 copy-start.2
  69.5 18.1 %all-to-all-start.2 = ((bf16[32,64,128]{2,1,0:T(8,128)(2,1)}), bf16[32,64,128]{2,1,0:T(8,128)(2,1)S(1)}, u32[]{:S(2)}, u32[]{:S(2)}) async-start(bf16[32,64,128]{2,1,0:T(8,128)(2,1)} %get-tuple-element.34), calls=%async_computation.2 | async-start | bytes 1048576 | tf_op jit(solution)/shard_map/all_to_all | solution.py:413
  77.1 24.2 %collective-permute-start.7 = (bf16[4,128,128]{2,1,0:T(8,128)(2,1)S(1)}, bf16[4,128,128]{2,1,0:T(8,128)(2,1)S(1)}, u32[]{:S(2)}, u32[]{:S(2)}) collective-permute-start(bf16[4,128,128]{2,1,0:T(8,128)(2,1)S(1)} %get-tuple-element.39), channel_id=1, source_target_pairs={{0,1},{2,3},{4,5},{6,7},{8,9},{10,11},{12,13},{14,15},{1,0},{3,2},... | collective-permute-start | bytes 393224 | tf_op jit(solution)/shard_map/ppermute | solution.py:392
  83.5 0.6 copy-start.10
  83.5 0.7 copy-start.11
  87.6 0.8 copy-start.3
  90.1 30.7 %all-to-all-start.3 = ((f32[16,8,128]{2,1,0:T(8,128)}), f32[16,8,128]{2,1,0:T(8,128)S(1)}, u32[]{:S(2)}, u32[]{:S(2)}) async-start(f32[16,8,128]{2,1,0:T(8,128)} %prefix_sums.1), calls=%async_computation.3 | async-start | bytes 131072 | tf_op jit(solution)/shard_map/all_to_all | solution.py:439
  101.3 0.6 copy-start.9
  103.8 10.1 %collective-permute-start.10 = (bf16[384,128]{1,0:T(8,128)(2,1)}, bf16[384,128]{1,0:T(8,128)(2,1)S(1)}, u32[]{:S(2)}, u32[]{:S(2)}) collective-permute-start(bf16[384,128]{1,0:T(8,128)(2,1)} %get-tuple-element.44), channel_id=1, source_target_pairs={{0,6},{2,4},{4,2},{6,0},{1,7},{3,5},{5,3},{7,1},{8,14},{10,12},{12... | collective-permute-start | bytes 294920 | tf_op jit(solution)/shard_map/ppermute | solution.py:339
  109.4 6.7 %collective-permute-start.8 = (bf16[384,128]{1,0:T(8,128)(2,1)}, bf16[384,128]{1,0:T(8,128)(2,1)S(1)}, u32[]{:S(2)}, u32[]{:S(2)}) collective-permute-start(bf16[384,128]{1,0:T(8,128)(2,1)} %get-tuple-element.42), channel_id=1, source_target_pairs={{0,2},{2,0},{4,6},{6,4},{1,3},{3,1},{5,7},{7,5},{8,10},{10,8},{12,... | collective-permute-start | bytes 294920 | tf_op jit(solution)/shard_map/ppermute | solution.py:339
  111.3 9.5 %collective-permute-start.9 = (bf16[384,128]{1,0:T(8,128)(2,1)}, bf16[384,128]{1,0:T(8,128)(2,1)S(1)}, u32[]{:S(2)}, u32[]{:S(2)}) collective-permute-start(bf16[384,128]{1,0:T(8,128)(2,1)} %get-tuple-element.43), channel_id=1, source_target_pairs={{0,4},{2,6},{4,0},{6,2},{1,5},{3,7},{5,1},{7,3},{8,12},{10,14},{12... | collective-permute-start | bytes 294920 | tf_op jit(solution)/shard_map/ppermute | solution.py:339
  113.9 7.0 %copy-start.6 = (bf16[384,128]{1,0:T(8,128)(2,1)}, bf16[384,128]{1,0:T(8,128)(2,1)S(1)}, u32[]{:S(2)}) copy-start(bf16[384,128]{1,0:T(8,128)(2,1)S(1)} %collective-permute-done.10.back3) | copy-start | bytes 294916
  116.1 4.8 %copy-start.7 = (bf16[384,128]{1,0:T(8,128)(2,1)}, bf16[384,128]{1,0:T(8,128)(2,1)S(1)}, u32[]{:S(2)}) copy-start(bf16[384,128]{1,0:T(8,128)(2,1)S(1)} %collective-permute-done.8.back1) | copy-start | bytes 294916
  120.9 0.6 copy-start.8
  120.9 0.7 copy-start.4

commit v5 on v4

--- a/solution.py
+++ b/solution.py
@@ -259,22 +259,21 @@
         )
 
 
-def near_kernel(keep, got_plus, got_minus, out):
-    for slot in range(HEADS):
-        out[slot] = sum(a[slot].astype(jnp.float32) for a in (keep, got_plus, got_minus))
-
-
-def merge_kernel(near, got8, dq, out0, out1, out2, out3):
+def arrived_kernel(got_plus, got_minus, out):
+    out[...] = jnp.zeros_like(out)
+
+
+def merge_kernel(keep, got_plus, got_minus, got8, dq, out0, out1, out2, out3):
     cq = lax.axis_index("cq")
     wide = GROUPS * ROWS
     for step, out in enumerate((out0, out1, out2, out3)):
         slot = jnp.bitwise_xor(cq, step)
         out[0:wide, :] = dq[step]
-        total = near[slot] + got8[slot].astype(jnp.float32)
+        total = sum(a[slot].astype(jnp.float32) for a in (keep, got_plus, got_minus, got8))
         out[wide : wide + ROWS, :] = total.astype(jnp.bfloat16)
 
 
-def prefix_sum_kernel(parts, out):
+def prefix_sum_kernel(parts, arrived, out):
     total = jnp.sum(parts[...].astype(jnp.float32), axis=0)
     for part in range(2):
         for piece in range(2 * HEADS):
@@ -411,31 +410,33 @@
     )(*bulk, pref, norms, dq_part)
 
     parts = lax.all_to_all(pgrad, "sib", 0, 0)
-    near = pl.pallas_call(
-        near_kernel,
-        out_shape=shape((HEADS, ROWS, LANES), jnp.float32),
-        in_specs=vmem(3),
+    arrived = pl.pallas_call(
+        arrived_kernel,
+        out_shape=shape((8, LANES), jnp.float32),
+        in_specs=[pl.BlockSpec(memory_space=pl.ANY)] * 2,
         out_specs=vmem(1)[0],
-        cost_estimate=cost(MERGE_COST, 1 << 20),
-        name="near_sums",
-    )(keep, got_plus, got_minus)
-    parts, near = lax.optimization_barrier((parts, near))
+        cost_estimate=cost(MERGE_COST, 1 << 10),
+        name="arrived",
+    )(got_plus, got_minus)
+    parts, arrived, got_plus, got_minus = lax.optimization_barrier(
+        (parts, arrived, got_plus, got_minus)
+    )
     back = pl.pallas_call(
         merge_kernel,
         out_shape=(shape((wide + ROWS, LANES), bf16),) * 4,
-        in_specs=vmem(3),
+        in_specs=vmem(5),
         out_specs=tuple(vmem(4)),
         cost_estimate=cost(MERGE_COST, 1 << 20),
         name="merge_grads",
-    )(near, got8, dq)
+    )(keep, got_plus, got_minus, got8, dq)
     small = pl.pallas_call(
         prefix_sum_kernel,
         out_shape=shape((16, 8, LANES), jnp.float32),
-        in_specs=vmem(1),
+        in_specs=vmem(1) + [pl.BlockSpec(memory_space=pl.ANY)],
         out_specs=vmem(1)[0],
         cost_estimate=cost(1 << 18, 1 << 19),
         name="prefix_sums",
-    )(parts)
+    )(parts, arrived)
     small = lax.all_to_all(small, Z, 0, 0)
     back = [back[0]] + [swap(back[d], d) for d in (1, 2, 3)]
 

time: 124 us -> 122 us (0.984)
    ppermute x1, starting transfers between devices: 1.3 us -> 7.83 us  [on_device(): oth_lo = lax.ppermute(jnp.stack(pairs[0:2]), Z, ring(4, early))]
    ppermute x1, starting transfers between devices: 7.96 us -> 2.36 us  [on_device(): oth_hi = lax.ppermute(jnp.stack(pairs[2:4]), Z, ring(-4, early))]
    ppermute x6, waiting for transfers between devices: 9.14 us -> 4.69 us  [swap(): return lax.ppermute(array, 'cq', [(i, i ^ step) for i in range(HEADS)])]
    all_to_all x1, starting transfers between devices: 11.1 us -> 8.26 us  [on_device(): small = lax.all_to_all(small, Z, 0, 0)]
    ppermute x1, waiting for transfers between devices: 0.01 us -> 2.09 us  [on_device(): got8 = lax.ppermute(send8, Z, ring(8))]
    ppermute x1, waiting for transfers between devices: 8.2 us -> 9.99 us  [on_device(): oth_hi = lax.ppermute(jnp.stack(pairs[2:4]), Z, ring(-4, early))]
where the time goes in v5:
time: 122 us; the launch traced here: 121 us
  starting transfers between devices  76.1 us (62%)
  Pallas kernels  20.2 us (17%)
  waiting for transfers between devices  18.2 us (15%)
  local copies, waits for them, and re-layouts  5.56 us (5%)
    ppermute x6, starting transfers between devices, swap(): return lax.ppermute(array, 'cq', [(i, i ^ step) for i in range(HEADS)])  20.2 us
    all_to_all x1, starting transfers between devices, on_device(): pre = lax.all_to_all(pre, ('cb', 'cq'), 0, 0)  12.5 us
    ppermute x1, waiting for transfers between devices, on_device(): oth_hi = lax.ppermute(jnp.stack(pairs[2:4]), Z, ring(-4, early))  9.99 us
    all_to_all x1, starting transfers between devices, on_device(): small = lax.all_to_all(small, Z, 0, 0)  8.26 us
    ppermute x1, starting transfers between devices, on_device(): oth_lo = lax.ppermute(jnp.stack(pairs[0:2]), Z, ring(4, early))  7.83 us
    all_to_all x1, starting transfers between devices, on_device(): pref = lax.all_to_all(spread, 'sib', 0, 0)  7.62 us
    all_to_all x1, starting transfers between devices, on_device(): parts = lax.all_to_all(pgrad, 'sib', 0, 0)  7.37 us
    ppermute x1, starting transfers between devices, on_device(): got8 = lax.ppermute(send8, Z, ring(8))  7.29 us
  transfers between devices with their start and end apart: 15, of which 5 were waited for; matrix products, arithmetic and copies ran while one was open for 1% of the time, Pallas kernels for 11%

profile of v5, /device:TPU:2, one launch (start us, length us, event | category | flops | bytes accessed | tf_op | source)
XLA Modules:
  0.0 121.0 jit_solution(12746032863942852306)
XLA Ops:
  0.6 1.3 %pack_prefix.1.pre = bf16[8,16,128]{2,1,0:T(8,128)(2,1)} custom-call(bf16[4,512]{1,0:T(4,128)(2,1)} %pk.1, bf16[4,512]{1,0:T(4,128)(2,1)} %pv.1), custom_call_target="tpu_custom_call" | custom-call | flops 1024 | bytes 65536 | tf_op jit(solution)/shard_map/pack_prefix/pallas_call | solution.py:318
  2.0 12.5 %all-to-all-start = ((bf16[8,16,128]{2,1,0:T(8,128)(2,1)}), bf16[8,16,128]{2,1,0:T(8,128)(2,1)S(1)}, u32[]{:S(2)}, u32[]{:S(2)}) async-start(bf16[8,16,128]{2,1,0:T(8,128)(2,1)} %pack_prefix.1.pre), calls=%async_computation | async-start | bytes 65536 | tf_op jit(solution)/shard_map/all_to_all | solution.py:341
  14.5 2.4 %pack_heads.1 = (bf16[784,128]{1,0:T(8,128)(2,1)}, bf16[784,128]{1,0:T(8,128)(2,1)}, bf16[784,128]{1,0:T(8,128)(2,1)}, bf16[784,128]{1,0:T(8,128)(2,1)}) custom-call(s32[32]{0:T(128)} %lengths.1, bf16[2,128,512]{2,1,0:T(8,128)(2,1)} %bitcast.16, bf16[2,128,512]{2,1,0:T(8,128)(2,1)} %bitcast.17, bf16[2,128,512]{2,1,0:T(8,128)(2,1)} %bitcast.18, ...), custom_call_target="tpu_custom_call" | custom-call | flops 8589934592 | bytes 2097152 | tf_op jit(solution)/shard_map/pack_heads/pallas_call | solution.py:326
  16.9 3.9 %collective-permute-start = (bf16[784,128]{1,0:T(8,128)(2,1)}, bf16[784,128]{1,0:T(8,128)(2,1)S(1)}, u32[]{:S(2)}, u32[]{:S(2)}) collective-permute-start(bf16[784,128]{1,0:T(8,128)(2,1)} %get-tuple-element.31), channel_id=1, source_target_pairs={{0,2},{2,0},{4,6},{6,4},{1,3},{3,1},{5,7},{7,5},{8,10},{10,8},{12,... | collective-permute-start | bytes 602120 | tf_op jit(solution)/shard_map/ppermute | solution.py:338
  20.8 4.3 %collective-permute-start.1 = (bf16[784,128]{1,0:T(8,128)(2,1)}, bf16[784,128]{1,0:T(8,128)(2,1)S(1)}, u32[]{:S(2)}, u32[]{:S(2)}) collective-permute-start(bf16[784,128]{1,0:T(8,128)(2,1)} %get-tuple-element.32), channel_id=1, source_target_pairs={{0,4},{2,6},{4,0},{6,2},{1,5},{3,7},{5,1},{7,3},{8,12},{10,14},{12... | collective-permute-start | bytes 602120 | tf_op jit(solution)/shard_map/ppermute | solution.py:338
  25.1 1.9 %collective-permute-start.2 = (bf16[784,128]{1,0:T(8,128)(2,1)}, bf16[784,128]{1,0:T(8,128)(2,1)S(1)}, u32[]{:S(2)}, u32[]{:S(2)}) collective-permute-start(bf16[784,128]{1,0:T(8,128)(2,1)} %get-tuple-element.33), channel_id=1, source_target_pairs={{0,6},{2,4},{4,2},{6,0},{1,7},{3,5},{5,3},{7,1},{8,14},{10,12},{12... | collective-permute-start | bytes 602120 | tf_op jit(solution)/shard_map/ppermute | solution.py:338
  27.0 0.8 slice_bitcast_fusion.3
  27.9 0.0 all-to-all-done.pre
  27.9 0.6 copy-done.5
  28.5 1.6 %spread_prefix.1 = bf16[32,64,128]{2,1,0:T(8,128)(2,1)} custom-call(bf16[8,16,128]{2,1,0:T(8,128)(2,1)} %copy-done.5), custom_call_target="tpu_custom_call" | custom-call | flops 262144 | bytes 524288 | tf_op jit(solution)/shard_map/spread_prefix/pallas_call | solution.py:346
  30.1 7.6 %all-to-all-start.1 = ((bf16[32,64,128]{2,1,0:T(8,128)(2,1)}), bf16[32,64,128]{2,1,0:T(8,128)(2,1)S(1)}, u32[]{:S(2)}, u32[]{:S(2)}) async-start(bf16[32,64,128]{2,1,0:T(8,128)(2,1)} %spread_prefix.1), calls=%async_computation.1 | async-start | bytes 1048576 | tf_op jit(solution)/shard_map/all_to_all | solution.py:354
  37.7 0.0 collective-permute-done.far1
  37.8 7.8 %collective-permute-start.3 = (bf16[2,256,128]{2,1,0:T(8,128)(2,1)S(1)}, bf16[2,256,128]{2,1,0:T(8,128)(2,1)S(1)}, u32[]{:S(2)}, u32[]{:S(2)}) collective-permute-start(bf16[2,256,128]{2,1,0:T(8,128)(2,1)S(1)} %pad_maximum_fusion), channel_id=1, source_target_pairs={{0,8},{2,10},{4,12},{6,14},{1,9},{3,11},{5,13},{7,15},{16,24},{18,... | collective-permute-start | bytes 393224 | tf_op jit(solution)/shard_map/ppermute | solution.py:344
  45.6 0.0 collective-permute-done.1.far2
  45.6 0.0 copy-start
  45.7 0.0 collective-permute-done.2.far3
  45.7 2.4 %collective-permute-start.4 = (bf16[2,256,128]{2,1,0:T(8,128)(2,1)S(1)}, bf16[2,256,128]{2,1,0:T(8,128)(2,1)S(1)}, u32[]{:S(2)}, u32[]{:S(2)}) collective-permute-start(bf16[2,256,128]{2,1,0:T(8,128)(2,1)S(1)} %pad_maximum_fusion.1), channel_id=1, source_target_pairs={{0,9},{2,11},{4,13},{6,15},{1,8},{3,10},{5,12},{7,14},{16,25},{18,... | collective-permute-start | bytes 393224 | tf_op jit(solution)/shard_map/ppermute | solution.py:345
  48.1 0.1 all-to-all-done.1.pref
  48.2 1.3 %prefix_norms.1.pre_norms = f32[8,1024]{1,0:T(8,128)S(1)} custom-call(bf16[784,128]{1,0:T(8,128)(2,1)S(1)} %copy-done, bf16[784,128]{1,0:T(8,128)(2,1)S(1)} %collective-permute-done.far1, bf16[784,128]{1,0:T(8,128)(2,1)S(1)} %collective-permute-done.1.far2, bf16[784,128]{1,0:T(8,128)(2,1)S(1)} %collective-permute-done.2.far3, ...), custom_call_target="tpu_custom_call" | custom-call | flops 8589934592 | bytes 1048576 | tf_op jit(solution)/shard_map/prefix_norms/pallas_call | solution.py:360
  49.6 10.0 %collective-permute-done.4.oth_hi = bf16[2,256,128]{2,1,0:T(8,128)(2,1)S(1)} collective-permute-done((bf16[2,256,128]{2,1,0:T(8,128)(2,1)S(1)}, bf16[2,256,128]{2,1,0:T(8,128)(2,1)S(1)}, u32[]{:S(2)}, u32[]{:S(2)}) %collective-permute-start.4) | collective-permute-done | bytes 131104 | tf_op jit(solution)/shard_map/ppermute | solution.py:345
  59.6 4.0 %sibling_grads.1 = (bf16[4,128,128]{2,1,0:T(8,128)(2,1)S(1)}, bf16[4,128,128]{2,1,0:T(8,128)(2,1)S(1)}, bf16[4,128,128]{2,1,0:T(8,128)(2,1)S(1)}, bf16[4,128,128...) custom-call(bf16[784,128]{1,0:T(8,128)(2,1)S(1)} %copy-done, ...), custom_call_target="tpu_custom_call" | custom-call | flops 1342177280 | bytes 4194304 | tf_op jit(solution)/shard_map/sibling_grads/pallas_call | solution.py:373
  63.6 1.3 %collective-permute-start.5 = (bf16[4,128,128]{2,1,0:T(8,128)(2,1)S(1)}, bf16[4,128,128]{2,1,0:T(8,128)(2,1)S(1)}, u32[]{:S(2)}, u32[]{:S(2)}) collective-permute-start(bf16[4,128,128]{2,1,0:T(8,128)(2,1)S(1)} %get-tuple-element.38), channel_id=1, source_target_pairs={{8,1},{10,3},{12,5},{14,7},{9,0},{11,2},{13,4},{15,6},{24,17},{26,... | collective-permute-start | bytes 393224 | tf_op jit(solution)/shard_map/ppermute | solution.py:392
  64.9 1.3 %collective-permute-start.6 = (bf16[4,128,128]{2,1,0:T(8,128)(2,1)S(1)}, bf16[4,128,128]{2,1,0:T(8,128)(2,1)S(1)}, u32[]{:S(2)}, u32[]{:S(2)}) collective-permute-start(bf16[4,128,128]{2,1,0:T(8,128)(2,1)S(1)} %get-tuple-element.39), channel_id=1, source_target_pairs={{8,0},{10,2},{12,4},{14,6},{9,1},{11,3},{13,5},{15,7},{24,16},{26,... | collective-permute-start | bytes 393224 | tf_op jit(solution)/shard_map/ppermute | solution.py:393
  66.2 3.3 %prefix_grads.1 = (bf16[32,64,128]{2,1,0:T(8,128)(2,1)}, bf16[4,256,128]{2,1,0:T(8,128)(2,1)S(1)}) custom-call(bf16[784,128]{1,0:T(8,128)(2,1)S(1)} %copy-done, bf16[784,128]{1,0:T(8,128)(2,1)S(1)} %collective-permute-done.far1, bf16[784,128]{1,0:T(8,128)(2,1)S(1)} %collective-permute-done.1.far2, bf16[784,128]{1,0:T(8,128)(2,1)S(1)} %collective-permute-done.2.far3, ...), custom_call_target="tpu_custom_call" | custom-call | flops 68719476736 | bytes 4194304 | tf_op jit(solution)/shard_map/prefix_grads/pallas_call | solution.py:395
  69.5 0.7 copy-done.2
  70.2 7.4 %all-to-all-start.2 = ((bf16[32,64,128]{2,1,0:T(8,128)(2,1)}), bf16[32,64,128]{2,1,0:T(8,128)(2,1)S(1)}, u32[]{:S(2)}, u32[]{:S(2)}) async-start(bf16[32,64,128]{2,1,0:T(8,128)(2,1)} %get-tuple-element.37), calls=%async_computation.2 | async-start | bytes 1048576 | tf_op jit(solution)/shard_map/all_to_all | solution.py:412
  77.6 7.3 %collective-permute-start.7 = (bf16[4,128,128]{2,1,0:T(8,128)(2,1)S(1)}, bf16[4,128,128]{2,1,0:T(8,128)(2,1)S(1)}, u32[]{:S(2)}, u32[]{:S(2)}) collective-permute-start(bf16[4,128,128]{2,1,0:T(8,128)(2,1)S(1)} %get-tuple-element.42), channel_id=1, source_target_pairs={{0,1},{2,3},{4,5},{6,7},{8,9},{10,11},{12,13},{14,15},{1,0},{3,2},... | collective-permute-start | bytes 393224 | tf_op jit(solution)/shard_map/ppermute | solution.py:391
  84.9 0.0 collective-permute-done.5.got_plus
  84.9 0.0 collective-permute-done.6.got_minus
  84.9 0.6 copy-done.9
  85.5 0.7 copy-done.10
  86.2 0.6 arrived.1
  86.7 1.3 %all-to-all-done.2.parts = bf16[32,64,128]{2,1,0:T(8,128)(2,1)S(1)} async-done(((bf16[32,64,128]{2,1,0:T(8,128)(2,1)}), bf16[32,64,128]{2,1,0:T(8,128)(2,1)S(1)}, u32[]{:S(2)}, u32[]{:S(2)}) %all-to-all-start.2) | async-done | bytes 524320 | tf_op jit(solution)/shard_map/all_to_all | solution.py:412
  88.1 0.8 copy-done.3
  88.8 1.8 %prefix_sums.1 = f32[16,8,128]{2,1,0:T(8,128)} custom-call(bf16[32,64,128]{2,1,0:T(8,128)(2,1)} %copy-done.3, f32[8,128]{1,0:T(8,128)} %arrived.1), custom_call_target="tpu_custom_call" | custom-call | flops 262144 | bytes 524288 | tf_op jit(solution)/shard_map/prefix_sums/pallas_call | solution.py:432
  90.6 8.3 %all-to-all-start.3 = ((f32[16,8,128]{2,1,0:T(8,128)}), f32[16,8,128]{2,1,0:T(8,128)S(1)}, u32[]{:S(2)}, u32[]{:S(2)}) async-start(f32[16,8,128]{2,1,0:T(8,128)} %prefix_sums.1), calls=%async_computation.3 | async-start | bytes 131072 | tf_op jit(solution)/shard_map/all_to_all | solution.py:440
  98.9 2.1 %collective-permute-done.7.got8 = bf16[4,128,128]{2,1,0:T(8,128)(2,1)S(1)} collective-permute-done((bf16[4,128,128]{2,1,0:T(8,128)(2,1)S(1)}, bf16[4,128,128]{2,1,0:T(8,128)(2,1)S(1)}, u32[]{:S(2)}, u32[]{:S(2)}) %collective-permute-start.7) | collective-permute-done | bytes 131104 | tf_op jit(solution)/shard_map/ppermute | solution.py:391
  101.0 0.6 copy-done.11
  101.6 2.0 %merge_grads.1 = (bf16[384,128]{1,0:T(8,128)(2,1)}, bf16[384,128]{1,0:T(8,128)(2,1)}, bf16[384,128]{1,0:T(8,128)(2,1)}, bf16[384,128]{1,0:T(8,128)(2,1)}) custom-call(bf16[4,128,128]{2,1,0:T(8,128)(2,1)} %copy-done.1, bf16[4,128,128]{2,1,0:T(8,128)(2,1)} %copy-done.9, bf16[4,128,128]{2,1,0:T(8,128)(2,1)} %copy-done.10, bf16[4,128,128]{2,1,0:T(8,128)(2,1)} %copy-done.11, ...), custom_call_target="tpu_custom_call" | custom-call | flops 68719476736 | bytes 1048576 | tf_op jit(solution)/shard_map/merge_grads/pallas_call | solution.py:424
  103.6 1.9 %collective-permute-start.8 = (bf16[384,128]{1,0:T(8,128)(2,1)}, bf16[384,128]{1,0:T(8,128)(2,1)S(1)}, u32[]{:S(2)}, u32[]{:S(2)}) collective-permute-start(bf16[384,128]{1,0:T(8,128)(2,1)} %get-tuple-element.45), channel_id=1, source_target_pairs={{0,2},{2,0},{4,6},{6,4},{1,3},{3,1},{5,7},{7,5},{8,10},{10,8},{12,... | collective-permute-start | bytes 294920 | tf_op jit(solution)/shard_map/ppermute | solution.py:338
  105.5 4.1 %collective-permute-start.9 = (bf16[384,128]{1,0:T(8,128)(2,1)}, bf16[384,128]{1,0:T(8,128)(2,1)S(1)}, u32[]{:S(2)}, u32[]{:S(2)}) collective-permute-start(bf16[384,128]{1,0:T(8,128)(2,1)} %get-tuple-element.46), channel_id=1, source_target_pairs={{0,4},{2,6},{4,0},{6,2},{1,5},{3,7},{5,1},{7,3},{8,12},{10,14},{12... | collective-permute-start | bytes 294920 | tf_op jit(solution)/shard_map/ppermute | solution.py:338
  109.6 4.1 %collective-permute-start.10 = (bf16[384,128]{1,0:T(8,128)(2,1)}, bf16[384,128]{1,0:T(8,128)(2,1)S(1)}, u32[]{:S(2)}, u32[]{:S(2)}) collective-permute-start(bf16[384,128]{1,0:T(8,128)(2,1)} %get-tuple-element.47), channel_id=1, source_target_pairs={{0,6},{2,4},{4,2},{6,0},{1,7},{3,5},{5,3},{7,1},{8,14},{10,12},{12... | collective-permute-start | bytes 294920 | tf_op jit(solution)/shard_map/ppermute | solution.py:338
  113.7 0.0 collective-permute-done.8.back1
  113.7 4.7 %collective-permute-done.9.back2 = bf16[384,128]{1,0:T(8,128)(2,1)S(1)} collective-permute-done((bf16[384,128]{1,0:T(8,128)(2,1)}, bf16[384,128]{1,0:T(8,128)(2,1)S(1)}, u32[]{:S(2)}, u32[]{:S(2)}) %collective-permute-start.9) | collective-permute-done | bytes 98336 | tf_op jit(solution)/shard_map/ppermute | solution.py:338
  118.4 0.6 copy-done.7
  119.1 0.0 copy-done.8
  119.1 0.0 copy-done.4
  119.1 1.8 %unpack_heads.1 = (bf16[2,128,512]{2,1,0:T(8,128)(2,1)}, bf16[64,512]{1,0:T(8,128)(2,1)}, bf16[64,512]{1,0:T(8,128)(2,1)}, bf16[2,512]{1,0:T(2,128)(2,1)}, bf16[2,512]{1,0:T(2,128)(2,1)}) custom-call(bf16[384,128]{1,0:T(8,128)(2,1)} %get-tuple-element.44.back0, bf16[384,128]{1,0:T(8,128)(2,1)} %copy-done.6, bf16[384,128]{1,0:T(8,128)(2,1)} %copy-done.7, ...), custom_call_target="tpu_custom_call" | custom-call | flops 262144 | bytes 1048576 | tf_op jit(solution)/shard_map/unpack_heads/pallas_call | solution.py:443
  (22 shorter events, 0.1 us)
Async XLA Ops:
  2.0 25.9 %all-to-all-start = ((bf16[8,16,128]{2,1,0:T(8,128)(2,1)}), bf16[8,16,128]{2,1,0:T(8,128)(2,1)S(1)}, u32[]{:S(2)}, u32[]{:S(2)}) async-start(bf16[8,16,128]{2,1,0:T(8,128)(2,1)} %pack_prefix.1.pre), calls=%async_computation | async-start | bytes 65536 | tf_op jit(solution)/shard_map/all_to_all | solution.py:341
  16.9 20.8 %collective-permute-start = (bf16[784,128]{1,0:T(8,128)(2,1)}, bf16[784,128]{1,0:T(8,128)(2,1)S(1)}, u32[]{:S(2)}, u32[]{:S(2)}) collective-permute-start(bf16[784,128]{1,0:T(8,128)(2,1)} %get-tuple-element.31), channel_id=1, source_target_pairs={{0,2},{2,0},{4,6},{6,4},{1,3},{3,1},{5,7},{7,5},{8,10},{10,8},{12,... | collective-permute-start | bytes 602120 | tf_op jit(solution)/shard_map/ppermute | solution.py:338
  20.8 24.8 %collective-permute-start.1 = (bf16[784,128]{1,0:T(8,128)(2,1)}, bf16[784,128]{1,0:T(8,128)(2,1)S(1)}, u32[]{:S(2)}, u32[]{:S(2)}) collective-permute-start(bf16[784,128]{1,0:T(8,128)(2,1)} %get-tuple-element.32), channel_id=1, source_target_pairs={{0,4},{2,6},{4,0},{6,2},{1,5},{3,7},{5,1},{7,3},{8,12},{10,14},{12... | collective-permute-start | bytes 602120 | tf_op jit(solution)/shard_map/ppermute | solution.py:338
  25.1 20.6 %collective-permute-start.2 = (bf16[784,128]{1,0:T(8,128)(2,1)}, bf16[784,128]{1,0:T(8,128)(2,1)S(1)}, u32[]{:S(2)}, u32[]{:S(2)}) collective-permute-start(bf16[784,128]{1,0:T(8,128)(2,1)} %get-tuple-element.33), channel_id=1, source_target_pairs={{0,6},{2,4},{4,2},{6,0},{1,7},{3,5},{5,3},{7,1},{8,14},{10,12},{12... | collective-permute-start | bytes 602120 | tf_op jit(solution)/shard_map/ppermute | solution.py:338
  27.9 0.6 copy-start.5
  30.1 18.1 %all-to-all-start.1 = ((bf16[32,64,128]{2,1,0:T(8,128)(2,1)}), bf16[32,64,128]{2,1,0:T(8,128)(2,1)S(1)}, u32[]{:S(2)}, u32[]{:S(2)}) async-start(bf16[32,64,128]{2,1,0:T(8,128)(2,1)} %spread_prefix.1), calls=%async_computation.1 | async-start | bytes 1048576 | tf_op jit(solution)/shard_map/all_to_all | solution.py:354
  37.8 11.8 %collective-permute-start.3 = (bf16[2,256,128]{2,1,0:T(8,128)(2,1)S(1)}, bf16[2,256,128]{2,1,0:T(8,128)(2,1)S(1)}, u32[]{:S(2)}, u32[]{:S(2)}) collective-permute-start(bf16[2,256,128]{2,1,0:T(8,128)(2,1)S(1)} %pad_maximum_fusion), channel_id=1, source_target_pairs={{0,8},{2,10},{4,12},{6,14},{1,9},{3,11},{5,13},{7,15},{16,24},{18,... | collective-permute-start | bytes 393224 | tf_op jit(solution)/shard_map/ppermute | solution.py:344
  45.6 2.6 %copy-start = (bf16[784,128]{1,0:T(8,128)(2,1)S(1)}, bf16[784,128]{1,0:T(8,128)(2,1)}, u32[]{:S(2)}) copy-start(bf16[784,128]{1,0:T(8,128)(2,1)} %get-tuple-element.30.own) | copy-start | bytes 602116
  45.7 13.9 %collective-permute-start.4 = (bf16[2,256,128]{2,1,0:T(8,128)(2,1)S(1)}, bf16[2,256,128]{2,1,0:T(8,128)(2,1)S(1)}, u32[]{:S(2)}, u32[]{:S(2)}) collective-permute-start(bf16[2,256,128]{2,1,0:T(8,128)(2,1)S(1)} %pad_maximum_fusion.1), channel_id=1, source_target_pairs={{0,9},{2,11},{4,13},{6,15},{1,8},{3,10},{5,12},{7,14},{16,25},{18,... | collective-permute-start | bytes 393224 | tf_op jit(solution)/shard_map/ppermute | solution.py:345
  63.6 5.9 %copy-start.1 = (bf16[4,128,128]{2,1,0:T(8,128)(2,1)}, bf16[4,128,128]{2,1,0:T(8,128)(2,1)S(1)}, u32[]{:S(2)}) copy-start(bf16[4,128,128]{2,1,0:T(8,128)(2,1)S(1)} %get-tuple-element.34.keep) | copy-start | bytes 393220
  63.6 21.3 %collective-permute-start.5 = (bf16[4,128,128]{2,1,0:T(8,128)(2,1)S(1)}, bf16[4,128,128]{2,1,0:T(8,128)(2,1)S(1)}, u32[]{:S(2)}, u32[]{:S(2)}) collective-permute-start(bf16[4,128,128]{2,1,0:T(8,128)(2,1)S(1)} %get-tuple-element.38), channel_id=1, source_target_pairs={{8,1},{10,3},{12,5},{14,7},{9,0},{11,2},{13,4},{15,6},{24,17},{26,... | collective-permute-start | bytes 393224 | tf_op jit(solution)/shard_map/ppermute | solution.py:392
  64.9 20.0 %collective-permute-start.6 = (bf16[4,128,128]{2,1,0:T(8,128)(2,1)S(1)}, bf16[4,128,128]{2,1,0:T(8,128)(2,1)S(1)}, u32[]{:S(2)}, u32[]{:S(2)}) collective-permute-start(bf16[4,128,128]{2,1,0:T(8,128)(2,1)S(1)} %get-tuple-element.39), channel_id=1, source_target_pairs={{8,0},{10,2},{12,4},{14,6},{9,1},{11,3},{13,5},{15,7},{24,16},{26,... | collective-permute-start | bytes 393224 | tf_op jit(solution)/shard_map/ppermute | solution.py:393
  69.5 0.7 copy-start.2
  70.2 17.9 %all-to-all-start.2 = ((bf16[32,64,128]{2,1,0:T(8,128)(2,1)}), bf16[32,64,128]{2,1,0:T(8,128)(2,1)S(1)}, u32[]{:S(2)}, u32[]{:S(2)}) async-start(bf16[32,64,128]{2,1,0:T(8,128)(2,1)} %get-tuple-element.37), calls=%async_computation.2 | async-start | bytes 1048576 | tf_op jit(solution)/shard_map/all_to_all | solution.py:412
  77.6 23.4 %collective-permute-start.7 = (bf16[4,128,128]{2,1,0:T(8,128)(2,1)S(1)}, bf16[4,128,128]{2,1,0:T(8,128)(2,1)S(1)}, u32[]{:S(2)}, u32[]{:S(2)}) collective-permute-start(bf16[4,128,128]{2,1,0:T(8,128)(2,1)S(1)} %get-tuple-element.42), channel_id=1, source_target_pairs={{0,1},{2,3},{4,5},{6,7},{8,9},{10,11},{12,13},{14,15},{1,0},{3,2},... | collective-permute-start | bytes 393224 | tf_op jit(solution)/shard_map/ppermute | solution.py:391
  84.9 0.6 copy-start.9
  85.5 0.7 copy-start.10
  88.0 0.8 copy-start.3
  90.6 27.8 %all-to-all-start.3 = ((f32[16,8,128]{2,1,0:T(8,128)}), f32[16,8,128]{2,1,0:T(8,128)S(1)}, u32[]{:S(2)}, u32[]{:S(2)}) async-start(f32[16,8,128]{2,1,0:T(8,128)} %prefix_sums.1), calls=%async_computation.3 | async-start | bytes 131072 | tf_op jit(solution)/shard_map/all_to_all | solution.py:440
  101.0 0.6 copy-start.11
  103.6 10.1 %collective-permute-start.8 = (bf16[384,128]{1,0:T(8,128)(2,1)}, bf16[384,128]{1,0:T(8,128)(2,1)S(1)}, u32[]{:S(2)}, u32[]{:S(2)}) collective-permute-start(bf16[384,128]{1,0:T(8,128)(2,1)} %get-tuple-element.45), channel_id=1, source_target_pairs={{0,2},{2,0},{4,6},{6,4},{1,3},{3,1},{5,7},{7,5},{8,10},{10,8},{12,... | collective-permute-start | bytes 294920 | tf_op jit(solution)/shard_map/ppermute | solution.py:338
  105.5 12.9 %collective-permute-start.9 = (bf16[384,128]{1,0:T(8,128)(2,1)}, bf16[384,128]{1,0:T(8,128)(2,1)S(1)}, u32[]{:S(2)}, u32[]{:S(2)}) collective-permute-start(bf16[384,128]{1,0:T(8,128)(2,1)} %get-tuple-element.46), channel_id=1, source_target_pairs={{0,4},{2,6},{4,0},{6,2},{1,5},{3,7},{5,1},{7,3},{8,12},{10,14},{12... | collective-permute-start | bytes 294920 | tf_op jit(solution)/shard_map/ppermute | solution.py:338
  109.6 8.8 %collective-permute-start.10 = (bf16[384,128]{1,0:T(8,128)(2,1)}, bf16[384,128]{1,0:T(8,128)(2,1)S(1)}, u32[]{:S(2)}, u32[]{:S(2)}) collective-permute-start(bf16[384,128]{1,0:T(8,128)(2,1)} %get-tuple-element.47), channel_id=1, source_target_pairs={{0,6},{2,4},{4,2},{6,0},{1,7},{3,5},{5,3},{7,1},{8,14},{10,12},{12... | collective-permute-start | bytes 294920 | tf_op jit(solution)/shard_map/ppermute | solution.py:338
  113.7 4.7 %copy-start.6 = (bf16[384,128]{1,0:T(8,128)(2,1)}, bf16[384,128]{1,0:T(8,128)(2,1)S(1)}, u32[]{:S(2)}) copy-start(bf16[384,128]{1,0:T(8,128)(2,1)S(1)} %collective-permute-done.8.back1) | copy-start | bytes 294916
  118.4 0.6 copy-start.7
  118.4 0.7 copy-start.8
  118.4 0.7 copy-start.4

commit v6 on v5

--- a/solution.py
+++ b/solution.py
@@ -224,7 +224,7 @@
 
 def prefix_kernel(
     chunk, own, far1, far2, far3, pref, norms, dq_part,
-    pgrad, dq,
+    pgrad, msg0, msg1, msg2, msg3,
     keys, values, keys_t, dk_acc, dv_acc,
 ):
     scale = 1.0 / math.sqrt(LANES)
@@ -246,8 +246,8 @@
         dk_acc[rows, :] = dot_nn(ds, queries)
         dq_t = dq_t + dot_nn(keys_t[:, rows], ds)
     total = (dq_t.T * scale).astype(jnp.bfloat16)
-    for step in range(HEADS):
-        dq[step, :, :] = total[step * GROUPS * ROWS : (step + 1) * GROUPS * ROWS]
+    for step, msg in enumerate((msg0, msg1, msg2, msg3)):
+        msg[0 : GROUPS * ROWS, :] = total[step * GROUPS * ROWS : (step + 1) * GROUPS * ROWS]
 
     for part in range(2):
         rows = slice(part * pre // 2, (part + 1) * pre // 2)
@@ -263,14 +263,12 @@
     out[...] = jnp.zeros_like(out)
 
 
-def merge_kernel(keep, got_plus, got_minus, got8, dq, out0, out1, out2, out3):
+def merge_kernel(keep, got_plus, got_minus, got8, m0, m1, m2, m3, out0, out1, out2, out3):
     cq = lax.axis_index("cq")
-    wide = GROUPS * ROWS
     for step, out in enumerate((out0, out1, out2, out3)):
         slot = jnp.bitwise_xor(cq, step)
-        out[0:wide, :] = dq[step]
         total = sum(a[slot].astype(jnp.float32) for a in (keep, got_plus, got_minus, got8))
-        out[wide : wide + ROWS, :] = total.astype(jnp.bfloat16)
+        out[...] = total.astype(jnp.bfloat16)
 
 
 def prefix_sum_kernel(parts, arrived, out):
@@ -392,11 +390,11 @@
     got_plus = lax.ppermute(plus, Z, ring(4, late))
     got_minus = lax.ppermute(minus, Z, ring(-4, late))
 
-    pgrad, dq = pl.pallas_call(
+    pgrad, *msgs = pl.pallas_call(
         functools.partial(prefix_kernel, min(512, n_sib * 32)),
-        out_shape=(shape((n_sib, 64, LANES), bf16), shape((HEADS, wide, LANES), bf16)),
+        out_shape=(shape((n_sib, 64, LANES), bf16),) + (shape((wide + ROWS, LANES), bf16),) * 4,
         in_specs=vmem(7),
-        out_specs=tuple(vmem(2)),
+        out_specs=tuple(vmem(5)),
         scratch_shapes=[
             pltpu.VMEM((pre_rows, LANES), bf16),
             pltpu.VMEM((pre_rows, LANES), bf16),
@@ -424,11 +422,14 @@
     back = pl.pallas_call(
         merge_kernel,
         out_shape=(shape((wide + ROWS, LANES), bf16),) * 4,
-        in_specs=vmem(5),
-        out_specs=tuple(vmem(4)),
+        grid=(1,),
+        in_specs=[pl.BlockSpec((HEADS, ROWS, LANES), lambda i: (0, 0, 0))] * 4
+        + [pl.BlockSpec(memory_space=pl.ANY)] * 4,
+        out_specs=(pl.BlockSpec((ROWS, LANES), lambda i: (wide // ROWS, 0)),) * 4,
+        input_output_aliases={4: 0, 5: 1, 6: 2, 7: 3},
         cost_estimate=cost(MERGE_COST, 1 << 20),
         name="merge_grads",
-    )(keep, got_plus, got_minus, got8, dq)
+    )(keep, got_plus, got_minus, got8, *msgs)
     small = pl.pallas_call(
         prefix_sum_kernel,
         out_shape=shape((16, 8, LANES), jnp.float32),

time: 122 us -> 124 us (1.016)
  local copies, waits for them, and re-layouts: 5.56 us -> 7.46 us
    unnamed x24 -> x30, local copies, waits for them, and re-layouts: 4.69 us -> 6.6 us
  transfers between devices with their start and end apart: 15 -> 15, of which waited for: 5 -> 5; matrix products, arithmetic and copies ran while one was open for 1% -> 1% of each run, Pallas kernels for 11% -> 10%
where the time goes in v6:
time: 124 us; the launch traced here: 123 us
  starting transfers between devices  76.1 us (61%)
  Pallas kernels  20 us (16%)
  waiting for transfers between devices  18.2 us (15%)
  local copies, waits for them, and re-layouts  7.46 us (6%)
    ppermute x6, starting transfers between devices, swap(): return lax.ppermute(array, 'cq', [(i, i ^ step) for i in range(HEADS)])  20.2 us
    all_to_all x1, starting transfers between devices, on_device(): pre = lax.all_to_all(pre, ('cb', 'cq'), 0, 0)  12.5 us
    ppermute x1, waiting for transfers between devices, on_device(): oth_hi = lax.ppermute(jnp.stack(pairs[2:4]), Z, ring(-4, early))  9.99 us
    all_to_all x1, starting transfers between devices, on_device(): small = lax.all_to_all(small, Z, 0, 0)  8.27 us
    ppermute x1, starting transfers between devices, on_device(): oth_lo = lax.ppermute(jnp.stack(pairs[0:2]), Z, ring(4, early))  7.83 us
    all_to_all x1, starting transfers between devices, on_device(): pref = lax.all_to_all(spread, 'sib', 0, 0)  7.62 us
    all_to_all x1, starting transfers between devices, on_device(): parts = lax.all_to_all(pgrad, 'sib', 0, 0)  7.38 us
    ppermute x1, starting transfers between devices, on_device(): got8 = lax.ppermute(send8, Z, ring(8))  7.3 us
  transfers between devices with their start and end apart: 15, of which 5 were waited for; matrix products, arithmetic and copies ran while one was open for 1% of the time, Pallas kernels for 10%

profile of v6, /device:TPU:2, one launch (start us, length us, event | category | flops | bytes accessed | tf_op | source)
XLA Modules:
  0.0 122.7 jit_solution(4251436955529319717)
XLA Ops:
  0.6 1.3 %pack_prefix.1.pre = bf16[8,16,128]{2,1,0:T(8,128)(2,1)} custom-call(bf16[4,512]{1,0:T(4,128)(2,1)} %pk.1, bf16[4,512]{1,0:T(4,128)(2,1)} %pv.1), custom_call_target="tpu_custom_call" | custom-call | flops 1024 | bytes 65536 | tf_op jit(solution)/shard_map/pack_prefix/pallas_call | solution.py:316
  2.0 12.5 %all-to-all-start = ((bf16[8,16,128]{2,1,0:T(8,128)(2,1)}), bf16[8,16,128]{2,1,0:T(8,128)(2,1)S(1)}, u32[]{:S(2)}, u32[]{:S(2)}) async-start(bf16[8,16,128]{2,1,0:T(8,128)(2,1)} %pack_prefix.1.pre), calls=%async_computation | async-start | bytes 65536 | tf_op jit(solution)/shard_map/all_to_all | solution.py:339
  14.5 2.4 %pack_heads.1 = (bf16[784,128]{1,0:T(8,128)(2,1)}, bf16[784,128]{1,0:T(8,128)(2,1)}, bf16[784,128]{1,0:T(8,128)(2,1)}, bf16[784,128]{1,0:T(8,128)(2,1)}) custom-call(s32[32]{0:T(128)} %lengths.1, bf16[2,128,512]{2,1,0:T(8,128)(2,1)} %bitcast.16, bf16[2,128,512]{2,1,0:T(8,128)(2,1)} %bitcast.17, bf16[2,128,512]{2,1,0:T(8,128)(2,1)} %bitcast.18, ...), custom_call_target="tpu_custom_call" | custom-call | flops 8589934592 | bytes 2097152 | tf_op jit(solution)/shard_map/pack_heads/pallas_call | solution.py:324
  16.9 3.9 %collective-permute-start = (bf16[784,128]{1,0:T(8,128)(2,1)}, bf16[784,128]{1,0:T(8,128)(2,1)S(1)}, u32[]{:S(2)}, u32[]{:S(2)}) collective-permute-start(bf16[784,128]{1,0:T(8,128)(2,1)} %get-tuple-element.34), channel_id=1, source_target_pairs={{0,2},{2,0},{4,6},{6,4},{1,3},{3,1},{5,7},{7,5},{8,10},{10,8},{12,... | collective-permute-start | bytes 602120 | tf_op jit(solution)/shard_map/ppermute | solution.py:336
  20.8 4.3 %collective-permute-start.1 = (bf16[784,128]{1,0:T(8,128)(2,1)}, bf16[784,128]{1,0:T(8,128)(2,1)S(1)}, u32[]{:S(2)}, u32[]{:S(2)}) collective-permute-start(bf16[784,128]{1,0:T(8,128)(2,1)} %get-tuple-element.35), channel_id=1, source_target_pairs={{0,4},{2,6},{4,0},{6,2},{1,5},{3,7},{5,1},{7,3},{8,12},{10,14},{12... | collective-permute-start | bytes 602120 | tf_op jit(solution)/shard_map/ppermute | solution.py:336
  25.1 1.9 %collective-permute-start.2 = (bf16[784,128]{1,0:T(8,128)(2,1)}, bf16[784,128]{1,0:T(8,128)(2,1)S(1)}, u32[]{:S(2)}, u32[]{:S(2)}) collective-permute-start(bf16[784,128]{1,0:T(8,128)(2,1)} %get-tuple-element.36), channel_id=1, source_target_pairs={{0,6},{2,4},{4,2},{6,0},{1,7},{3,5},{5,3},{7,1},{8,14},{10,12},{12... | collective-permute-start | bytes 602120 | tf_op jit(solution)/shard_map/ppermute | solution.py:336
  27.0 0.8 slice_bitcast_fusion.3
  27.9 0.0 all-to-all-done.pre
  27.9 0.6 copy-done.8
  28.5 1.6 %spread_prefix.1 = bf16[32,64,128]{2,1,0:T(8,128)(2,1)} custom-call(bf16[8,16,128]{2,1,0:T(8,128)(2,1)} %copy-done.8), custom_call_target="tpu_custom_call" | custom-call | flops 262144 | bytes 524288 | tf_op jit(solution)/shard_map/spread_prefix/pallas_call | solution.py:344
  30.1 7.6 %all-to-all-start.1 = ((bf16[32,64,128]{2,1,0:T(8,128)(2,1)}), bf16[32,64,128]{2,1,0:T(8,128)(2,1)S(1)}, u32[]{:S(2)}, u32[]{:S(2)}) async-start(bf16[32,64,128]{2,1,0:T(8,128)(2,1)} %spread_prefix.1), calls=%async_computation.1 | async-start | bytes 1048576 | tf_op jit(solution)/shard_map/all_to_all | solution.py:352
  37.8 0.0 collective-permute-done.far1
  37.8 7.8 %collective-permute-start.3 = (bf16[2,256,128]{2,1,0:T(8,128)(2,1)S(1)}, bf16[2,256,128]{2,1,0:T(8,128)(2,1)S(1)}, u32[]{:S(2)}, u32[]{:S(2)}) collective-permute-start(bf16[2,256,128]{2,1,0:T(8,128)(2,1)S(1)} %pad_maximum_fusion), channel_id=1, source_target_pairs={{0,8},{2,10},{4,12},{6,14},{1,9},{3,11},{5,13},{7,15},{16,24},{18,... | collective-permute-start | bytes 393224 | tf_op jit(solution)/shard_map/ppermute | solution.py:342
  45.7 0.0 copy-start.1
  45.7 0.0 collective-permute-done.2.far3
  45.7 2.4 %collective-permute-start.4 = (bf16[2,256,128]{2,1,0:T(8,128)(2,1)S(1)}, bf16[2,256,128]{2,1,0:T(8,128)(2,1)S(1)}, u32[]{:S(2)}, u32[]{:S(2)}) collective-permute-start(bf16[2,256,128]{2,1,0:T(8,128)(2,1)S(1)} %pad_maximum_fusion.1), channel_id=1, source_target_pairs={{0,9},{2,11},{4,13},{6,15},{1,8},{3,10},{5,12},{7,14},{16,25},{18,... | collective-permute-start | bytes 393224 | tf_op jit(solution)/shard_map/ppermute | solution.py:343
  48.1 0.1 all-to-all-done.1.pref
  48.3 1.3 %prefix_norms.1.pre_norms = f32[8,1024]{1,0:T(8,128)S(1)} custom-call(bf16[784,128]{1,0:T(8,128)(2,1)S(1)} %copy-done.1, bf16[784,128]{1,0:T(8,128)(2,1)S(1)} %collective-permute-done.far1, bf16[784,128]{1,0:T(8,128)(2,1)S(1)} %collective-permute-done.1.far2, bf16[784,128]{1,0:T(8,128)(2,1)S(1)} %collective-permute-done.2.far3, ...), custom_call_target="tpu_custom_call" | custom-call | flops 8589934592 | bytes 1048576 | tf_op jit(solution)/shard_map/prefix_norms/pallas_call | solution.py:358
  49.6 10.0 %collective-permute-done.4.oth_hi = bf16[2,256,128]{2,1,0:T(8,128)(2,1)S(1)} collective-permute-done((bf16[2,256,128]{2,1,0:T(8,128)(2,1)S(1)}, bf16[2,256,128]{2,1,0:T(8,128)(2,1)S(1)}, u32[]{:S(2)}, u32[]{:S(2)}) %collective-permute-start.4) | collective-permute-done | bytes 131104 | tf_op jit(solution)/shard_map/ppermute | solution.py:343
  59.6 4.0 %sibling_grads.1 = (bf16[4,128,128]{2,1,0:T(8,128)(2,1)S(1)}, bf16[4,128,128]{2,1,0:T(8,128)(2,1)S(1)}, bf16[4,128,128]{2,1,0:T(8,128)(2,1)S(1)}, bf16[4,128,128...) custom-call(bf16[784,128]{1,0:T(8,128)(2,1)S(1)} %copy-done.1, ...), custom_call_target="tpu_custom_call" | custom-call | flops 1342177280 | bytes 4194304 | tf_op jit(solution)/shard_map/sibling_grads/pallas_call | solution.py:371
  63.6 0.0 copy-start.5
  63.6 1.3 %collective-permute-start.5 = (bf16[4,128,128]{2,1,0:T(8,128)(2,1)S(1)}, bf16[4,128,128]{2,1,0:T(8,128)(2,1)S(1)}, u32[]{:S(2)}, u32[]{:S(2)}) collective-permute-start(bf16[4,128,128]{2,1,0:T(8,128)(2,1)S(1)} %get-tuple-element.41), channel_id=1, source_target_pairs={{8,1},{10,3},{12,5},{14,7},{9,0},{11,2},{13,4},{15,6},{24,17},{26,... | collective-permute-start | bytes 393224 | tf_op jit(solution)/shard_map/ppermute | solution.py:390
  64.9 1.3 %collective-permute-start.6 = (bf16[4,128,128]{2,1,0:T(8,128)(2,1)S(1)}, bf16[4,128,128]{2,1,0:T(8,128)(2,1)S(1)}, u32[]{:S(2)}, u32[]{:S(2)}) collective-permute-start(bf16[4,128,128]{2,1,0:T(8,128)(2,1)S(1)} %get-tuple-element.42), channel_id=1, source_target_pairs={{8,0},{10,2},{12,4},{14,6},{9,1},{11,3},{13,5},{15,7},{24,16},{26,... | collective-permute-start | bytes 393224 | tf_op jit(solution)/shard_map/ppermute | solution.py:391
  66.2 3.3 %prefix_grads.1 = (bf16[32,64,128]{2,1,0:T(8,128)(2,1)}, bf16[384,128]{1,0:T(8,128)(2,1)S(1)}, bf16[384,128]{1,0:T(8,128)(2,1)S(1)}, bf16[384,128]{1,0:T(8,128)(2,1)S(1)}, bf16[384,128]{1,0:T(8,128)(2,1)S(1)}) custom-call(bf16[784,128]{1,0:T(8,128)(2,1)S(1)} %copy-done.1, bf16[784,128]{1,0:T(8,128)(2,1)S(1)} %collective-permute-done.far1, ...), custom_call_target="tpu_custom_call" | custom-call | flops 68719476736 | bytes 4194304 | tf_op jit(solution)/shard_map/prefix_grads/pallas_call | solution.py:393
  69.5 0.6 copy-done
  70.1 0.6 copy-done.2
  70.8 0.6 copy-done.3
  71.4 0.6 copy-done.4
  72.1 7.4 %all-to-all-start.2 = ((bf16[32,64,128]{2,1,0:T(8,128)(2,1)}), bf16[32,64,128]{2,1,0:T(8,128)(2,1)S(1)}, u32[]{:S(2)}, u32[]{:S(2)}) async-start(bf16[32,64,128]{2,1,0:T(8,128)(2,1)} %get-tuple-element.40), calls=%async_computation.2 | async-start | bytes 1048576 | tf_op jit(solution)/shard_map/all_to_all | solution.py:410
  79.4 7.3 %collective-permute-start.7 = (bf16[4,128,128]{2,1,0:T(8,128)(2,1)S(1)}, bf16[4,128,128]{2,1,0:T(8,128)(2,1)S(1)}, u32[]{:S(2)}, u32[]{:S(2)}) collective-permute-start(bf16[4,128,128]{2,1,0:T(8,128)(2,1)S(1)} %get-tuple-element.45), channel_id=1, source_target_pairs={{0,1},{2,3},{4,5},{6,7},{8,9},{10,11},{12,13},{14,15},{1,0},{3,2},... | collective-permute-start | bytes 393224 | tf_op jit(solution)/shard_map/ppermute | solution.py:389
  86.8 0.6 copy-done.12
  87.4 0.6 copy-done.13
  88.1 0.6 arrived.1
  88.7 1.3 %all-to-all-done.2.parts = bf16[32,64,128]{2,1,0:T(8,128)(2,1)S(1)} async-done(((bf16[32,64,128]{2,1,0:T(8,128)(2,1)}), bf16[32,64,128]{2,1,0:T(8,128)(2,1)S(1)}, u32[]{:S(2)}, u32[]{:S(2)}) %all-to-all-start.2) | async-done | bytes 524320 | tf_op jit(solution)/shard_map/all_to_all | solution.py:410
  89.9 0.8 copy-done.6
  90.7 1.8 %prefix_sums.1 = f32[16,8,128]{2,1,0:T(8,128)} custom-call(bf16[32,64,128]{2,1,0:T(8,128)(2,1)} %copy-done.6, f32[8,128]{1,0:T(8,128)} %arrived.1), custom_call_target="tpu_custom_call" | custom-call | flops 262144 | bytes 524288 | tf_op jit(solution)/shard_map/prefix_sums/pallas_call | solution.py:433
  92.5 8.3 %all-to-all-start.3 = ((f32[16,8,128]{2,1,0:T(8,128)}), f32[16,8,128]{2,1,0:T(8,128)S(1)}, u32[]{:S(2)}, u32[]{:S(2)}) async-start(f32[16,8,128]{2,1,0:T(8,128)} %prefix_sums.1), calls=%async_computation.3 | async-start | bytes 131072 | tf_op jit(solution)/shard_map/all_to_all | solution.py:441
  100.8 2.0 %collective-permute-done.7.got8 = bf16[4,128,128]{2,1,0:T(8,128)(2,1)S(1)} collective-permute-done((bf16[4,128,128]{2,1,0:T(8,128)(2,1)S(1)}, bf16[4,128,128]{2,1,0:T(8,128)(2,1)S(1)}, u32[]{:S(2)}, u32[]{:S(2)}) %collective-permute-start.7) | collective-permute-done | bytes 131104 | tf_op jit(solution)/shard_map/ppermute | solution.py:389
  102.8 0.6 copy-done.14
  103.5 1.8 %merge_grads.1 = (bf16[384,128]{1,0:T(8,128)(2,1)}, bf16[384,128]{1,0:T(8,128)(2,1)}, bf16[384,128]{1,0:T(8,128)(2,1)}, bf16[384,128]{1,0:T(8,128)(2,1)}) custom-call(bf16[4,128,128]{2,1,0:T(8,128)(2,1)} %copy-done.5, bf16[4,128,128]{2,1,0:T(8,128)(2,1)} %copy-done.12, ...), custom_call_target="tpu_custom_call", output_to_operand_aliasing={{0}: (4, {}), {1}: (5, {}), {2}: (6, {}), {3}: (7, {})} | custom-call | flops 68719476736 | bytes 1048576 | tf_op jit(solution)/shard_map/merge_grads/pallas_call | solution.py:422
  105.3 1.9 %collective-permute-start.8 = (bf16[384,128]{1,0:T(8,128)(2,1)}, bf16[384,128]{1,0:T(8,128)(2,1)S(1)}, u32[]{:S(2)}, u32[]{:S(2)}) collective-permute-start(bf16[384,128]{1,0:T(8,128)(2,1)} %get-tuple-element.51), channel_id=1, source_target_pairs={{0,2},{2,0},{4,6},{6,4},{1,3},{3,1},{5,7},{7,5},{8,10},{10,8},{12,... | collective-permute-start | bytes 294920 | tf_op jit(solution)/shard_map/ppermute | solution.py:336
  107.2 4.1 %collective-permute-start.9 = (bf16[384,128]{1,0:T(8,128)(2,1)}, bf16[384,128]{1,0:T(8,128)(2,1)S(1)}, u32[]{:S(2)}, u32[]{:S(2)}) collective-permute-start(bf16[384,128]{1,0:T(8,128)(2,1)} %get-tuple-element.52), channel_id=1, source_target_pairs={{0,4},{2,6},{4,0},{6,2},{1,5},{3,7},{5,1},{7,3},{8,12},{10,14},{12... | collective-permute-start | bytes 294920 | tf_op jit(solution)/shard_map/ppermute | solution.py:336
  111.3 4.0 %collective-permute-start.10 = (bf16[384,128]{1,0:T(8,128)(2,1)}, bf16[384,128]{1,0:T(8,128)(2,1)S(1)}, u32[]{:S(2)}, u32[]{:S(2)}) collective-permute-start(bf16[384,128]{1,0:T(8,128)(2,1)} %get-tuple-element.53), channel_id=1, source_target_pairs={{0,6},{2,4},{4,2},{6,0},{1,7},{3,5},{5,3},{7,1},{8,14},{10,12},{12... | collective-permute-start | bytes 294920 | tf_op jit(solution)/shard_map/ppermute | solution.py:336
  115.4 4.7 %collective-permute-done.9.back2 = bf16[384,128]{1,0:T(8,128)(2,1)S(1)} collective-permute-done((bf16[384,128]{1,0:T(8,128)(2,1)}, bf16[384,128]{1,0:T(8,128)(2,1)S(1)}, u32[]{:S(2)}, u32[]{:S(2)}) %collective-permute-start.9) | collective-permute-done | bytes 98336 | tf_op jit(solution)/shard_map/ppermute | solution.py:336
  120.1 0.6 copy-done.10
  120.7 0.1 copy-done.11
  120.8 0.0 copy-done.7
  120.8 1.8 %unpack_heads.1 = (bf16[2,128,512]{2,1,0:T(8,128)(2,1)}, bf16[64,512]{1,0:T(8,128)(2,1)}, bf16[64,512]{1,0:T(8,128)(2,1)}, bf16[2,512]{1,0:T(2,128)(2,1)}, bf16[2,512]{1,0:T(2,128)(2,1)}) custom-call(bf16[384,128]{1,0:T(8,128)(2,1)} %get-tuple-element.50.back0, bf16[384,128]{1,0:T(8,128)(2,1)} %copy-done.9, bf16[384,128]{1,0:T(8,128)(2,1)} %copy-done.10, ...), custom_call_target="tpu_custom_call" | custom-call | flops 262144 | bytes 1048576 | tf_op jit(solution)/shard_map/unpack_heads/pallas_call | solution.py:444
  (28 shorter events, 0.1 us)
Async XLA Ops:
  2.0 25.9 %all-to-all-start = ((bf16[8,16,128]{2,1,0:T(8,128)(2,1)}), bf16[8,16,128]{2,1,0:T(8,128)(2,1)S(1)}, u32[]{:S(2)}, u32[]{:S(2)}) async-start(bf16[8,16,128]{2,1,0:T(8,128)(2,1)} %pack_prefix.1.pre), calls=%async_computation | async-start | bytes 65536 | tf_op jit(solution)/shard_map/all_to_all | solution.py:339
  16.9 20.8 %collective-permute-start = (bf16[784,128]{1,0:T(8,128)(2,1)}, bf16[784,128]{1,0:T(8,128)(2,1)S(1)}, u32[]{:S(2)}, u32[]{:S(2)}) collective-permute-start(bf16[784,128]{1,0:T(8,128)(2,1)} %get-tuple-element.34), channel_id=1, source_target_pairs={{0,2},{2,0},{4,6},{6,4},{1,3},{3,1},{5,7},{7,5},{8,10},{10,8},{12,... | collective-permute-start | bytes 602120 | tf_op jit(solution)/shard_map/ppermute | solution.py:336
  20.8 24.8 %collective-permute-start.1 = (bf16[784,128]{1,0:T(8,128)(2,1)}, bf16[784,128]{1,0:T(8,128)(2,1)S(1)}, u32[]{:S(2)}, u32[]{:S(2)}) collective-permute-start(bf16[784,128]{1,0:T(8,128)(2,1)} %get-tuple-element.35), channel_id=1, source_target_pairs={{0,4},{2,6},{4,0},{6,2},{1,5},{3,7},{5,1},{7,3},{8,12},{10,14},{12... | collective-permute-start | bytes 602120 | tf_op jit(solution)/shard_map/ppermute | solution.py:336
  25.1 20.6 %collective-permute-start.2 = (bf16[784,128]{1,0:T(8,128)(2,1)}, bf16[784,128]{1,0:T(8,128)(2,1)S(1)}, u32[]{:S(2)}, u32[]{:S(2)}) collective-permute-start(bf16[784,128]{1,0:T(8,128)(2,1)} %get-tuple-element.36), channel_id=1, source_target_pairs={{0,6},{2,4},{4,2},{6,0},{1,7},{3,5},{5,3},{7,1},{8,14},{10,12},{12... | collective-permute-start | bytes 602120 | tf_op jit(solution)/shard_map/ppermute | solution.py:336
  27.9 0.6 copy-start.8
  30.1 18.1 %all-to-all-start.1 = ((bf16[32,64,128]{2,1,0:T(8,128)(2,1)}), bf16[32,64,128]{2,1,0:T(8,128)(2,1)S(1)}, u32[]{:S(2)}, u32[]{:S(2)}) async-start(bf16[32,64,128]{2,1,0:T(8,128)(2,1)} %spread_prefix.1), calls=%async_computation.1 | async-start | bytes 1048576 | tf_op jit(solution)/shard_map/all_to_all | solution.py:352
  37.8 11.8 %collective-permute-start.3 = (bf16[2,256,128]{2,1,0:T(8,128)(2,1)S(1)}, bf16[2,256,128]{2,1,0:T(8,128)(2,1)S(1)}, u32[]{:S(2)}, u32[]{:S(2)}) collective-permute-start(bf16[2,256,128]{2,1,0:T(8,128)(2,1)S(1)} %pad_maximum_fusion), channel_id=1, source_target_pairs={{0,8},{2,10},{4,12},{6,14},{1,9},{3,11},{5,13},{7,15},{16,24},{18,... | collective-permute-start | bytes 393224 | tf_op jit(solution)/shard_map/ppermute | solution.py:342
  45.7 2.6 %copy-start.1 = (bf16[784,128]{1,0:T(8,128)(2,1)S(1)}, bf16[784,128]{1,0:T(8,128)(2,1)}, u32[]{:S(2)}) copy-start(bf16[784,128]{1,0:T(8,128)(2,1)} %get-tuple-element.33.own) | copy-start | bytes 602116
  45.7 13.9 %collective-permute-start.4 = (bf16[2,256,128]{2,1,0:T(8,128)(2,1)S(1)}, bf16[2,256,128]{2,1,0:T(8,128)(2,1)S(1)}, u32[]{:S(2)}, u32[]{:S(2)}) collective-permute-start(bf16[2,256,128]{2,1,0:T(8,128)(2,1)S(1)} %pad_maximum_fusion.1), channel_id=1, source_target_pairs={{0,9},{2,11},{4,13},{6,15},{1,8},{3,10},{5,12},{7,14},{16,25},{18,... | collective-permute-start | bytes 393224 | tf_op jit(solution)/shard_map/ppermute | solution.py:343
  63.6 5.9 %copy-start.5 = (bf16[4,128,128]{2,1,0:T(8,128)(2,1)}, bf16[4,128,128]{2,1,0:T(8,128)(2,1)S(1)}, u32[]{:S(2)}) copy-start(bf16[4,128,128]{2,1,0:T(8,128)(2,1)S(1)} %get-tuple-element.37.keep) | copy-start | bytes 393220
  63.6 23.2 %collective-permute-start.5 = (bf16[4,128,128]{2,1,0:T(8,128)(2,1)S(1)}, bf16[4,128,128]{2,1,0:T(8,128)(2,1)S(1)}, u32[]{:S(2)}, u32[]{:S(2)}) collective-permute-start(bf16[4,128,128]{2,1,0:T(8,128)(2,1)S(1)} %get-tuple-element.41), channel_id=1, source_target_pairs={{8,1},{10,3},{12,5},{14,7},{9,0},{11,2},{13,4},{15,6},{24,17},{26,... | collective-permute-start | bytes 393224 | tf_op jit(solution)/shard_map/ppermute | solution.py:390
  64.9 21.9 %collective-permute-start.6 = (bf16[4,128,128]{2,1,0:T(8,128)(2,1)S(1)}, bf16[4,128,128]{2,1,0:T(8,128)(2,1)S(1)}, u32[]{:S(2)}, u32[]{:S(2)}) collective-permute-start(bf16[4,128,128]{2,1,0:T(8,128)(2,1)S(1)} %get-tuple-element.42), channel_id=1, source_target_pairs={{8,0},{10,2},{12,4},{14,6},{9,1},{11,3},{13,5},{15,7},{24,16},{26,... | collective-permute-start | bytes 393224 | tf_op jit(solution)/shard_map/ppermute | solution.py:391
  69.5 0.6 copy-start
  70.1 0.6 copy-start.2
  70.8 0.6 copy-start.3
  71.4 0.6 copy-start.4
  72.1 17.9 %all-to-all-start.2 = ((bf16[32,64,128]{2,1,0:T(8,128)(2,1)}), bf16[32,64,128]{2,1,0:T(8,128)(2,1)S(1)}, u32[]{:S(2)}, u32[]{:S(2)}) async-start(bf16[32,64,128]{2,1,0:T(8,128)(2,1)} %get-tuple-element.40), calls=%async_computation.2 | async-start | bytes 1048576 | tf_op jit(solution)/shard_map/all_to_all | solution.py:410
  79.4 23.4 %collective-permute-start.7 = (bf16[4,128,128]{2,1,0:T(8,128)(2,1)S(1)}, bf16[4,128,128]{2,1,0:T(8,128)(2,1)S(1)}, u32[]{:S(2)}, u32[]{:S(2)}) collective-permute-start(bf16[4,128,128]{2,1,0:T(8,128)(2,1)S(1)} %get-tuple-element.45), channel_id=1, source_target_pairs={{0,1},{2,3},{4,5},{6,7},{8,9},{10,11},{12,13},{14,15},{1,0},{3,2},... | collective-permute-start | bytes 393224 | tf_op jit(solution)/shard_map/ppermute | solution.py:389
  86.8 0.7 copy-start.12
  87.4 0.7 copy-start.13
  89.9 0.8 copy-start.6
  92.5 27.6 %all-to-all-start.3 = ((f32[16,8,128]{2,1,0:T(8,128)}), f32[16,8,128]{2,1,0:T(8,128)S(1)}, u32[]{:S(2)}, u32[]{:S(2)}) async-start(f32[16,8,128]{2,1,0:T(8,128)} %prefix_sums.1), calls=%async_computation.3 | async-start | bytes 131072 | tf_op jit(solution)/shard_map/all_to_all | solution.py:441
  102.8 0.6 copy-start.14
  105.3 10.1 %collective-permute-start.8 = (bf16[384,128]{1,0:T(8,128)(2,1)}, bf16[384,128]{1,0:T(8,128)(2,1)S(1)}, u32[]{:S(2)}, u32[]{:S(2)}) collective-permute-start(bf16[384,128]{1,0:T(8,128)(2,1)} %get-tuple-element.51), channel_id=1, source_target_pairs={{0,2},{2,0},{4,6},{6,4},{1,3},{3,1},{5,7},{7,5},{8,10},{10,8},{12,... | collective-permute-start | bytes 294920 | tf_op jit(solution)/shard_map/ppermute | solution.py:336
  107.2 12.9 %collective-permute-start.9 = (bf16[384,128]{1,0:T(8,128)(2,1)}, bf16[384,128]{1,0:T(8,128)(2,1)S(1)}, u32[]{:S(2)}, u32[]{:S(2)}) collective-permute-start(bf16[384,128]{1,0:T(8,128)(2,1)} %get-tuple-element.52), channel_id=1, source_target_pairs={{0,4},{2,6},{4,0},{6,2},{1,5},{3,7},{5,1},{7,3},{8,12},{10,14},{12... | collective-permute-start | bytes 294920 | tf_op jit(solution)/shard_map/ppermute | solution.py:336
  111.3 8.8 %collective-permute-start.10 = (bf16[384,128]{1,0:T(8,128)(2,1)}, bf16[384,128]{1,0:T(8,128)(2,1)S(1)}, u32[]{:S(2)}, u32[]{:S(2)}) collective-permute-start(bf16[384,128]{1,0:T(8,128)(2,1)} %get-tuple-element.53), channel_id=1, source_target_pairs={{0,6},{2,4},{4,2},{6,0},{1,7},{3,5},{5,3},{7,1},{8,14},{10,12},{12... | collective-permute-start | bytes 294920 | tf_op jit(solution)/shard_map/ppermute | solution.py:336
  115.4 4.7 %copy-start.9 = (bf16[384,128]{1,0:T(8,128)(2,1)}, bf16[384,128]{1,0:T(8,128)(2,1)S(1)}, u32[]{:S(2)}) copy-start(bf16[384,128]{1,0:T(8,128)(2,1)S(1)} %collective-permute-done.8.back1) | copy-start | bytes 294916
  120.1 0.6 copy-start.10
  120.1 0.7 copy-start.11
  120.1 0.7 copy-start.7
